TPU v7x, 32 devices: a whole 2x2x4 slice. The times are simulated.
32 devices in a mesh: seq: 4 (over x, core), tensor: 4 (over z), dp: 2 (over y).
Axes of the slice: x: 2, y: 2, z: 4, core: 2. Of those that a mesh axis runs over, the one named last changes fastest.
Arguments:
- states: bfloat16 [8, 2048, 2048], P('dp', 'seq'), may hold values from -6 to 6
- ln1_gain: bfloat16 [2048], P('dp'), may hold values from 0.099609375 to 1.8984375
- ln1_bias: bfloat16 [2048], P('dp'), may hold values from -4 to 4
- ln2_gain: bfloat16 [2048], P('dp'), may hold values from 0.099609375 to 1.8984375
- ln2_bias: bfloat16 [2048], P('dp'), may hold values from -4 to 4
- qkv_weight: bfloat16 [2048, 6144], P('dp', 'tensor'), may hold values from -0.125 to 0.125
- qkv_bias: bfloat16 [6144], P(('tensor', 'dp')), may hold values from -4 to 4
- dense_weight: bfloat16 [2048, 2048], P('tensor', 'dp'), may hold values from -1 to 1
- dense_bias: bfloat16 [2048], P('dp'), may hold values from -4 to 4
- up_weight: bfloat16 [2048, 8192], P('dp', 'tensor'), may hold values from -0.125 to 0.125
- up_bias: bfloat16 [8192], P(('tensor', 'dp')), may hold values from -4 to 4
- down_weight: bfloat16 [8192, 2048], P('tensor', 'dp'), may hold values from -0.09375 to 0.09375
- out_bias: bfloat16 [2048], P('dp'), may hold values from -4 to 4
- out_grad: bfloat16 [8, 2048, 2048], P('dp', 'seq'), may hold values from -6 to 6
Outputs:
- output: bfloat16 [8, 2048, 2048], P('dp', 'seq', 'tensor')
- input_grad: float32 [8, 2048, 2048], P('dp', 'seq', 'tensor')
- ln1_gain_grad: float32 [2048], P(('tensor', 'dp'))
- ln1_bias_grad: float32 [2048], P(('tensor', 'dp'))
- ln2_gain_grad: float32 [2048], P(('tensor', 'dp'))
- ln2_bias_grad: float32 [2048], P(('tensor', 'dp'))
- qkv_weight_grad: float32 [2048, 6144], P('dp', 'tensor')
- qkv_bias_grad: float32 [6144], P(('tensor', 'dp'))
- dense_weight_grad: float32 [2048, 2048], P('tensor', 'dp')
- dense_bias_grad: float32 [2048], P('dp')
- up_weight_grad: float32 [2048, 8192], P('dp', 'tensor')
- up_bias_grad: float32 [8192], P(('tensor', 'dp'))
- down_weight_grad: float32 [8192, 2048], P('tensor', 'dp')
- out_bias_grad: float32 [2048], P('dp')
All inputs are finite; a program needn't handle non-finite values.
Results may differ from a plain program's by a relative error of at most 0.019.
Values may be sent and summed in bfloat16 or wider, within the bound.
A program may use at most 320 MiB of HBM per device.

v0:
```python
import jax
import jax.numpy as jnp
from jax import lax
from jax.sharding import PartitionSpec as P

HD = 128
ROT = 32


epsilon = 1e-05


def from_behind(block, axis, distance):
    devices = range(lax.axis_size(axis))
    route = [(i - distance, i) for i in devices if i - distance in devices]
    return lax.ppermute(block, axis, route)


def shifted(block, axis, distance):
    devices = range(lax.axis_size(axis))
    route = [((i - distance) % len(devices), i) for i in devices]
    return lax.ppermute(block, axis, route)


def norm_parts(values, scale_in, shift_in):
    center = values - jnp.mean(values, -1, keepdims=True)
    inverse = lax.rsqrt(jnp.mean(center * center, -1, keepdims=True) + epsilon)
    unit_rows = center * inverse
    return (unit_rows * scale_in + shift_in, unit_rows, inverse)


def norm_back(grad_rows, unit_rows, inverse, scale_in):
    scaled = grad_rows * scale_in
    return inverse * (
        scaled
        - jnp.mean(scaled, -1, keepdims=True)
        - unit_rows * jnp.mean(scaled * unit_rows, -1, keepdims=True)
    )


def turn_tables(first_place, length):
    half_rot = ROT // 2
    frequency = 10000.0 ** (-jnp.arange(half_rot, dtype=jnp.float32) * 2.0 / ROT)
    places = (first_place + jnp.arange(length)).astype(jnp.float32)
    angles = places[:, None] * frequency[None, :]
    angles = jnp.concatenate([angles, angles], -1)
    return (jnp.cos(angles)[:, None, :], jnp.sin(angles)[:, None, :])


def rotate(values, cosine, sine_table):
    half_rot = ROT // 2
    rotated_part = values[..., :ROT]
    turned = jnp.concatenate([-rotated_part[..., half_rot:], rotated_part[..., :half_rot]], -1)
    return jnp.concatenate([rotated_part * cosine + turned * sine_table, values[..., ROT:]], -1)


def rotate_back(grad_rows, cosine, sine_table):
    half_rot = ROT // 2
    rotated_part = grad_rows[..., :ROT]
    scaled = rotated_part * sine_table
    turned = jnp.concatenate([scaled[..., half_rot:], -scaled[..., :half_rot]], -1)
    return jnp.concatenate([rotated_part * cosine + turned, grad_rows[..., ROT:]], -1)


def gelu_exact(values):
    return jax.nn.gelu(values, approximate=False)


def keep_same(state_now):
    return state_now


def masked_scores(queries, keys_in, query_places, key_first, factor):
    key_count = keys_in.shape[0]
    scores = (
        jnp.einsum("qhd,khd->hqk", queries, keys_in, preferred_element_type=jnp.float32) * factor
    )
    allowed = query_places[:, None] >= (key_first + jnp.arange(key_count))[None, :]
    return jnp.where(allowed[None], scores, -1e30)


def block_terms(
    queries,
    keys_in,
    values_in,
    attended_grad,
    log_total,
    row_delta,
    query_places,
    key_first,
    factor,
):
    scores = masked_scores(queries, keys_in, query_places, key_first, factor)
    weights = jnp.exp(scores - log_total[:, :, None])
    value_part = jnp.einsum(
        "hqk,qhd->khd",
        weights.astype(jnp.bfloat16),
        attended_grad,
        preferred_element_type=jnp.float32,
    )
    weight_grad = jnp.einsum(
        "qhd,khd->hqk", attended_grad, values_in, preferred_element_type=jnp.float32
    )
    score_grad = (weights * (weight_grad - row_delta[:, :, None])).astype(jnp.bfloat16)
    query_part = (
        jnp.einsum("hqk,khd->qhd", score_grad, keys_in, preferred_element_type=jnp.float32) * factor
    )
    key_part = (
        jnp.einsum("hqk,qhd->khd", score_grad, queries, preferred_element_type=jnp.float32) * factor
    )
    return (query_part, key_part, value_part)


def on_device(
    states,
    ln1_gain,
    ln1_bias,
    ln2_gain,
    ln2_bias,
    qkv_weight,
    qkv_bias,
    dense_weight,
    dense_bias,
    up_weight,
    up_bias,
    down_weight,
    out_bias,
    out_grad,
):
    micro_count, row_count, feature_count = states.shape
    head_count = qkv_weight.shape[1] // (3 * HD)
    col_count = feature_count // lax.axis_size("tensor")
    col_first = lax.axis_index("tensor") * col_count
    seq_index = lax.axis_index("seq")
    seq_devices = lax.axis_size("seq")
    row_first = seq_index * row_count
    query_last = row_first + row_count - 1
    query_places = row_first + jnp.arange(row_count)
    factor = HD ** (-0.5)
    cosine, sine_table = turn_tables(row_first, row_count)
    f32 = jnp.float32
    bf16 = jnp.bfloat16
    norm_acc = jnp.zeros((4, col_count), f32)
    qkv_w_acc = jnp.zeros((feature_count, qkv_weight.shape[1]), f32)
    qkv_b_acc = jnp.zeros((qkv_weight.shape[1],), f32)
    dense_acc = jnp.zeros((dense_weight.shape[0], feature_count), f32)
    bias_acc = jnp.zeros((feature_count,), f32)
    up_w_acc = jnp.zeros((feature_count, up_weight.shape[1]), f32)
    up_b_acc = jnp.zeros((up_weight.shape[1],), f32)
    down_acc = jnp.zeros((down_weight.shape[0], feature_count), f32)
    output_rows = []
    grad_rows = []
    for micro_index in range(micro_count):
        gathered = (
            lax.all_gather(ln1_gain, "dp", axis=0, tiled=True),
            lax.all_gather(ln1_bias, "dp", axis=0, tiled=True),
            lax.all_gather(ln2_gain, "dp", axis=0, tiled=True),
            lax.all_gather(ln2_bias, "dp", axis=0, tiled=True),
            lax.all_gather(qkv_weight, "dp", axis=0, tiled=True),
            lax.all_gather(qkv_bias, "dp", axis=0, tiled=True),
            lax.all_gather(dense_weight, "dp", axis=1, tiled=True),
            lax.all_gather(dense_bias, "dp", axis=0, tiled=True),
            lax.all_gather(up_weight, "dp", axis=0, tiled=True),
            lax.all_gather(up_bias, "dp", axis=0, tiled=True),
            lax.all_gather(down_weight, "dp", axis=1, tiled=True),
            lax.all_gather(out_bias, "dp", axis=0, tiled=True),
        )
        (
            gain_one,
            shift_one,
            gain_two,
            shift_two,
            qkv_full,
            qkv_shift,
            dense_full,
            dense_shift,
            up_full,
            up_shift,
            down_full,
            out_shift,
        ) = gathered
        gain_one_f = gain_one.astype(f32)
        gain_two_f = gain_two.astype(f32)
        inputs = states[micro_index].astype(f32)
        normed_one, unit_one, inverse_one = norm_parts(inputs, gain_one_f, shift_one.astype(f32))
        normed_one = normed_one.astype(bf16)
        projected = jnp.dot(normed_one, qkv_full, preferred_element_type=f32) + qkv_shift.astype(
            f32
        )
        projected = projected.reshape(row_count, head_count, 3, HD)
        queries = rotate(projected[:, :, 0], cosine, sine_table).astype(bf16)
        keys_local = rotate(projected[:, :, 1], cosine, sine_table).astype(bf16)
        values_local = projected[:, :, 2].astype(bf16)
        initial = (
            jnp.full((head_count, row_count), -1e30, f32),
            jnp.zeros((head_count, row_count), f32),
            jnp.zeros((row_count, head_count, HD), f32),
        )
        kv_piece = (
            lax.all_gather(keys_local, "seq", axis=0, tiled=True),
            lax.all_gather(values_local, "seq", axis=0, tiled=True),
        )
        key_first = jnp.int32(0)

        def absorb_process(state_now):
            run_max, run_total, run_acc = state_now
            scores = masked_scores(queries, kv_piece[0], query_places, key_first, factor)
            new_max = jnp.maximum(run_max, jnp.max(scores, -1))
            weights = jnp.exp(scores - new_max[:, :, None])
            shrink = jnp.exp(run_max - new_max)
            run_total = jnp.sum(weights, -1)
            run_acc = run_acc * shrink.T[:, :, None] + jnp.einsum(
                "hqk,khd->qhd", weights.astype(bf16), kv_piece[1], preferred_element_type=f32
            )
            return (new_max, run_total, run_acc)

        run_max, run_total, run_acc = lax.cond(
            key_first <= query_last, absorb_process, keep_same, initial
        )
        log_total = run_max + jnp.log(run_total)
        attended = run_acc / run_total.T[:, :, None]
        attended_low = attended.reshape(row_count, head_count * HD).astype(bf16)
        normed_two, unit_two, inverse_two = norm_parts(inputs, gain_two_f, shift_two.astype(f32))
        normed_two = normed_two.astype(bf16)
        pre_act = jnp.dot(normed_two, up_full, preferred_element_type=f32) + up_shift.astype(f32)
        activated = gelu_exact(pre_act).astype(bf16)
        partial_sum = jnp.dot(attended_low, dense_full, preferred_element_type=f32) + jnp.dot(
            activated, down_full, preferred_element_type=f32
        )
        branch_cols = lax.psum_scatter(
            partial_sum.astype(jnp.bfloat16), "tensor", scatter_dimension=1, tiled=True
        ).astype(jnp.float32)
        bias_cols = lax.dynamic_slice_in_dim(
            dense_shift.astype(f32) + out_shift.astype(f32), col_first, col_count, 0
        )
        state_cols = lax.dynamic_slice_in_dim(inputs, col_first, col_count, 1)
        output_rows.append((state_cols + branch_cols + bias_cols[None, :]).astype(bf16))
        cotangent = out_grad[micro_index]
        cotangent_f = cotangent.astype(f32)
        bias_acc = bias_acc + jnp.sum(cotangent_f, 0)
        down_acc = down_acc + jnp.einsum(
            "tf,td->fd", activated, cotangent, preferred_element_type=f32
        )
        dense_acc = dense_acc + jnp.einsum(
            "ta,td->ad", attended_low, cotangent, preferred_element_type=f32
        )
        act_grad = jnp.einsum("td,fd->tf", cotangent, down_full, preferred_element_type=f32)
        pre_grad = jax.vjp(gelu_exact, pre_act)[1](act_grad)[0].astype(bf16)
        up_b_acc = up_b_acc + jnp.sum(pre_grad.astype(f32), 0)
        up_w_acc = up_w_acc + jnp.einsum(
            "td,tf->df", normed_two, pre_grad, preferred_element_type=f32
        )
        two_grad = jnp.einsum("tf,df->td", pre_grad, up_full, preferred_element_type=f32)
        attended_grad = (
            jnp.einsum("td,ad->ta", cotangent, dense_full, preferred_element_type=f32)
            .astype(bf16)
            .reshape(row_count, head_count, HD)
        )
        row_delta = jnp.sum(attended_grad.astype(f32) * attended, -1).T

        def cycle_step(step, carry):
            query_grad, keys_in, values_in, key_acc, value_acc = carry
            anchor = (seq_index - step) % seq_devices
            key_first = anchor * row_count

            def cycle_process(parts):
                grad_now, key_now, value_now = parts
                query_part, key_part, value_part = block_terms(
                    queries,
                    keys_in,
                    values_in,
                    attended_grad,
                    log_total,
                    row_delta,
                    query_places,
                    key_first,
                    factor,
                )
                return (grad_now + query_part, key_now + key_part, value_now + value_part)

            query_grad, key_acc, value_acc = lax.cond(
                key_first <= query_last, cycle_process, keep_same, (query_grad, key_acc, value_acc)
            )
            keys_in, values_in = from_behind((keys_in, values_in), "seq", 1)
            key_acc, value_acc = (
                shifted(key_acc.astype(jnp.bfloat16), "seq", 1).astype(key_acc.dtype),
                shifted(value_acc.astype(jnp.bfloat16), "seq", 1).astype(value_acc.dtype),
            )
            return (query_grad, keys_in, values_in, key_acc, value_acc)

        zero_block = jnp.zeros((row_count, head_count, HD), f32)
        cycle_start = (zero_block, keys_local, values_local, zero_block, zero_block)
        query_grad, moved_keys, moved_values, key_grad, value_grad = lax.fori_loop(
            0, seq_devices, cycle_step, cycle_start
        )
        qkv_grad = jnp.stack(
            [
                rotate_back(query_grad, cosine, sine_table),
                rotate_back(key_grad, cosine, sine_table),
                value_grad,
            ],
            2,
        )
        qkv_grad = qkv_grad.reshape(row_count, head_count * 3 * HD).astype(bf16)
        qkv_b_acc = qkv_b_acc + jnp.sum(qkv_grad.astype(f32), 0)
        qkv_w_acc = qkv_w_acc + jnp.einsum(
            "td,tc->dc", normed_one, qkv_grad, preferred_element_type=f32
        )
        one_grad = jnp.einsum("tc,dc->td", qkv_grad, qkv_full, preferred_element_type=f32)
        input_part = norm_back(one_grad, unit_one, inverse_one, gain_one_f) + norm_back(
            two_grad, unit_two, inverse_two, gain_two_f
        )
        norm_terms = jnp.stack(
            [
                jnp.sum(one_grad * unit_one, 0),
                jnp.sum(one_grad, 0),
                jnp.sum(two_grad * unit_two, 0),
                jnp.sum(two_grad, 0),
            ]
        )
        input_cols, norm_cols = (
            lax.psum_scatter(
                input_part.astype(jnp.bfloat16), "tensor", scatter_dimension=1, tiled=True
            ).astype(jnp.float32),
            lax.psum_scatter(
                norm_terms.astype(jnp.bfloat16), "tensor", scatter_dimension=1, tiled=True
            ).astype(jnp.float32),
        )
        norm_acc = norm_acc + norm_cols
        grad_rows.append(
            lax.dynamic_slice_in_dim(cotangent_f, col_first, col_count, 1) + input_cols
        )
    totals = (
        lax.psum(norm_acc[0].astype(jnp.bfloat16), "seq").astype(jnp.float32),
        lax.psum(norm_acc[1].astype(jnp.bfloat16), "seq").astype(jnp.float32),
        lax.psum(norm_acc[2].astype(jnp.bfloat16), "seq").astype(jnp.float32),
        lax.psum(norm_acc[3].astype(jnp.bfloat16), "seq").astype(jnp.float32),
        lax.psum(qkv_w_acc.astype(jnp.bfloat16), "seq").astype(jnp.float32),
        lax.psum(qkv_b_acc.astype(jnp.bfloat16), "seq").astype(jnp.float32),
        lax.psum(dense_acc.astype(jnp.bfloat16), "seq").astype(jnp.float32),
        lax.psum(bias_acc.astype(jnp.bfloat16), "seq").astype(jnp.float32),
        lax.psum(up_w_acc.astype(jnp.bfloat16), "seq").astype(jnp.float32),
        lax.psum(up_b_acc.astype(jnp.bfloat16), "seq").astype(jnp.float32),
        lax.psum(down_acc.astype(jnp.bfloat16), "seq").astype(jnp.float32),
    )
    shares = (
        lax.psum_scatter(
            totals[0].astype(jnp.bfloat16), "dp", scatter_dimension=0, tiled=True
        ).astype(jnp.float32),
        lax.psum_scatter(
            totals[1].astype(jnp.bfloat16), "dp", scatter_dimension=0, tiled=True
        ).astype(jnp.float32),
        lax.psum_scatter(
            totals[2].astype(jnp.bfloat16), "dp", scatter_dimension=0, tiled=True
        ).astype(jnp.float32),
        lax.psum_scatter(
            totals[3].astype(jnp.bfloat16), "dp", scatter_dimension=0, tiled=True
        ).astype(jnp.float32),
        lax.psum_scatter(
            totals[4].astype(jnp.bfloat16), "dp", scatter_dimension=0, tiled=True
        ).astype(jnp.float32),
        lax.psum_scatter(
            totals[5].astype(jnp.bfloat16), "dp", scatter_dimension=0, tiled=True
        ).astype(jnp.float32),
        lax.psum_scatter(
            totals[6].astype(jnp.bfloat16), "dp", scatter_dimension=1, tiled=True
        ).astype(jnp.float32),
        lax.psum_scatter(
            totals[7].astype(jnp.bfloat16), "dp", scatter_dimension=0, tiled=True
        ).astype(jnp.float32),
        lax.psum_scatter(
            totals[8].astype(jnp.bfloat16), "dp", scatter_dimension=0, tiled=True
        ).astype(jnp.float32),
        lax.psum_scatter(
            totals[9].astype(jnp.bfloat16), "dp", scatter_dimension=0, tiled=True
        ).astype(jnp.float32),
        lax.psum_scatter(
            totals[10].astype(jnp.bfloat16), "dp", scatter_dimension=1, tiled=True
        ).astype(jnp.float32),
    )
    output = jnp.stack(output_rows, 0)
    input_grad = jnp.stack(grad_rows, 0)
    return (
        output,
        input_grad,
        shares[0],
        shares[1],
        shares[2],
        shares[3],
        shares[4],
        shares[5],
        shares[6],
        shares[7],
        shares[8],
        shares[9],
        shares[10],
        shares[7],
    )


def solution(mesh):
    placed = (
        P("dp", "seq", None),
        P("dp"),
        P("dp"),
        P("dp"),
        P("dp"),
        P("dp", "tensor"),
        P(("tensor", "dp")),
        P("tensor", "dp"),
        P("dp"),
        P("dp", "tensor"),
        P(("tensor", "dp")),
        P("tensor", "dp"),
        P("dp"),
        P("dp", "seq", None),
    )
    return jax.shard_map(
        on_device,
        mesh=mesh,
        in_specs=placed,
        out_specs=(
            P("dp", "seq", "tensor"),
            P("dp", "seq", "tensor"),
            P(("tensor", "dp")),
            P(("tensor", "dp")),
            P(("tensor", "dp")),
            P(("tensor", "dp")),
            P("dp", "tensor"),
            P(("tensor", "dp")),
            P("tensor", "dp"),
            P("dp"),
            P("dp", "tensor"),
            P(("tensor", "dp")),
            P("tensor", "dp"),
            P("dp"),
        ),
        check_vma=False,
    )
```

profile of v0, /device:TPU:0, one launch (start us, length us, event | category | flops | bytes accessed | tf_op | source)
XLA Modules:
  0.0 2371.4 jit_solution(17841508609253118939)
XLA Ops:
  30.9 61.8 %all-gather.18.cloned.1.call-done = bf16[2048,1536]{1,0:T(8,128)(2,1)} async-done(((bf16[1024,1536]{1,0:T(8,128)(2,1)}), bf16[2048,1536]{1,0:T(8,128)(2,1)}) %all-gather.18.cloned.1.call-update) | async-done | bytes 6291472 | tf_op jit(solution)/shard_map/all_gather | solution.py:159
  126.8 71.6 %all-gather.24.cloned.1.call-done = bf16[2048,2048]{1,0:T(8,128)(2,1)} async-done(((bf16[1024,2048]{1,0:T(8,128)(2,1)}), bf16[2048,2048]{1,0:T(8,128)(2,1)}) %all-gather.24.cloned.1.call-update) | async-done | bytes 8388624 | tf_op jit(solution)/shard_map/all_gather | solution.py:163
  198.4 18.7 multiply_convert_fusion.9
  217.1 86.9 %all-gather.26.cloned.1.call-done = bf16[2048,2048]{1,0:T(8,128)(2,1)} async-done(((bf16[2048,1024]{1,0:T(8,128)(2,1)}), bf16[2048,2048]{1,0:T(8,128)(2,1)}) %all-gather.26.cloned.1.call-update) | async-done | bytes 8388624 | tf_op jit(solution)/shard_map/all_gather | solution.py:165
  304.0 14.3 convert_reduce_fusion.1
  328.0 24.0 %all-gather.38.cloned.1.call-done = bf16[2048,4,1,128]{0,3,2,1:T(8,128)(2,1)} async-done(((bf16[512,4,1,128]{0,3,2,1:T(8,128)(2,1)}), bf16[2048,4,1,128]{0,3,2,1:T(8,128)(2,1)}) %all-gather.38.cloned.1.call-update) | async-done | bytes 2097168 | tf_op jit(solution)/shard_map/all_gather | solution.py:201
  352.1 30.9 %conditional.10 = (f32[4,512]{1,0:T(4,128)}, f32[4,512]{1,0:T(4,128)}, f32[4,512]{1,0:T(4,128)S(1)}, f32[512,4,128]{0,2,1:T(8,128)}) conditional(s32[]{:T(128)} %convert_element_type.737, () %tuple.168, (s32[512]{0:T(512)S(1)}, bf16[512,4,128]{0,2,1:T(8,128)(2,1)S(1)}, bf16[2048,4,128]{0,2,1:T(8,128)(2,1)}, bf16[2048,4,128]{0,2,1:T(8,128)(2,1)}) %tuple.547), branch_computations={%region_16.17_spmd, %region_17.20_spmd} | conditional | flops 2194933760 | bytes 137971808 | solution.py:217
  393.9 122.3 %while.98 = (s32[]{:T(128)}, f32[512,4,128]{2,0,1:T(8,128)}, bf16[512,4,128]{2,0,1:T(8,128)(2,1)S(1)}, bf16[512,4,128]{2,0,1:T(8,128)(2,1)S(1)}, f32[512,4,128]{...) while((s32[]{:T(128)}, f32[512,4,128]{2,0,1:T(8,128)}, ...), condition=%wide.region_52.53_spmd.clone, body=%wide.region_49.52_spmd.clone.sunk | while | flops 1355809792 | bytes 63214320 | solution.py:293
  422.8 16.9 collective-permute-start.10
  453.9 14.9 collective-permute-start.10
  469.7 9.9 collective-permute-start.11
  490.1 15.4 collective-permute-start.10
  528.7 13.3 multiply_reduce_fusion.3
  599.9 12.8 fusion.328
  639.8 10.4 fusion.175
  668.2 42.7 %multiply_convert_fusion.11 = (bf16[512,2048]{1,0:T(8,128)(2,1)}, f32[512,2048]{1,0:T(8,128)}, bf16[512,2048]{1,0:T(8,128)(2,1)}, f32[512,2048]{1,0:T(8,128)}, b...) fusion(f32[2048]{0:T(1024)S(1)} %copy-done.164, f32[512,2048]{1,0:T(8,128)S(1)} %fusion.330, ...), kind=kOutput, calls=%fused_computation.253 | convolution fusion | flops 4508876800 | bytes 41971712 | tf_op jit(solution)/shard_map/dot_general | solution.py:225
  717.8 30.5 %conditional.11 = (f32[4,512]{1,0:T(4,128)}, f32[4,512]{1,0:T(4,128)}, f32[4,512]{1,0:T(4,128)S(1)}, f32[512,4,128]{0,2,1:T(8,128)}) conditional(s32[]{:T(128)} %convert_element_type.737, () %tuple.170, (s32[512]{0:T(512)S(1)}, bf16[512,4,128]{0,2,1:T(8,128)(2,1)}, bf16[2048,4,128]{0,2,1:T(8,128)(2,1)}, bf16[2048,4,128]{0,2,1:T(8,128)(2,1)}) %tuple.546), branch_computations={%region_23.24_spmd, %region_24.27_spmd} | conditional | flops 2194933760 | bytes 137971808 | solution.py:217
  756.4 154.0 %while.99 = (s32[]{:T(128)}, f32[512,4,128]{2,0,1:T(8,128)}, bf16[512,4,128]{2,0,1:T(8,128)(2,1)S(1)}, bf16[512,4,128]{2,0,1:T(8,128)(2,1)S(1)}, f32[512,4,128]{...) while((s32[]{:T(128)}, f32[512,4,128]{2,0,1:T(8,128)}, ...), condition=%wide.region_62.63_spmd.clone, body=%wide.region_59.62_spmd.clone.sunk | while | flops 1355809792 | bytes 75797344 | solution.py:293
  759.3 9.9 conditional.23
  770.0 15.3 collective-permute-start.14
  803.7 22.0 collective-permute-start.14
  844.0 12.5 collective-permute-start.14
  858.6 12.2 collective-permute-start.15
  884.1 13.1 collective-permute-start.14
  915.5 30.6 %conditional.9 = (f32[4,512]{1,0:T(4,128)}, f32[4,512]{1,0:T(4,128)}, f32[4,512]{1,0:T(4,128)S(1)}, f32[512,4,128]{0,2,1:T(8,128)}) conditional(s32[]{:T(128)} %convert_element_type.737, () %tuple.166, (s32[512]{0:T(512)S(1)}, bf16[512,4,128]{0,2,1:T(8,128)(2,1)}, bf16[2048,4,128]{0,2,1:T(8,128)(2,1)}, bf16[2048,4,128]{0,2,1:T(8,128)(2,1)}) %tuple.545), branch_computations={%region_9.10_spmd, %region_10.13_spmd} | conditional | flops 2194933760 | bytes 137971808 | solution.py:217
  954.0 151.1 %while.97 = (s32[]{:T(128)}, f32[512,4,128]{2,0,1:T(8,128)}, bf16[512,4,128]{2,0,1:T(8,128)(2,1)S(1)}, bf16[512,4,128]{2,0,1:T(8,128)(2,1)S(1)}, f32[512,4,128]{...) while((s32[]{:T(128)}, f32[512,4,128]{2,0,1:T(8,128)}, ...), condition=%wide.region_42.43_spmd.clone, body=%wide.region_39.42_spmd.clone.sunk | while | flops 1355809792 | bytes 75797344 | solution.py:293
  956.8 9.8 conditional.21
  967.5 12.5 collective-permute-start.6
  998.3 22.3 collective-permute-start.6
  1038.9 12.6 collective-permute-start.6
  1053.5 12.2 collective-permute-start.7
  1079.0 13.1 collective-permute-start.6
  1110.3 30.5 %conditional.8 = (f32[4,512]{1,0:T(4,128)}, f32[4,512]{1,0:T(4,128)}, f32[4,512]{1,0:T(4,128)S(1)}, f32[512,4,128]{0,2,1:T(8,128)}) conditional(s32[]{:T(128)} %convert_element_type.737, () %tuple.164, (s32[512]{0:T(512)S(1)}, bf16[512,4,128]{0,2,1:T(8,128)(2,1)}, bf16[2048,4,128]{0,2,1:T(8,128)(2,1)}, bf16[2048,4,128]{0,2,1:T(8,128)(2,1)}) %tuple.544), branch_computations={%region_2.0_spmd, %region_3.6_spmd} | conditional | flops 2194933760 | bytes 137971808 | solution.py:217
  1148.8 143.3 %while.96 = (s32[]{:T(128)}, f32[512,4,128]{2,0,1:T(8,128)}, bf16[512,4,128]{2,0,1:T(8,128)(2,1)S(1)}, bf16[512,4,128]{2,0,1:T(8,128)(2,1)}, f32[512,4,128]{2,0,...) while((s32[]{:T(128)}, f32[512,4,128]{2,0,1:T(8,128)}, ...), condition=%wide.region_32.33_spmd.clone, body=%wide.region_29.32_spmd.clone.sunk | while | flops 1355809792 | bytes 65311500 | solution.py:293
  1159.5 12.5 collective-permute-start.2
  1188.3 22.3 collective-permute-start.2
  1226.9 14.8 collective-permute-start.2
  1241.7 10.0 collective-permute-start.3
  1264.1 16.1 collective-permute-start.2
  1354.2 17.2 add_convert_fusion.2
  1372.1 12.9 convert_reduce_fusion.3
  1385.1 11.6 fusion.324
  1396.6 13.0 convert_reduce_fusion.2
  1418.3 13.2 convert_reduce_fusion
  1431.5 21.0 add_convert_fusion.1
  1452.6 12.8 fusion.187
  1465.4 10.5 fusion.197
  1484.5 21.8 add_convert_fusion
  1523.5 13.4 multiply_reduce_fusion
  1552.2 15.4 multiply_reduce_fusion.1
  1638.4 31.4 %reduce-scatter.47.cloned.1.call-done = bf16[2048,1024]{1,0:T(8,128)(2,1)} async-done(((bf16[2048,2048]{1,0:T(8,128)(2,1)}), bf16[2048,1024]{1,0:T(8,128)(2,1)}) %reduce-scatter.47.cloned.1.call-update) | async-done | bytes 4194320 | tf_op jit(solution)/shard_map/reduce_scatter | solution.py:377
  1686.1 10.1 bitcast_convert_fusion.3
  1696.3 10.1 slice_convert_fusion.15
  1716.7 21.2 reduce-scatter.51.cloned.1.call-done
  1738.9 21.0 reduce-scatter.55.cloned.1.call-done
  1779.4 25.0 %reduce-scatter.37.cloned.1.call-done = bf16[512,512]{1,0:T(8,128)(2,1)} async-done(((bf16[512,2048]{1,0:T(8,128)(2,1)}), bf16[512,512]{1,0:T(8,128)(2,1)}) %reduce-scatter.37.cloned.1.call-update) | async-done | bytes 524304 | tf_op jit(solution)/shard_map/reduce_scatter | solution.py:322
  1806.0 44.1 %reduce-scatter.29.cloned.1.call-done = bf16[512,512]{1,0:T(8,128)(2,1)} async-done(((bf16[512,2048]{1,0:T(8,128)(2,1)}), bf16[512,512]{1,0:T(8,128)(2,1)}) %reduce-scatter.29.cloned.1.call-update) | async-done | bytes 524304 | tf_op jit(solution)/shard_map/reduce_scatter | solution.py:230
  1850.0 45.5 %reduce-scatter.27.cloned.1.call-done = bf16[512,512]{1,0:T(8,128)(2,1)} async-done(((bf16[512,2048]{1,0:T(8,128)(2,1)}), bf16[512,512]{1,0:T(8,128)(2,1)}) %reduce-scatter.27.cloned.1.call-update) | async-done | bytes 524304 | tf_op jit(solution)/shard_map/reduce_scatter | solution.py:230
  1895.6 45.5 %reduce-scatter.31.cloned.1.call-done = bf16[512,512]{1,0:T(8,128)(2,1)} async-done(((bf16[512,2048]{1,0:T(8,128)(2,1)}), bf16[512,512]{1,0:T(8,128)(2,1)}) %reduce-scatter.31.cloned.1.call-update) | async-done | bytes 524304 | tf_op jit(solution)/shard_map/reduce_scatter | solution.py:230
  1941.0 46.1 %reduce-scatter.25.cloned.1.call-done = bf16[512,512]{1,0:T(8,128)(2,1)} async-done(((bf16[512,2048]{1,0:T(8,128)(2,1)}), bf16[512,512]{1,0:T(8,128)(2,1)}) %reduce-scatter.25.cloned.1.call-update) | async-done | bytes 524304 | tf_op jit(solution)/shard_map/reduce_scatter | solution.py:230
  1992.2 40.3 %reduce-scatter.33.cloned.1.call-done = bf16[512,512]{1,0:T(8,128)(2,1)} async-done(((bf16[512,2048]{1,0:T(8,128)(2,1)}), bf16[512,512]{1,0:T(8,128)(2,1)}) %reduce-scatter.33.cloned.1.call-update) | async-done | bytes 524304 | tf_op jit(solution)/shard_map/reduce_scatter | solution.py:322
  2034.1 43.8 %reduce-scatter.35.cloned.1.call-done = bf16[512,512]{1,0:T(8,128)(2,1)} async-done(((bf16[512,2048]{1,0:T(8,128)(2,1)}), bf16[512,512]{1,0:T(8,128)(2,1)}) %reduce-scatter.35.cloned.1.call-update) | async-done | bytes 524304 | tf_op jit(solution)/shard_map/reduce_scatter | solution.py:322
  2079.5 44.1 %reduce-scatter.39.cloned.1.call-done = bf16[512,512]{1,0:T(8,128)(2,1)} async-done(((bf16[512,2048]{1,0:T(8,128)(2,1)}), bf16[512,512]{1,0:T(8,128)(2,1)}) %reduce-scatter.39.cloned.1.call-update) | async-done | bytes 524304 | tf_op jit(solution)/shard_map/reduce_scatter | solution.py:322
  2127.6 219.8 %all-reduce.12.cloned.1.call-done = (bf16[1024,1536]{1,0:T(8,128)(2,1)}, bf16[512,1024]{1,0:T(8,128)(2,1)}, bf16[1024,2048]{1,0:T(8,128)(2,1)}, bf16[2048,1024]{1,0:T(8,128)(2,1)}) async-done(((bf16[1024,1536]{1,0:T(8,128)(2,1)}, bf16[512,1024]{1,0:T(8,128)(2,1)}, bf16[1024,2048]{1,0:T(8,128)(2,1)}, bf16[2048,1024]{1,0:T(8,128)(2,1)}), (bf16[1024,1536]{1,0:T(8,128)(2,1)}, bf16[512,1024]{1,0:T(8,128)(2,1)}, ...) | async-done | bytes 12582928 | tf_op jit(solution)/shard_map/psum | solution.py:338
  (1070 shorter events, 917.2 us)
Async XLA Ops:
  7.2 85.5 %all-gather.18.cloned.1.call-start = ((), (), s32[]{:S(2)}) async-start(), calls=%async_computation.16 | async-start | bytes 9437184 | tf_op jit(solution)/shard_map/all_gather | solution.py:159
  7.9 190.5 %all-gather.24.cloned.1.call-start = ((), (), s32[]{:S(2)}) async-start(), calls=%async_computation.19 | async-start | bytes 12582912 | tf_op jit(solution)/shard_map/all_gather | solution.py:163
  8.7 295.3 %all-gather.26.cloned.1.call-start = ((), (), s32[]{:S(2)}) async-start(), calls=%async_computation.20 | async-start | bytes 12582912 | tf_op jit(solution)/shard_map/all_gather | solution.py:165
  9.4 318.6 %all-gather.30.cloned.1.call-start = ((), (), s32[]{:S(2)}) async-start(), calls=%async_computation.24 | async-start | bytes 2621440 | tf_op jit(solution)/shard_map/all_gather | solution.py:200
  106.5 245.5 %all-gather.38.cloned.1.call-start = ((), (), s32[]{:S(2)}) async-start(), calls=%async_computation.34 | async-start | bytes 2621440 | tf_op jit(solution)/shard_map/all_gather | solution.py:201
  107.5 279.2 %all-gather.22.cloned.1.call-start = ((), (), s32[]{:S(2)}) async-start(), calls=%async_computation.18 | async-start | bytes 3145728 | tf_op jit(solution)/shard_map/all_gather | solution.py:161
  108.1 609.7 %all-gather.32.cloned.1.call-start = ((), (), s32[]{:S(2)}) async-start(), calls=%async_computation.26 | async-start | bytes 2621440 | tf_op jit(solution)/shard_map/all_gather | solution.py:200
  403.9 8.9 collective-permute-start.10
  404.7 13.6 collective-permute-start.11
  406.3 13.0 collective-permute-start.8
  408.2 11.1 collective-permute-start.9
  422.8 24.1 %collective-permute-start.10 = (bf16[512,4,128]{2,0,1:T(8,128)(2,1)}, bf16[512,4,128]{2,0,1:T(8,128)(2,1)}, u32[]{:S(2)}, u32[]{:S(2)}) collective-permute-start(bf16[512,4,128]{2,0,1:T(8,128)(2,1)} %convert_element_type.1208), channel_id=1, source_target_pairs={{24,0},{0,8},{8,16},{16,24},{25,1},{1,9},{9,17},{17,25},{26,2},{2,... | collective-permute-start | bytes 1572872 | tf_op jit(solution)/shard_map/while/body/eval_jaxpr/ppermute | solution.py:22
  440.6 8.8 collective-permute-start.11
  453.9 29.6 %collective-permute-start.10 = (bf16[512,4,128]{2,0,1:T(8,128)(2,1)}, bf16[512,4,128]{2,0,1:T(8,128)(2,1)}, u32[]{:S(2)}, u32[]{:S(2)}) collective-permute-start(bf16[512,4,128]{2,0,1:T(8,128)(2,1)} %convert_element_type.1208), channel_id=1, source_target_pairs={{24,0},{0,8},{8,16},{16,24},{25,1},{1,9},{9,17},{17,25},{26,2},{2,... | collective-permute-start | bytes 1572872 | tf_op jit(solution)/shard_map/while/body/eval_jaxpr/ppermute | solution.py:22
  469.7 15.9 collective-permute-start.11
  490.1 22.5 collective-permute-start.10
  506.4 8.8 collective-permute-start.11
  591.4 126.4 %all-gather.40.cloned.1.call-start = ((), (), s32[]{:S(2)}) async-start(), calls=%async_computation.35 | async-start | bytes 2621440 | tf_op jit(solution)/shard_map/all_gather | solution.py:201
  592.3 323.1 %all-gather.28.cloned.1.call-start = ((), (), s32[]{:S(2)}) async-start(), calls=%async_computation.22 | async-start | bytes 2621440 | tf_op jit(solution)/shard_map/all_gather | solution.py:200
  595.3 320.1 %all-gather.36.cloned.1.call-start = ((), (), s32[]{:S(2)}) async-start(), calls=%async_computation.33 | async-start | bytes 2621440 | tf_op jit(solution)/shard_map/all_gather | solution.py:201
  597.5 512.8 %all-gather.20.cloned.1.call-start = ((), (), s32[]{:S(2)}) async-start(), calls=%async_computation.17 | async-start | bytes 2621440 | tf_op jit(solution)/shard_map/all_gather | solution.py:200
  599.7 510.6 %all-gather.34.cloned.1.call-start = ((), (), s32[]{:S(2)}) async-start(), calls=%async_computation.32 | async-start | bytes 2621440 | tf_op jit(solution)/shard_map/all_gather | solution.py:201
  650.2 988.2 %reduce-scatter.43.cloned.1.call-start = ((), (), s32[]{:S(2)}) async-start(), calls=%async_computation.37 | async-start | bytes 3145728 | tf_op jit(solution)/shard_map/reduce_scatter | solution.py:365
  770.0 23.3 collective-permute-start.14
  787.5 8.9 collective-permute-start.15
  789.5 9.0 collective-permute-start.12
  803.7 30.4 %collective-permute-start.14 = (bf16[512,4,128]{2,0,1:T(8,128)(2,1)}, bf16[512,4,128]{2,0,1:T(8,128)(2,1)}, u32[]{:S(2)}, u32[]{:S(2)}) collective-permute-start(bf16[512,4,128]{2,0,1:T(8,128)(2,1)} %convert_element_type.1213), channel_id=1, source_target_pairs={{24,0},{0,8},{8,16},{16,24},{25,1},{1,9},{9,17},{17,25},{26,2},{2,... | collective-permute-start | bytes 1572872 | tf_op jit(solution)/shard_map/while/body/eval_jaxpr/ppermute | solution.py:22
  827.8 8.9 collective-permute-start.15
  844.0 30.7 %collective-permute-start.14 = (bf16[512,4,128]{2,0,1:T(8,128)(2,1)}, bf16[512,4,128]{2,0,1:T(8,128)(2,1)}, u32[]{:S(2)}, u32[]{:S(2)}) collective-permute-start(bf16[512,4,128]{2,0,1:T(8,128)(2,1)} %convert_element_type.1213), channel_id=1, source_target_pairs={{24,0},{0,8},{8,16},{16,24},{25,1},{1,9},{9,17},{17,25},{26,2},{2,... | collective-permute-start | bytes 1572872 | tf_op jit(solution)/shard_map/while/body/eval_jaxpr/ppermute | solution.py:22
  858.6 18.2 collective-permute-start.15
  884.1 21.5 collective-permute-start.14
  899.3 8.9 collective-permute-start.15
  967.5 20.9 collective-permute-start.6
  982.1 8.9 collective-permute-start.7
  998.3 30.7 %collective-permute-start.6 = (bf16[512,4,128]{2,0,1:T(8,128)(2,1)}, bf16[512,4,128]{2,0,1:T(8,128)(2,1)}, u32[]{:S(2)}, u32[]{:S(2)}) collective-permute-start(bf16[512,4,128]{2,0,1:T(8,128)(2,1)} %convert_element_type.1203), channel_id=1, source_target_pairs={{24,0},{0,8},{8,16},{16,24},{25,1},{1,9},{9,17},{17,25},{26,2},{2,... | collective-permute-start | bytes 1572872 | tf_op jit(solution)/shard_map/while/body/eval_jaxpr/ppermute | solution.py:22
  1022.7 8.9 collective-permute-start.7
  1038.9 30.7 %collective-permute-start.6 = (bf16[512,4,128]{2,0,1:T(8,128)(2,1)}, bf16[512,4,128]{2,0,1:T(8,128)(2,1)}, u32[]{:S(2)}, u32[]{:S(2)}) collective-permute-start(bf16[512,4,128]{2,0,1:T(8,128)(2,1)} %convert_element_type.1203), channel_id=1, source_target_pairs={{24,0},{0,8},{8,16},{16,24},{25,1},{1,9},{9,17},{17,25},{26,2},{2,... | collective-permute-start | bytes 1572872 | tf_op jit(solution)/shard_map/while/body/eval_jaxpr/ppermute | solution.py:22
  1053.5 18.2 collective-permute-start.7
  1079.0 21.4 collective-permute-start.6
  1094.2 8.9 collective-permute-start.7
  1159.5 18.9 collective-permute-start.2
  1172.1 8.8 collective-permute-start.3
  1188.3 28.8 %collective-permute-start.2 = (bf16[512,4,128]{2,0,1:T(8,128)(2,1)}, bf16[512,4,128]{2,0,1:T(8,128)(2,1)S(1)}, u32[]{:S(2)}, u32[]{:S(2)}) collective-permute-start(bf16[512,4,128]{2,0,1:T(8,128)(2,1)} %convert_element_type.1198), channel_id=1, source_target_pairs={{24,0},{0,8},{8,16},{16,24},{25,1},{1,9},{9,17},{17,25},{26,2},{2,... | collective-permute-start | bytes 1572872 | tf_op jit(solution)/shard_map/while/body/eval_jaxpr/ppermute | solution.py:22
  1210.7 8.8 collective-permute-start.3
  1226.9 28.8 %collective-permute-start.2 = (bf16[512,4,128]{2,0,1:T(8,128)(2,1)}, bf16[512,4,128]{2,0,1:T(8,128)(2,1)S(1)}, u32[]{:S(2)}, u32[]{:S(2)}) collective-permute-start(bf16[512,4,128]{2,0,1:T(8,128)(2,1)} %convert_element_type.1198), channel_id=1, source_target_pairs={{24,0},{0,8},{8,16},{16,24},{25,1},{1,9},{9,17},{17,25},{26,2},{2,... | collective-permute-start | bytes 1572872 | tf_op jit(solution)/shard_map/while/body/eval_jaxpr/ppermute | solution.py:22
  1241.7 15.0 collective-permute-start.3
  1264.1 22.5 collective-permute-start.2
  1280.3 8.8 collective-permute-start.3
  1318.4 319.9 %reduce-scatter.41.cloned.1.call-start = ((), (), s32[]{:S(2)}) async-start(), calls=%async_computation.36 | async-start | bytes 9437184 | tf_op jit(solution)/shard_map/reduce_scatter | solution.py:359
  1371.5 266.9 %reduce-scatter.45.cloned.1.call-start = ((), (), s32[]{:S(2)}) async-start(), calls=%async_computation.38 | async-start | bytes 12582912 | tf_op jit(solution)/shard_map/reduce_scatter | solution.py:371
  1452.5 217.3 %reduce-scatter.47.cloned.1.call-start = ((), (), s32[]{:S(2)}) async-start(), calls=%async_computation.39 | async-start | bytes 12582912 | tf_op jit(solution)/shard_map/reduce_scatter | solution.py:377
  1506.4 200.2 %reduce-scatter.53.cloned.1.call-start = ((), (), s32[]{:S(2)}) async-start(), calls=%async_computation.42 | async-start | bytes 655360
  1538.3 177.4 %reduce-scatter.49.cloned.1.call-start = ((), (), s32[]{:S(2)}) async-start(), calls=%async_computation.40 | async-start | bytes 655360
  1568.8 169.1 %reduce-scatter.51.cloned.1.call-start = ((), (), s32[]{:S(2)}) async-start(), calls=%async_computation.41 | async-start | bytes 655360
  1570.1 189.9 %reduce-scatter.55.cloned.1.call-start = ((), (), s32[]{:S(2)}) async-start(), calls=%async_computation.43 | async-start | bytes 655360
  1571.3 233.1 %reduce-scatter.37.cloned.1.call-start = ((), (), s32[]{:S(2)}) async-start(), calls=%async_computation.30 | async-start | bytes 2621440 | tf_op jit(solution)/shard_map/reduce_scatter | solution.py:322
  1577.6 272.4 %reduce-scatter.29.cloned.1.call-start = ((), (), s32[]{:S(2)}) async-start(), calls=%async_computation.25 | async-start | bytes 2621440 | tf_op jit(solution)/shard_map/reduce_scatter | solution.py:230
  1588.2 307.3 %reduce-scatter.27.cloned.1.call-start = ((), (), s32[]{:S(2)}) async-start(), calls=%async_computation.23 | async-start | bytes 2621440 | tf_op jit(solution)/shard_map/reduce_scatter | solution.py:230
  1598.6 342.4 %reduce-scatter.31.cloned.1.call-start = ((), (), s32[]{:S(2)}) async-start(), calls=%async_computation.27 | async-start | bytes 2621440 | tf_op jit(solution)/shard_map/reduce_scatter | solution.py:230
  1608.9 378.3 %reduce-scatter.25.cloned.1.call-start = ((), (), s32[]{:S(2)}) async-start(), calls=%async_computation.21 | async-start | bytes 2621440 | tf_op jit(solution)/shard_map/reduce_scatter | solution.py:230
  1619.2 413.4 %reduce-scatter.33.cloned.1.call-start = ((), (), s32[]{:S(2)}) async-start(), calls=%async_computation.28 | async-start | bytes 2621440 | tf_op jit(solution)/shard_map/reduce_scatter | solution.py:322
  1625.7 452.2 %reduce-scatter.35.cloned.1.call-start = ((), (), s32[]{:S(2)}) async-start(), calls=%async_computation.29 | async-start | bytes 2621440 | tf_op jit(solution)/shard_map/reduce_scatter | solution.py:322
  1632.0 491.6 %reduce-scatter.39.cloned.1.call-start = ((), (), s32[]{:S(2)}) async-start(), calls=%async_computation.31 | async-start | bytes 2621440 | tf_op jit(solution)/shard_map/reduce_scatter | solution.py:322
  1638.3 709.1 %all-reduce.12.cloned.1.call-start = ((), (), s32[]{:S(2)}) async-start(), calls=%async_computation.44 | async-start | bytes 25165824 | tf_op jit(solution)/shard_map/psum | solution.py:338
  (241 other events, 4196.1 us)
Sparse Core Ops, SparseCore 0:
  9.6 83.0 all-gather.17
  94.2 104.1 all-gather.23
  199.9 103.9 all-gather.25
  305.4 22.5 all-gather.29
  329.4 22.5 all-gather.37
  353.5 33.1 all-gather.21
  591.5 38.3 all-gather.31
  631.5 22.5 all-gather.39
  655.6 22.6 all-gather.27
  679.8 22.5 all-gather.35
  703.9 22.5 all-gather.19
  727.9 22.5 all-gather.33
  1318.6 47.7 reduce-scatter.42
  1371.6 92.6 reduce-scatter.40
  1467.0 100.6 reduce-scatter.44
  1570.5 99.2 reduce-scatter.46
  1672.0 21.6 reduce-scatter.52
  1695.7 19.9 reduce-scatter.48
  1718.0 19.9 reduce-scatter.50
  1740.0 19.8 reduce-scatter.54
  1762.2 42.1 reduce-scatter.36
  1806.8 43.1 reduce-scatter.28
  1852.3 43.1 reduce-scatter.26
  1897.8 43.1 reduce-scatter.30
  1943.9 43.1 reduce-scatter.24
  1989.4 43.1 reduce-scatter.32
  2034.7 43.1 reduce-scatter.34
  2080.4 43.1 reduce-scatter.38
  2126.3 221.0 all-reduce.11
where the time goes:
time: 2380 us; the launch traced here: 2370 us
  waiting for transfers between devices  903 us (38%)
  matrix products  547 us (23%)
  starting transfers between devices  373 us (16%)
  other arithmetic  295 us (12%)
  local copies, waits for them, and re-layouts  181 us (8%)
  blocking collectives  50.2 us (2%)
    ppermute x32, starting transfers between devices, shifted(): return lax.ppermute(block, axis, route)  308 us
    psum x1, waiting for transfers between devices, on_device(): lax.psum(qkv_w_acc.astype(jnp.bfloat16), 'seq').astype(jnp.float32)  220 us
    reduce_scatter x4, waiting for transfers between devices, on_device(): lax.psum_scatter(partial_sum.astype(jnp.bfloat16), 'tensor', scatter_dime...  181 us
    reduce_scatter x4, waiting for transfers between devices, on_device(): lax.psum_scatter(input_part.astype(jnp.bfloat16), 'tensor', scatter_dimen...  153 us
    all_gather x1, waiting for transfers between devices, on_device(): lax.all_gather(down_weight, 'dp', axis=1, tiled=True)  86.9 us
    dot_general x4, matrix products, on_device(): jnp.dot(normed_two, up_full, preferred_element_type=f32)  78.7 us
    all_gather x1, waiting for transfers between devices, on_device(): lax.all_gather(up_weight, 'dp', axis=0, tiled=True)  71.6 us
    ppermute x32, starting transfers between devices, from_behind(): return lax.ppermute(block, axis, route)  62.3 us
  transfers between devices with their start and end apart: 93, of which 32 were waited for; matrix products, arithmetic and copies ran while one was open for 33% of the time, Pallas kernels for 0%

commit v1 on v0

v1 whole, which is shorter than its diff:
```python
import functools
import math

import jax
import jax.numpy as jnp
from jax import lax
from jax.experimental import pallas as pl
from jax.experimental.pallas import tpu as pltpu
from jax.sharding import PartitionSpec as P

HD = 128
ROT = 32
EPS = 1e-05
F32 = jnp.float32
BF16 = jnp.bfloat16
NT = (((1,), (1,)), ((), ()))
NN = (((1,), (0,)), ((), ()))
TN = (((0,), (0,)), ((), ()))


def mm(a, b, dims=NN):
    return lax.dot_general(a, b, dims, preferred_element_type=F32)


def swap(block, axis, distance):
    return lax.ppermute(block, axis, [(i, i ^ distance) for i in range(lax.axis_size(axis))])


def ordered(mine, other, second):
    return jnp.where(
        second, jnp.concatenate([other, mine], 0), jnp.concatenate([mine, other], 0)
    )


def halves(array, index, axis):
    size = array.shape[axis] // 2
    return tuple(
        lax.dynamic_slice_in_dim(array, place * size, size, axis) for place in (index, 1 - index)
    )


def gather_other(shard, core):
    size = shard.shape[0] // 2
    got = swap(lax.dynamic_slice_in_dim(shard, core * size, size, 0), "dp", 1)
    return ordered(got, swap(got, "seq", 1), core == 1)


def reduce_grad(lhs_own, rhs_own, lhs_oth, rhs_oth, core):
    own_keep, own_send = halves(lhs_own, core, 1)
    oth_keep, oth_send = halves(lhs_oth, core, 1)
    sent = swap(
        (mm(own_send, rhs_own, TN).astype(BF16), mm(oth_send, rhs_oth, TN).astype(BF16)), "seq", 1
    )
    oth = (mm(oth_keep, rhs_oth, TN) + sent[1].astype(F32)).astype(BF16)
    got = swap(oth, "dp", 1)
    own = (mm(own_keep, rhs_own, TN) + sent[0].astype(F32) + got.astype(F32)).astype(BF16)
    step = 2
    while step < lax.axis_size("seq"):
        own = (own.astype(F32) + swap(own, "seq", step).astype(F32)).astype(BF16)
        step *= 2
    return ordered(own, swap(own, "seq", 1), core == 1).astype(F32)


def turn_tables(first_place, length):
    half_rot = ROT // 2
    frequency = 10000.0 ** (-jnp.arange(half_rot, dtype=F32) * 2.0 / ROT)
    places = (first_place + jnp.arange(length)).astype(F32)
    angles = places[:, None] * frequency[None, :]
    return jnp.cos(angles), jnp.sin(angles)


def rotate(values, cosine, sine):
    half_rot = ROT // 2
    low = values[..., :half_rot]
    high = values[..., half_rot:ROT]
    return jnp.concatenate(
        [low * cosine - high * sine, high * cosine + low * sine, values[..., ROT:]], -1
    )


def attention_kernel(
    parts, rows, block, scale, cos_ref, sin_ref, *refs
):
    ins = refs[:parts]
    outs = refs[parts : 2 * parts]
    q_s, k_s, v_s, g_s, kt_s, vt_s, prob_s, dk_s, dv_s, o_s, dq_s = refs[2 * parts :]
    index = lax.axis_index("seq")
    length = parts * rows
    for k in range(parts):
        at = pl.ds(pl.multiple_of((index ^ k) * rows, rows), rows)
        q_s[at, :] = ins[k][0, :, 0:HD]
        k_s[at, :] = ins[k][0, :, HD : 2 * HD]
        v_s[at, :] = ins[k][0, :, 2 * HD : 3 * HD]
        g_s[at, :] = ins[k][0, :, 3 * HD : 4 * HD]
    for j in range(length // block):
        at = slice(j * block, (j + 1) * block)
        kt_s[:, at] = k_s[at, :].T
        vt_s[:, at] = v_s[at, :].T
    dk_s[...] = jnp.zeros_like(dk_s)
    dv_s[...] = jnp.zeros_like(dv_s)
    factor = scale * math.log2(math.e)
    for i in range(length // block):
        qat = slice(i * block, (i + 1) * block)
        q = q_s[qat, :]
        g = g_s[qat, :]
        gt = g.T.astype(F32)

        def keys(j):
            return pl.ds(pl.multiple_of(j * block, block), block)

        def score(j, top, masked):
            s = mm(k_s[keys(j), :], q, NT)
            if masked:
                key = lax.broadcasted_iota(jnp.int32, s.shape, 0)
                query = lax.broadcasted_iota(jnp.int32, s.shape, 1)
                s = jnp.where(key <= query, s, -1e30)
            prob_s[keys(j), :] = s
            return jnp.maximum(top, jnp.max(s.reshape(block // 8, 8, block), 0))

        top = jnp.full((8, block), -1e30, F32)
        top = lax.fori_loop(0, i, lambda j, t: score(j, t, False), top)
        top = jnp.max(score(i, top, True), 0, keepdims=True)

        def weigh(j, carry):
            total, acc = carry
            e = jnp.exp2((prob_s[keys(j), :] - top) * factor)
            prob_s[keys(j), :] = e
            total = total + jnp.sum(e.reshape(block // 8, 8, block), 0)
            return total, acc + mm(vt_s[:, keys(j)], e.astype(BF16))

        total, acc = lax.fori_loop(
            0, i + 1, weigh, (jnp.zeros((8, block), F32), jnp.zeros((HD, block), F32))
        )
        inverse = 1.0 / jnp.sum(total, 0, keepdims=True)
        acc = acc * inverse
        delta = jnp.sum(acc * gt, 0, keepdims=True)
        o_s[qat, :] = acc.T.astype(BF16)

        def back(j, dqt):
            p = prob_s[keys(j), :] * inverse
            ds = (p * (mm(v_s[keys(j), :], g, NT) - delta)).astype(BF16)
            dv_s[keys(j), :] += mm(p.astype(BF16), g)
            dk_s[keys(j), :] += mm(ds, q)
            return dqt + mm(kt_s[:, keys(j)], ds)

        dqt = lax.fori_loop(0, i + 1, back, jnp.zeros((HD, block), F32))
        dq_s[qat, :] = dqt.T
    half_rot = ROT // 2
    lane = lax.broadcasted_iota(jnp.int32, (rows, HD), 1)
    for k in range(parts):
        at = pl.ds(pl.multiple_of((index ^ k) * rows, rows), rows)
        cosine = cos_ref[at, :]
        sine = sin_ref[at, :]

        def turn_back(w):
            turned = jnp.where(
                lane < half_rot, pltpu.roll(w, HD - half_rot, 1), pltpu.roll(w, half_rot, 1)
            )
            return (w * cosine + turned * sine) * scale

        outs[k][0, :, 0:HD] = o_s[at, :]
        outs[k][0, :, HD : 2 * HD] = turn_back(dq_s[at, :]).astype(BF16)
        outs[k][0, :, 2 * HD : 3 * HD] = turn_back(dk_s[at, :]).astype(BF16)
        outs[k][0, :, 3 * HD : 4 * HD] = dv_s[at, :].astype(BF16)


def attention(blocks):
    parts = len(blocks)
    _, rows, width = blocks[0].shape
    length = parts * rows
    block = min(256, rows)
    cosine, sine = turn_tables(0, length)
    rest = HD - ROT
    cos_full = jnp.concatenate([cosine, cosine, jnp.ones((length, rest), F32)], 1)
    sin_full = jnp.concatenate([sine, -sine, jnp.zeros((length, rest), F32)], 1)
    scale = HD ** (-0.5)
    pair = length * length * HD
    whole = pl.BlockSpec((1, rows, width), lambda: (0, 0, 0))
    table = pl.BlockSpec((length, HD), lambda: (0, 0))
    return pl.pallas_call(
        functools.partial(attention_kernel, parts, rows, block, scale),
        out_shape=[jax.ShapeDtypeStruct((1, rows, width), BF16)] * parts,
        in_specs=[table, table] + [whole] * parts,
        out_specs=[whole] * parts,
        scratch_shapes=[pltpu.VMEM((length, HD), BF16)] * 4
        + [pltpu.VMEM((HD, length), BF16)] * 2
        + [pltpu.VMEM((length, block), F32)]
        + [pltpu.VMEM((length, HD), F32)] * 2
        + [pltpu.VMEM((length, HD), BF16)]
        + [pltpu.VMEM((length, HD), F32)],
        compiler_params=pltpu.CompilerParams(vmem_limit_bytes=40 * 1024 * 1024),
        cost_estimate=pl.CostEstimate(
            flops=6 * pair, bytes_accessed=8 * length * width, transcendentals=length * length // 2
        ),
    )(cos_full, sin_full, *blocks)


def on_device(
    states,
    ln1_gain,
    ln1_bias,
    ln2_gain,
    ln2_bias,
    qkv_weight,
    qkv_bias,
    dense_weight,
    dense_bias,
    up_weight,
    up_bias,
    down_weight,
    out_bias,
    out_grad,
):
    micros, rows, features = states.shape
    heads = qkv_weight.shape[1] // (3 * HD)
    tokens = micros * rows
    n = lax.axis_size("seq")
    pairs = heads * micros // n
    s = lax.axis_index("seq")
    core = s % 2
    d = lax.axis_index("dp")
    t = lax.axis_index("tensor")
    columns = features // lax.axis_size("tensor")

    def own_first(array, axis):
        return halves(array, d, axis)

    def absolute(own, other, axis=0):
        return jnp.where(
            d == 1, jnp.concatenate([other, own], axis), jnp.concatenate([own, other], axis)
        )

    small = (ln1_gain, ln1_bias, ln2_gain, ln2_bias, dense_bias, out_bias, qkv_bias, up_bias)
    small_got = swap(jnp.concatenate(small, 0), "dp", 1)
    other = []
    place = 0
    for vector in small:
        other.append(small_got[place : place + vector.shape[0]].astype(F32))
        place += vector.shape[0]
    qkv_other = gather_other(qkv_weight, core)
    up_other = gather_other(up_weight, core)
    dense_other = gather_other(dense_weight, core)
    down_other = gather_other(down_weight, core)

    x = states.reshape(tokens, features)
    xf = x.astype(F32)
    mean = jnp.mean(xf, -1, keepdims=True)
    center = xf - mean
    inverse = lax.rsqrt(jnp.mean(center * center, -1, keepdims=True) + EPS)
    x_own, x_oth = own_first(x, 1)
    unit_own = (x_own.astype(F32) - mean) * inverse
    unit_oth = (x_oth.astype(F32) - mean) * inverse
    g1 = (ln1_gain.astype(F32), other[0])
    g2 = (ln2_gain.astype(F32), other[2])
    one_own = (unit_own * g1[0] + ln1_bias.astype(F32)).astype(BF16)
    one_oth = (unit_oth * g1[1] + other[1]).astype(BF16)
    two_own = (unit_own * g2[0] + ln2_bias.astype(F32)).astype(BF16)
    two_oth = (unit_oth * g2[1] + other[3]).astype(BF16)
    cot = out_grad.reshape(tokens, features)
    cot_own, cot_oth = own_first(cot, 1)

    projected = (
        mm(one_own, qkv_weight) + mm(one_oth, qkv_other) + absolute(qkv_bias.astype(F32), other[6])
    )
    projected = projected.reshape(micros, rows, heads, 3, HD)
    cosine, sine = turn_tables(s * rows, rows)
    cosine = cosine[:, None, :]
    sine = sine[:, None, :]
    queries = rotate(projected[:, :, :, 0], cosine, sine)
    keys = rotate(projected[:, :, :, 1], cosine, sine)
    attended_grad = mm(cot_own, dense_weight, NT) + mm(cot_oth, dense_other, NT)
    payload = jnp.concatenate(
        [queries, keys, projected[:, :, :, 2], attended_grad.reshape(micros, rows, heads, HD)], -1
    ).astype(BF16)
    payload = payload.transpose(2, 0, 1, 3).reshape(n, pairs, 1, rows, 4 * HD)

    returned = []
    for pair in range(pairs):
        sent = [
            lax.dynamic_index_in_dim(payload[:, pair], s ^ k, 0, False) for k in range(n)
        ]
        blocks = [sent[0]] + [swap(sent[k], "seq", k) for k in range(1, n)]
        results = attention(blocks)
        back = jnp.stack([results[0]] + [swap(results[k], "seq", k) for k in range(1, n)])
        returned.append(
            jnp.concatenate(
                [lax.dynamic_slice_in_dim(back, s ^ j, 1, 0) for j in range(n)], 0
            )
        )
    returned = jnp.stack(returned, 1).reshape(heads, micros, rows, 4, HD)
    attended = returned[:, :, :, 0].transpose(1, 2, 0, 3).reshape(tokens, heads * HD)
    qkv_grad = (
        returned[:, :, :, 1:].transpose(1, 2, 0, 3, 4).reshape(tokens, heads * 3 * HD)
    )

    pre_act = mm(two_own, up_weight) + mm(two_oth, up_other) + absolute(
        up_bias.astype(F32), other[7]
    )
    tail = 0.5 * (1.0 + lax.erf(pre_act * math.sqrt(0.5)))
    activated = (pre_act * tail).astype(BF16)
    slope = (
        tail + pre_act * jnp.exp(-0.5 * pre_act * pre_act) * (1.0 / math.sqrt(2.0 * math.pi))
    ).astype(BF16)
    act_grad = mm(cot_own, down_weight, NT) + mm(cot_oth, down_other, NT)
    pre_grad = (act_grad * slope.astype(F32)).astype(BF16)

    down_grad = reduce_grad(activated, cot_own, activated, cot_oth, core)
    up_grad = reduce_grad(two_own, pre_grad, two_oth, pre_grad, core)
    dense_grad = reduce_grad(attended, cot_own, attended, cot_oth, core)
    qkv_w_grad = reduce_grad(one_own, qkv_grad, one_oth, qkv_grad, core)

    down_grad = down_grad
    partial = absolute(
        (mm(attended, dense_weight) + mm(activated, down_weight)).astype(BF16),
        (mm(attended, dense_other) + mm(activated, down_other)).astype(BF16),
        1,
    )
    branch = lax.psum_scatter(partial, "tensor", scatter_dimension=1, tiled=True).astype(F32)
    bias = absolute(
        dense_bias.astype(F32) + out_bias.astype(F32), other[4] + other[5]
    )
    first = t * columns
    output = (
        lax.dynamic_slice_in_dim(x, first, columns, 1).astype(F32)
        + branch
        + lax.dynamic_slice_in_dim(bias, first, columns, 0)
    ).astype(BF16)

    two_grad = (mm(pre_grad, up_weight, NT), mm(pre_grad, up_other, NT))
    one_grad = (mm(qkv_grad, qkv_weight, NT), mm(qkv_grad, qkv_other, NT))
    unit = (unit_own, unit_oth)

    def norm_back(grads, gains):
        scaled = [g * gain for g, gain in zip(grads, gains)]
        center = sum(jnp.sum(e, -1, keepdims=True) for e in scaled) / features
        along = sum(jnp.sum(e * u, -1, keepdims=True) for e, u in zip(scaled, unit)) / features
        return [inverse * (e - center - u * along) for e, u in zip(scaled, unit)]

    part_one = norm_back(one_grad, g1)
    part_two = norm_back(two_grad, g2)
    input_part = absolute(
        (part_one[0] + part_two[0]).astype(BF16), (part_one[1] + part_two[1]).astype(BF16), 1
    )
    input_cols = lax.psum_scatter(input_part, "tensor", scatter_dimension=1, tiled=True)
    input_grad = lax.dynamic_slice_in_dim(cot, first, columns, 1).astype(F32) + input_cols.astype(
        F32
    )

    norm_terms = absolute(
        *[
            jnp.stack(
                [
                    jnp.sum(one_grad[i] * unit[i], 0),
                    jnp.sum(one_grad[i], 0),
                    jnp.sum(two_grad[i] * unit[i], 0),
                    jnp.sum(two_grad[i], 0),
                ],
                1,
            )
            for i in range(2)
        ]
    )
    norm_terms = lax.psum(norm_terms, ("seq", "dp", "tensor"))
    vectors = lax.psum(
        jnp.concatenate(
            [
                jnp.sum(qkv_grad.astype(F32), 0),
                jnp.sum(pre_grad.astype(F32), 0),
                jnp.sum(cot.astype(F32), 0),
            ]
        ),
        ("seq", "dp"),
    )
    norm_count = columns // 2
    norm_mine = lax.dynamic_slice_in_dim(norm_terms, first + d * norm_count, norm_count, 0)
    vector_grads = []
    place = 0
    for size in (qkv_grad.shape[1], pre_grad.shape[1], features):
        vector_grads.append(
            lax.dynamic_slice_in_dim(vectors, place + d * (size // 2), size // 2, 0)
        )
        place += size

    def side_by_side(grad):
        return grad

    shape = (micros, rows, columns)
    return (
        output.reshape(shape),
        input_grad.reshape(shape),
        norm_mine[:, 0],
        norm_mine[:, 1],
        norm_mine[:, 2],
        norm_mine[:, 3],
        qkv_w_grad,
        vector_grads[0],
        side_by_side(dense_grad),
        vector_grads[2],
        up_grad,
        vector_grads[1],
        side_by_side(down_grad),
        vector_grads[2],
    )


def solution(mesh):
    placed = (
        P("dp", "seq", None),
        P("dp"),
        P("dp"),
        P("dp"),
        P("dp"),
        P("dp", "tensor"),
        P(("tensor", "dp")),
        P("tensor", "dp"),
        P("dp"),
        P("dp", "tensor"),
        P(("tensor", "dp")),
        P("tensor", "dp"),
        P("dp"),
        P("dp", "seq", None),
    )
    return jax.shard_map(
        on_device,
        mesh=mesh,
        in_specs=placed,
        out_specs=(
            P("dp", "seq", "tensor"),
            P("dp", "seq", "tensor"),
            P(("tensor", "dp")),
            P(("tensor", "dp")),
            P(("tensor", "dp")),
            P(("tensor", "dp")),
            P("dp", "tensor"),
            P(("tensor", "dp")),
            P("tensor", "dp"),
            P("dp"),
            P("dp", "tensor"),
            P(("tensor", "dp")),
            P("tensor", "dp"),
            P("dp"),
        ),
        check_vma=False,
    )
```

time: 2380 us -> 1180 us (0.50)
  waiting for transfers between devices: 903 us -> 237 us
  starting transfers between devices: 373 us -> 39.3 us
  matrix products: 547 us -> 315 us
  other arithmetic: 295 us -> 126 us
  Pallas kernels: 0 us -> 123 us
  local copies, waits for them, and re-layouts: 181 us -> 243 us
    reduce_scatter x12 -> x2, waiting for transfers between devices: 366 us -> 0.01 us  [the longest x1 0.01 us: on_device(): lax.psum_scatter(input_part, 'tensor', scatter_dimension=1, tiled=True)]
    ppermute x64 -> x53, starting transfers between devices: 371 us -> 39.3 us  [swap(): lax.ppermute(block, axis, [(i, i ^ distance) for i in range(lax.axis_size...]
    all_gather x12 -> x0, waiting for transfers between devices: 250 us -> none  [the longest x1 86.9 us: on_device(): lax.all_gather(down_weight, 'dp', axis=1, tiled=True)]
    dot_general x76 -> x32, matrix products: 547 us -> 315 us  [mm(): return lax.dot_general(a, b, dims, preferred_element_type=F32)]
    ppermute x64 -> x53, waiting for transfers between devices: 14.5 us -> 237 us  [swap(): lax.ppermute(block, axis, [(i, i ^ distance) for i in range(lax.axis_size...]
    psum x1 -> x0, waiting for transfers between devices: 220 us -> none  [on_device(): lax.psum(qkv_w_acc.astype(jnp.bfloat16), 'seq').astype(jnp.float32)]
    pallas_call x0 -> x4, Pallas kernels: none -> 123 us  [attention(): pl.pallas_call(functools.partial(attention_kernel, parts, rows, block, sc...]
    dynamic_slice x0 -> x31, local copies, waits for them, and re-layouts: none -> 103 us  [the longest x18 78.5 us: on_device(): lax.dynamic_index_in_dim(payload[:, pair], s ^ k, 0, False)]
  transfers between devices with their start and end apart: 93 -> 55, of which waited for: 32 -> 11; matrix products, arithmetic and copies ran while one was open for 33% -> 48% of each run, Pallas kernels for 0% -> 11%
where the time goes in v1:
time: 1180 us; the launch traced here: 1160 us
  matrix products  315 us (27%)
  local copies, waits for them, and re-layouts  243 us (21%)
  waiting for transfers between devices  237 us (20%)
  other arithmetic  126 us (11%)
  Pallas kernels  123 us (10%)
  blocking collectives  64.7 us (5%)
  starting transfers between devices  39.3 us (3%)
  between operations  15.8 us (1%)
    dot_general x32, matrix products, mm(): return lax.dot_general(a, b, dims, preferred_element_type=F32)  315 us
    ppermute x53, waiting for transfers between devices, swap(): lax.ppermute(block, axis, [(i, i ^ distance) for i in range(lax.axis_size...  237 us
    pallas_call x4, Pallas kernels, attention(): pl.pallas_call(functools.partial(attention_kernel, parts, rows, block, sc...  123 us
    dynamic_slice x18, local copies, waits for them, and re-layouts, on_device(): lax.dynamic_index_in_dim(payload[:, pair], s ^ k, 0, False)  78.5 us
    unnamed x194, local copies, waits for them, and re-layouts  48.2 us
    psum x1, blocking collectives, on_device(): norm_terms = lax.psum(norm_terms, ('seq', 'dp', 'tensor'))  39.7 us
    ppermute x53, starting transfers between devices, swap(): lax.ppermute(block, axis, [(i, i ^ distance) for i in range(lax.axis_size...  39.3 us
    psum x1, blocking collectives, on_device(): lax.psum(jnp.concatenate([jnp.sum(qkv_grad.astype(F32), 0), jnp.sum(pre_g...  25 us
  transfers between devices with their start and end apart: 55, of which 11 were waited for; matrix products, arithmetic and copies ran while one was open for 48% of the time, Pallas kernels for 11%

profile of v1, /device:TPU:0, one launch (start us, length us, event | category | flops | bytes accessed | tf_op | source)
XLA Modules:
  0.0 1164.1 jit_solution(12323047361677184874)
XLA Ops:
  24.5 15.4 %fusion.55 = f32[2048,2048]{1,0:T(8,128)} fusion(bf16[2048,1024]{1,0:T(8,128)(2,1)} %param.25, bf16[2048,2048]{1,0:T(8,128)(2,1)} %bitcast.139, s32[]{:T(128)S(6)} %select_n.203), kind=kOutput, calls=%fused_computation.124 | convolution fusion | flops 8589934592 | bytes 25165828 | tf_op jit(solution)/shard_map/dot_general | solution.py:22
  39.9 6.6 fusion.57
  51.1 5.7 fusion.1
  57.0 6.0 multiply_sine_fusion
  63.2 8.0 constant_dynamic-slice_fusion.38
  73.2 6.5 copy.134
  79.7 6.6 copy.135
  86.4 11.5 add_convert_fusion.4
  97.9 51.9 %collective-permute-done.3 = bf16[256,1024]{1,0:T(8,128)(2,1)} collective-permute-done((bf16[256,1024]{1,0:T(8,128)(2,1)}, bf16[256,1024]{1,0:T(8,128)(2,1)}, u32[]{:S(2)}, u32[]{:S(2)}) %collective-permute-start.3) | collective-permute-done | bytes 524320 | tf_op jit(solution)/shard_map/ppermute | solution.py:26
  150.3 9.6 fusion.126
  160.8 5.2 add_convert_fusion.13
  174.5 15.3 %add_add_fusion.1 = f32[2048,1536]{1,0:T(8,128)} fusion(f32[2048,1536]{1,0:T(8,128)} %fusion.126, bf16[2048,1024]{0,1:T(8,128)(2,1)} %get-tuple-element.142, f32[1536]{0:T(1024)S(1)} %maximum_select_fusion.19, bf16[512,1536]{1,0:T(8,128)(2,1)} %collective-permute-done.1, bf16[512,1536]{1,0:T(8,128)(2,1)} %collective-permute-done.2, pred[]{:T(512)S(6)} %eq.7), kind=kOutput, calls=%fused_computation.17 | convolution fusion | flops 6462898176 | bytes 32512000 | tf_op jit(solution)/shard_map/dot_general | solution.py:22
  189.8 12.7 %copy.99 = f32[2048,1536]{0,1:T(8,128)} copy(f32[2048,1536]{1,0:T(8,128)} %add_add_fusion.1) | data formatting | bytes 25165824 | tf_op jit(solution)/shard_map/add | solution.py:263
  202.5 15.6 %reshape.298 = f32[4,512,4,3,128]{1,0,4,3,2:T(4,128)} reshape(f32[2048,1536]{0,1:T(8,128)} %copy.99) | data formatting | bytes 25165824 | tf_op jit(solution)/shard_map/reshape | solution.py:265
  218.1 5.4 slice_bitcast_fusion.1
  229.6 13.1 %fusion.121 = (bf16[4,1,1,512,512]{3,1,4,0,2:T(2,128)(2,1)S(1)}, bf16[4,1,1,512,512]{3,1,4,0,2:T(2,128)(2,1)S(1)}, bf16[4,1,1,512,512]{3,1,4,0,2:T(2,128)(2,1)}, bf16[4,1,1,512,512]{3,1,4,0,2:T(2,128)(2,1)}) fusion(bf16[4,4,1,512,512]{3,1,4,0,2:T(4,128)(2,1)S(1)} %bitcast.135), kind=kLoop, calls=%fused_computation.266 | loop fusion | bytes 16777216 | tf_op jit(solution)/shard_map/slice | solution.py:280
  242.7 10.4 constant_dynamic-slice_fusion.8
  275.9 12.4 %constant_dynamic-slice_fusion.24 = (bf16[1,1,1,512,512]{3,1,4,0,2:T(2,128)(2,1)}, bf16[1,1,1,512,512]{3,1,4,0,2:T(2,128)(2,1)}, bf16[1,1,1,512,512]{3,1,4,0,2:T...) fusion(bf16[4,1,1,512,512]{3,1,4,0,2:T(2,128)(2,1)} %get-tuple-, ...), kind=kLoop, calls=%fused_computation.207 | loop fusion | bytes 8388624 | tf_op jit(solution)/shard_map/jit(dynamic_index_in_dim)/dynamic_slice | solution.py:280
  299.4 15.5 %fusion.127 = f32[2048,2048]{1,0:T(8,128)} fusion(bf16[2048,1024]{0,1:T(8,128)(2,1)} %get-tuple-element.186, bf16[1024,2048]{1,0:T(8,128)(2,1)} %param.23), kind=kOutput, calls=%fused_computation.272 | convolution fusion | flops 8589934592 | bytes 25165824 | tf_op jit(solution)/shard_map/dot_general | solution.py:22
  346.8 31.3 %shard_map.248 = (bf16[1,512,512]{2,1,0:T(8,128)(2,1)S(1)}, bf16[1,512,512]{2,1,0:T(8,128)(2,1)S(1)}, bf16[1,512,512]{2,1,0:T(8,128)(2,1)S(1)}, bf16[1,512,512]{2,1,0:T(8,128)(2,1)S(1)}) custom-call(f32[2048,128]{1,0:T(8,128)S(1)} %copy-done.2, f32[2048,128]{1,0:T(8,128)S(1)} %copy-done.3, bf16[1,512,512]{2,1,0:T(8,128)(2,1)S(1)} %bitcast.128, ...), custom_call_target="tpu_custom_call" | custom-call | flops 3221225472 | bytes 8388608 | tf_op jit(solution)/shard_map/pallas_call | solution.py:180
  380.3 30.8 %shard_map.247 = (bf16[1,512,512]{2,1,0:T(8,128)(2,1)S(1)}, bf16[1,512,512]{2,1,0:T(8,128)(2,1)S(1)}, bf16[1,512,512]{2,1,0:T(8,128)(2,1)S(1)}, bf16[1,512,512]{2,1,0:T(8,128)(2,1)S(1)}) custom-call(f32[2048,128]{1,0:T(8,128)S(1)} %copy-done.2, f32[2048,128]{1,0:T(8,128)S(1)} %copy-done.3, bf16[1,512,512]{2,1,0:T(8,128)(2,1)S(1)} %bitcast.127, ...), custom_call_target="tpu_custom_call" | custom-call | flops 3221225472 | bytes 8388608 | tf_op jit(solution)/shard_map/pallas_call | solution.py:180
  413.0 30.8 %shard_map.246 = (bf16[1,512,512]{2,1,0:T(8,128)(2,1)S(1)}, bf16[1,512,512]{2,1,0:T(8,128)(2,1)S(1)}, bf16[1,512,512]{2,1,0:T(8,128)(2,1)S(1)}, bf16[1,512,512]{2,1,0:T(8,128)(2,1)S(1)}) custom-call(f32[2048,128]{1,0:T(8,128)S(1)} %copy-done.2, f32[2048,128]{1,0:T(8,128)S(1)} %copy-done.3, bf16[1,512,512]{2,1,0:T(8,128)(2,1)S(1)} %bitcast.126, ...), custom_call_target="tpu_custom_call" | custom-call | flops 3221225472 | bytes 8388608 | tf_op jit(solution)/shard_map/pallas_call | solution.py:180
  446.0 30.5 %shard_map.245 = (bf16[1,512,512]{2,1,0:T(8,128)(2,1)S(1)}, bf16[1,512,512]{2,1,0:T(8,128)(2,1)}, bf16[1,512,512]{2,1,0:T(8,128)(2,1)}, bf16[1,512,512]{2,1,0:T(8,128)(2,1)}) custom-call(f32[2048,128]{1,0:T(8,128)S(1)} %copy-done.2, f32[2048,128]{1,0:T(8,128)S(1)} %copy-done.3, bf16[1,512,512]{2,1,0:T(8,128)(2,1)S(1)} %bitcast.125, ...), custom_call_target="tpu_custom_call" | custom-call | flops 3221225472 | bytes 8388608 | tf_op jit(solution)/shard_map/pallas_call | solution.py:180
  483.7 9.0 collective-permute-done.15
  494.4 8.8 collective-permute-done.16
  537.7 24.8 %multiply_convert_fusion.1 = (bf16[2048,2048]{1,0:T(8,128)(2,1)}, f32[2048,2048]{1,0:T(8,128)}) fusion(f32[2048]{0:T(1024)S(1)} %maximum_select_fusion.20, f32[2048,2048]{1,0:T(8,128)} %fusion.127, bf16[2048,1024]{0,1:T(8,128)(2,1)S(1)} %copy-done.23, bf16[512,2048]{1,0:T(8,128)(2,1)} %collective-permute-done.29, ...), kind=kOutput, calls=%fused_computation.13 | convolution fusion | flops 8638169088 | bytes 50339840 | tf_op jit(solution)/shard_map/dot_general | solution.py:22
  565.6 11.2 copy.125
  576.7 5.6 copy.144
  582.4 8.9 fusion.130
  591.3 24.1 %convert_reduce_fusion.2 = (f32[2048]{0:T(1024)}, bf16[2048,2048]{1,0:T(8,128)(2,1)}) fusion(f32[2048,2048]{1,0:T(8,128)} %get-tuple-element.211, f32[2048,2048]{1,0:T(8,128)} %fusion.55, bf16[1024,1024]{1,0:T(8,128)(2,1)} %collective-permute-done.31, bf16[1024,1024]{1,0:T(8,128)(2,1)} %collective-permute-done.32, pred[]{:T(512)S(6)} %eq.7, ...), kind=kOutput, calls=%fused_computation.11 | convolution fusion | flops 8671721472 | bytes 50339844 | tf_op jit(solution)/shard_map/dot_general | solution.py:22
  615.4 14.7 %fusion.129 = f32[2048,1024]{0,1:T(8,128)} fusion(bf16[2048,2048]{1,0:T(8,128)(2,1)} %get-tuple-element.209, bf16[1024,2048]{1,0:T(8,128)(2,1)} %param.23), kind=kOutput, calls=%fused_computation.274 | convolution fusion | flops 8589934592 | bytes 20971520 | tf_op jit(solution)/shard_map/dot_general | solution.py:22
  630.2 17.0 %fusion.78 = f32[2048,1024]{0,1:T(8,128)} fusion(bf16[2048,2048]{1,0:T(8,128)(2,1)} %get-tuple-element.209, bf16[512,2048]{1,0:T(8,128)(2,1)} %collective-permute-done.29, bf16[512,2048]{1,0:T(8,128)(2,1)} %collective-permute-done.30, pred[]{:T(512)S(6)} %eq.7), kind=kOutput, calls=%fused_computation.148 | convolution fusion | flops 8608808960 | bytes 20971520 | tf_op jit(solution)/shard_map/dot_general | solution.py:22
  647.3 23.7 %multiply_reduce_fusion.3 = (f32[1024]{0:T(1024)}, f32[2048]{0:T(1024)S(1)}, f32[2048]{0:T(1024)S(1)}, f32[1024]{0:T(1024)}, f32[1024]{0:T(1024)}, /*index=5*/f3...) fusion(bf16[2048,1024]{0,1:T(8,128)(2,1)S(1)} %copy-done.10, ...), kind=kOutput, calls=%fused_computation.25 | convolution fusion | flops 6527885312 | bytes 51511296 | tf_op jit(solution)/shard_map/dot_general | solution.py:22
  671.0 17.1 %multiply_convert_fusion.3 = (bf16[2048,1024]{0,1:T(8,128)(2,1)S(1)}, bf16[2048,1024]{0,1:T(8,128)(2,1)}) fusion(bf16[2048,1024]{0,1:T(8,128)(2,1)S(1)} %copy-done.10, f32[2048,1024]{0,1:T(8,128)} %fusion.78, f32[2048,1024]{0,1:T(8,128)} %get-tuple-element.212, f32[2048]{0:T(1024)S(1)} %add_multiply_fusion.1, f32[2048]{0:T(1024)S(1)} %add_multiply_fusion.2, ...), kind=kLoop, calls=%fused_computation.21 | loop fusion | flops 58720256 | bytes 50397184 | tf_op jit(solution)/shard_map/convert_element_type | solution.py:342
  688.1 8.7 maximum_select_fusion.1
  706.1 5.3 convert_reduce_fusion.1
  714.9 16.0 %fusion.77 = f32[2048,1024]{0,1:T(8,128)} fusion(bf16[2048,2048]{1,0:T(8,128)(2,1)} %get-tuple-element.210, bf16[1024,1024]{1,0:T(8,128)(2,1)} %collective-permute-done.31, bf16[1024,1024]{1,0:T(8,128)(2,1)} %collective-permute-done.32, pred[]{:T(512)S(6)} %eq.7), kind=kOutput, calls=%fused_computation.147 | convolution fusion | flops 8608808960 | bytes 20971520 | tf_op jit(solution)/shard_map/dot_general | solution.py:22
  730.8 6.3 add_convert_fusion.1
  737.2 14.0 %fusion.128 = f32[2048,1024]{0,1:T(8,128)} fusion(bf16[2048,2048]{1,0:T(8,128)(2,1)} %get-tuple-element.210, bf16[2048,1024]{1,0:T(8,128)(2,1)S(1)} %copy-done.30), kind=kOutput, calls=%fused_computation.273 | convolution fusion | flops 8589934592 | bytes 20971520 | tf_op jit(solution)/shard_map/dot_general | solution.py:22
  751.2 5.8 add_convert_fusion
  757.0 6.4 maximum_select_fusion
  763.4 9.9 fusion.39
  773.3 9.8 fusion.36
  783.1 5.7 convolution_convert_fusion
  788.9 6.1 convolution_convert_fusion.1
  795.0 7.0 convolution_convert_fusion.2
  802.8 8.0 fusion.26
  818.5 6.3 fusion.15
  824.9 6.5 add_convert_fusion.16
  833.3 7.9 add_convert_fusion.8
  841.6 9.8 add_convert_fusion.11
  854.3 5.0 fusion.34
  859.3 9.6 collective-permute-done.35
  872.2 41.7 %collective-permute-done.50 = bf16[1024,1024]{1,0:T(8,128)(2,1)} collective-permute-done((bf16[1024,1024]{1,0:T(8,128)(2,1)}, bf16[1024,1024]{1,0:T(8,128)(2,1)}, u32[]{:S(2)}, u32[]{:S(2)}) %collective-permute-start.50) | collective-permute-done | bytes 2097184 | tf_op jit(solution)/shard_map/ppermute | solution.py:26
  919.4 39.1 %collective-permute-done.45 = bf16[512,2048]{1,0:T(8,128)(2,1)} collective-permute-done((bf16[512,2048]{1,0:T(8,128)(2,1)}, bf16[512,2048]{1,0:T(8,128)(2,1)}, u32[]{:S(2)}, u32[]{:S(2)}) %collective-permute-start.45) | collective-permute-done | bytes 2097184 | tf_op jit(solution)/shard_map/ppermute | solution.py:26
  968.4 9.6 collective-permute-done.40
  982.0 14.1 %collective-permute-done.51 = bf16[1024,1024]{1,0:T(8,128)(2,1)S(1)} collective-permute-done((bf16[1024,1024]{1,0:T(8,128)(2,1)S(1)}, bf16[1024,1024]{1,0:T(8,128)(2,1)S(1)}, u32[]{:S(2)}, u32[]{:S(2)}) %collective-permute-start.51) | collective-permute-done | bytes 2097184 | tf_op jit(solution)/shard_map/ppermute | solution.py:26
  997.2 43.9 %collective-permute-done.46 = bf16[512,2048]{1,0:T(8,128)(2,1)S(1)} collective-permute-done((bf16[512,2048]{1,0:T(8,128)(2,1)S(1)}, bf16[512,2048]{1,0:T(8,128)(2,1)S(1)}, u32[]{:S(2)}, u32[]{:S(2)}) %collective-permute-start.46) | collective-permute-done | bytes 2097184 | tf_op jit(solution)/shard_map/ppermute | solution.py:26
  1044.5 6.2 collective-permute-done.41
  1052.1 25.0 %psum.15 = f32[5632]{0:T(1024)S(1)} all-reduce(f32[5632]{0:T(1024)S(1)} %pad_maximum_fusion.8), channel_id=1, replica_groups=mesh['seq'=4,'tensor'=4,'dp'=2] {'seq','dp'}, use_global_device_ids=true, to_apply=%region_24.25 | all-reduce | flops 5632 | bytes 45056 | tf_op jit(solution)/shard_map/psum | solution.py:364
  1078.5 39.7 %psum.14 = f32[2048,4]{0,1:T(4,128)S(1)} all-reduce(f32[2048,4]{0,1:T(4,128)S(1)} %maximum_select_fusion.18), channel_id=1, replica_groups=mesh['seq'=4,'tensor'=4,'dp'=2] {'seq','dp','tensor'}, use_global_device_ids=true, to_apply=%region_20.21 | all-reduce | flops 8192 | bytes 65536 | tf_op jit(solution)/shard_map/psum | solution.py:363
  1125.7 5.8 fusion.8
  1131.5 6.9 fusion.7
  1142.8 5.5 copy.132
  (403 shorter events, 234.8 us)
Async XLA Ops:
  7.3 1131.1 %reduce-scatter.5.cloned.1.call-start = ((), (), s32[]{:S(2)}) async-start(), calls=%async_computation.3 | async-start | bytes 10485760 | tf_op jit(solution)/shard_map/reduce_scatter | solution.py:344
  10.7 284.6 %collective-permute-start.29 = (bf16[512,2048]{1,0:T(8,128)(2,1)}, bf16[512,2048]{1,0:T(8,128)(2,1)}, u32[]{:S(2)}, u32[]{:S(2)}) collective-permute-start(bf16[512,2048]{1,0:T(8,128)(2,1)} %constant_dynamic-slice_fusion.3), channel_id=1, source_target_pairs={{0,1},{1,0},{2,3},{3,2},{4,5},{5,4},{6,7},{7,6},{8,9},{9,8},{10,11... | collective-permute-start | bytes 6291464 | tf_op jit(solution)/shard_map/ppermute | solution.py:26
  13.6 72.8 %copy-start.43 = (f32[1024]{0:T(1024)}, f32[1024]{0:T(1024)S(1)}, u32[]{:S(2)}) copy-start(f32[1024]{0:T(1024)S(1)} %get-tuple-element.200) | copy-start | bytes 12292
  13.7 72.7 %copy-start.45 = (f32[1024]{0:T(1024)}, f32[1024]{0:T(1024)S(1)}, u32[]{:S(2)}) copy-start(f32[1024]{0:T(1024)S(1)} %get-tuple-element.207) | copy-start | bytes 12292
  14.2 72.1 %collective-permute-start = (bf16[7936]{0:T(1024)(128)(2,1)S(1)}, bf16[7936]{0:T(1024)(128)(2,1)S(1)}, u32[]{:S(2)}, u32[]{:S(2)}) collective-permute-start(bf16[7936]{0:T(1024)(128)(2,1)S(1)} %dynamic-update-slice.19), channel_id=1, source_target_pairs={{0,1},{1,0},{2,3},{3,2},{4,5},{5,4},{6,7},{7,6},{8,9},{9,8},{10,11... | collective-permute-start | bytes 47624 | tf_op jit(solution)/shard_map/ppermute | solution.py:26
  17.4 278.2 %collective-permute-start.31 = (bf16[1024,1024]{1,0:T(8,128)(2,1)}, bf16[1024,1024]{1,0:T(8,128)(2,1)}, u32[]{:S(2)}, u32[]{:S(2)}) collective-permute-start(bf16[1024,1024]{1,0:T(8,128)(2,1)} %constant_dynamic-slice_fusion.2), channel_id=1, source_target_pairs={{0,1},{1,0},{2,3},{3,2},{4,5},{5,4},{6,7},{7,6},{8,9},{9,8},{10,11... | collective-permute-start | bytes 6291464 | tf_op jit(solution)/shard_map/ppermute | solution.py:26
  20.6 129.2 %collective-permute-start.1 = (bf16[512,1536]{1,0:T(8,128)(2,1)}, bf16[512,1536]{1,0:T(8,128)(2,1)}, u32[]{:S(2)}, u32[]{:S(2)}) collective-permute-start(bf16[512,1536]{1,0:T(8,128)(2,1)} %constant_dynamic-slice_fusion.37), channel_id=1, source_target_pairs={{0,1},{1,0},{2,3},{3,2},{4,5},{5,4},{6,7},{7,6},{8,9},{9,8},{10,11... | collective-permute-start | bytes 4718600 | tf_op jit(solution)/shard_map/ppermute | solution.py:26
  22.5 127.3 %collective-permute-start.3 = (bf16[256,1024]{1,0:T(8,128)(2,1)}, bf16[256,1024]{1,0:T(8,128)(2,1)}, u32[]{:S(2)}, u32[]{:S(2)}) collective-permute-start(bf16[256,1024]{1,0:T(8,128)(2,1)} %constant_dynamic-slice_fusion.36), channel_id=1, source_target_pairs={{0,1},{1,0},{2,3},{3,2},{4,5},{5,4},{6,7},{7,6},{8,9},{9,8},{10,11... | collective-permute-start | bytes 1572872 | tf_op jit(solution)/shard_map/ppermute | solution.py:26
  86.3 73.6 %copy-start.49 = (bf16[7936]{0:T(1024)(128)(2,1)}, bf16[7936]{0:T(1024)(128)(2,1)S(1)}, u32[]{:S(2)}) copy-start(bf16[7936]{0:T(1024)(128)(2,1)S(1)} %collective-permute-done) | copy-start | bytes 47620
  86.4 74.3 %slice-start.2 = ((s8[8388608]{0:T(1024)(128)(4,1)}), s8[4194304]{0:T(1024)(128)(4,1)S(1)}, s32[]{:S(2)}) async-start(s8[8388608]{0:T(1024)(128)(4,1)} %bitcast.144), calls=%async_computation.6 | async-start | bytes 8388608
  97.9 62.0 %copy-start.21 = (bf16[2048,1024]{0,1:T(8,128)(2,1)}, bf16[2048,1024]{0,1:T(8,128)(2,1)S(1)}, u32[]{:S(2)}) copy-start(bf16[2048,1024]{0,1:T(8,128)(2,1)S(1)} %get-tuple-element.187) | copy-start | bytes 12582916
  149.8 10.1 collective-permute-start.4
  149.8 24.6 %collective-permute-start.2 = (bf16[512,1536]{1,0:T(8,128)(2,1)}, bf16[512,1536]{1,0:T(8,128)(2,1)}, u32[]{:S(2)}, u32[]{:S(2)}) collective-permute-start(bf16[512,1536]{1,0:T(8,128)(2,1)} %collective-permute-done.1), channel_id=1, source_target_pairs={{0,8},{8,0},{16,24},{24,16},{1,9},{9,1},{17,25},{25,17},{2,10},{10... | collective-permute-start | bytes 4718600 | tf_op jit(solution)/shard_map/ppermute | solution.py:26
  256.6 40.7 %collective-permute-start.23 = (bf16[1,512,512]{2,1,0:T(8,128)(2,1)}, bf16[1,512,512]{2,1,0:T(8,128)(2,1)}, u32[]{:S(2)}, u32[]{:S(2)}) collective-permute-start(bf16[1,512,512]{2,1,0:T(8,128)(2,1)} %bitcast.188), channel_id=1, source_target_pairs={{0,8},{8,0},{16,24},{24,16},{1,9},{9,1},{17,25},{25,17},{2,10},{10... | collective-permute-start | bytes 1572872 | tf_op jit(solution)/shard_map/ppermute | solution.py:26
  260.1 37.2 %collective-permute-start.24 = (bf16[1,512,512]{2,1,0:T(8,128)(2,1)}, bf16[1,512,512]{2,1,0:T(8,128)(2,1)}, u32[]{:S(2)}, u32[]{:S(2)}) collective-permute-start(bf16[1,512,512]{2,1,0:T(8,128)(2,1)} %bitcast.187), channel_id=1, source_target_pairs={{0,16},{8,24},{16,0},{24,8},{1,17},{9,25},{17,1},{25,9},{2,18},{10... | collective-permute-start | bytes 1572872 | tf_op jit(solution)/shard_map/ppermute | solution.py:26
  265.3 32.4 %collective-permute-start.25 = (bf16[1,512,512]{2,1,0:T(8,128)(2,1)}, bf16[1,512,512]{2,1,0:T(8,128)(2,1)}, u32[]{:S(2)}, u32[]{:S(2)}) collective-permute-start(bf16[1,512,512]{2,1,0:T(8,128)(2,1)} %bitcast.186), channel_id=1, source_target_pairs={{0,24},{8,16},{16,8},{24,0},{1,25},{9,17},{17,9},{25,1},{2,26},{10... | collective-permute-start | bytes 1572872 | tf_op jit(solution)/shard_map/ppermute | solution.py:26
  295.2 47.6 %collective-permute-start.17 = (bf16[1,512,512]{2,1,0:T(8,128)(2,1)}, bf16[1,512,512]{2,1,0:T(8,128)(2,1)}, u32[]{:S(2)}, u32[]{:S(2)}) collective-permute-start(bf16[1,512,512]{2,1,0:T(8,128)(2,1)} %bitcast.183), channel_id=1, source_target_pairs={{0,8},{8,0},{16,24},{24,16},{1,9},{9,1},{17,25},{25,17},{2,10},{10... | collective-permute-start | bytes 1572872 | tf_op jit(solution)/shard_map/ppermute | solution.py:26
  295.5 47.3 %collective-permute-start.18 = (bf16[1,512,512]{2,1,0:T(8,128)(2,1)}, bf16[1,512,512]{2,1,0:T(8,128)(2,1)}, u32[]{:S(2)}, u32[]{:S(2)}) collective-permute-start(bf16[1,512,512]{2,1,0:T(8,128)(2,1)} %bitcast.181), channel_id=1, source_target_pairs={{0,16},{8,24},{16,0},{24,8},{1,17},{9,25},{17,1},{25,9},{2,18},{10... | collective-permute-start | bytes 1572872 | tf_op jit(solution)/shard_map/ppermute | solution.py:26
  297.2 80.8 %collective-permute-start.19 = (bf16[1,512,512]{2,1,0:T(8,128)(2,1)}, bf16[1,512,512]{2,1,0:T(8,128)(2,1)}, u32[]{:S(2)}, u32[]{:S(2)}) collective-permute-start(bf16[1,512,512]{2,1,0:T(8,128)(2,1)} %bitcast.177), channel_id=1, source_target_pairs={{0,24},{8,16},{16,8},{24,0},{1,25},{9,17},{17,9},{25,1},{2,26},{10... | collective-permute-start | bytes 1572872 | tf_op jit(solution)/shard_map/ppermute | solution.py:26
  297.3 82.6 %collective-permute-start.11 = (bf16[1,512,512]{2,1,0:T(8,128)(2,1)}, bf16[1,512,512]{2,1,0:T(8,128)(2,1)}, u32[]{:S(2)}, u32[]{:S(2)}) collective-permute-start(bf16[1,512,512]{2,1,0:T(8,128)(2,1)} %bitcast.179), channel_id=1, source_target_pairs={{0,8},{8,0},{16,24},{24,16},{1,9},{9,1},{17,25},{25,17},{2,10},{10... | collective-permute-start | bytes 1572872 | tf_op jit(solution)/shard_map/ppermute | solution.py:26
  297.7 82.2 %collective-permute-start.12 = (bf16[1,512,512]{2,1,0:T(8,128)(2,1)}, bf16[1,512,512]{2,1,0:T(8,128)(2,1)}, u32[]{:S(2)}, u32[]{:S(2)}) collective-permute-start(bf16[1,512,512]{2,1,0:T(8,128)(2,1)} %bitcast.178), channel_id=1, source_target_pairs={{0,16},{8,24},{16,0},{24,8},{1,17},{9,25},{17,1},{25,9},{2,18},{10... | collective-permute-start | bytes 1572872 | tf_op jit(solution)/shard_map/ppermute | solution.py:26
  342.9 68.3 %collective-permute-start.13 = (bf16[1,512,512]{2,1,0:T(8,128)(2,1)}, bf16[1,512,512]{2,1,0:T(8,128)(2,1)S(1)}, u32[]{:S(2)}, u32[]{:S(2)}) collective-permute-start(bf16[1,512,512]{2,1,0:T(8,128)(2,1)} %bitcast.185), channel_id=1, source_target_pairs={{0,24},{8,16},{16,8},{24,0},{1,25},{9,17},{17,9},{25,1},{2,26},{10... | collective-permute-start | bytes 1572872 | tf_op jit(solution)/shard_map/ppermute | solution.py:26
  342.9 70.1 %collective-permute-start.5 = (bf16[1,512,512]{2,1,0:T(8,128)(2,1)}, bf16[1,512,512]{2,1,0:T(8,128)(2,1)S(1)}, u32[]{:S(2)}, u32[]{:S(2)}) collective-permute-start(bf16[1,512,512]{2,1,0:T(8,128)(2,1)} %bitcast.184), channel_id=1, source_target_pairs={{0,8},{8,0},{16,24},{24,16},{1,9},{9,1},{17,25},{25,17},{2,10},{10... | collective-permute-start | bytes 1572872 | tf_op jit(solution)/shard_map/ppermute | solution.py:26
  378.1 65.7 %collective-permute-start.6 = (bf16[1,512,512]{2,1,0:T(8,128)(2,1)S(1)}, bf16[1,512,512]{2,1,0:T(8,128)(2,1)S(1)}, u32[]{:S(2)}, u32[]{:S(2)}) collective-permute-start(bf16[1,512,512]{2,1,0:T(8,128)(2,1)S(1)} %bitcast.182), channel_id=1, source_target_pairs={{0,16},{8,24},{16,0},{24,8},{1,17},{9,25},{17,1},{25,9},{2,18},{10... | collective-permute-start | bytes 1572872 | tf_op jit(solution)/shard_map/ppermute | solution.py:26
  379.9 64.4 %collective-permute-start.7 = (bf16[1,512,512]{2,1,0:T(8,128)(2,1)S(1)}, bf16[1,512,512]{2,1,0:T(8,128)(2,1)S(1)}, u32[]{:S(2)}, u32[]{:S(2)}) collective-permute-start(bf16[1,512,512]{2,1,0:T(8,128)(2,1)S(1)} %bitcast.180), channel_id=1, source_target_pairs={{0,24},{8,16},{16,8},{24,0},{1,25},{9,17},{17,9},{25,1},{2,26},{10... | collective-permute-start | bytes 1572872 | tf_op jit(solution)/shard_map/ppermute | solution.py:26
  379.9 66.1 %collective-permute-start.26 = (bf16[1,512,512]{2,1,0:T(8,128)(2,1)S(1)}, bf16[1,512,512]{2,1,0:T(8,128)(2,1)S(1)}, u32[]{:S(2)}, u32[]{:S(2)}) collective-permute-start(bf16[1,512,512]{2,1,0:T(8,128)(2,1)S(1)} %get-tuple-element.43), channel_id=1, source_target_pairs={{0,8},{8,0},{16,24},{24,16},{1,9},{9,1},{17,25},{25,17},{2,10},{10... | collective-permute-start | bytes 1572872 | tf_op jit(solution)/shard_map/ppermute | solution.py:26
  411.2 65.3 %collective-permute-start.27 = (bf16[1,512,512]{2,1,0:T(8,128)(2,1)S(1)}, bf16[1,512,512]{2,1,0:T(8,128)(2,1)S(1)}, u32[]{:S(2)}, u32[]{:S(2)}) collective-permute-start(bf16[1,512,512]{2,1,0:T(8,128)(2,1)S(1)} %get-tuple-element.44), channel_id=1, source_target_pairs={{0,16},{8,24},{16,0},{24,8},{1,17},{9,25},{17,1},{25,9},{2,18},{10... | collective-permute-start | bytes 1572872 | tf_op jit(solution)/shard_map/ppermute | solution.py:26
  412.9 64.0 %collective-permute-start.28 = (bf16[1,512,512]{2,1,0:T(8,128)(2,1)S(1)}, bf16[1,512,512]{2,1,0:T(8,128)(2,1)S(1)}, u32[]{:S(2)}, u32[]{:S(2)}) collective-permute-start(bf16[1,512,512]{2,1,0:T(8,128)(2,1)S(1)} %get-tuple-element.45), channel_id=1, source_target_pairs={{0,24},{8,16},{16,8},{24,0},{1,25},{9,17},{17,9},{25,1},{2,26},{10... | collective-permute-start | bytes 1572872 | tf_op jit(solution)/shard_map/ppermute | solution.py:26
  443.8 33.6 %collective-permute-start.20 = (bf16[1,512,512]{2,1,0:T(8,128)(2,1)S(1)}, bf16[1,512,512]{2,1,0:T(8,128)(2,1)S(1)}, u32[]{:S(2)}, u32[]{:S(2)}) collective-permute-start(bf16[1,512,512]{2,1,0:T(8,128)(2,1)S(1)} %get-tuple-element.39), channel_id=1, source_target_pairs={{0,8},{8,0},{16,24},{24,16},{1,9},{9,1},{17,25},{25,17},{2,10},{10... | collective-permute-start | bytes 1572872 | tf_op jit(solution)/shard_map/ppermute | solution.py:26
  444.3 33.6 %collective-permute-start.21 = (bf16[1,512,512]{2,1,0:T(8,128)(2,1)S(1)}, bf16[1,512,512]{2,1,0:T(8,128)(2,1)S(1)}, u32[]{:S(2)}, u32[]{:S(2)}) collective-permute-start(bf16[1,512,512]{2,1,0:T(8,128)(2,1)S(1)} %get-tuple-element.40), channel_id=1, source_target_pairs={{0,16},{8,24},{16,0},{24,8},{1,17},{9,25},{17,1},{25,9},{2,18},{10... | collective-permute-start | bytes 1572872 | tf_op jit(solution)/shard_map/ppermute | solution.py:26
  446.0 33.6 %collective-permute-start.22 = (bf16[1,512,512]{2,1,0:T(8,128)(2,1)S(1)}, bf16[1,512,512]{2,1,0:T(8,128)(2,1)S(1)}, u32[]{:S(2)}, u32[]{:S(2)}) collective-permute-start(bf16[1,512,512]{2,1,0:T(8,128)(2,1)S(1)} %get-tuple-element.41), channel_id=1, source_target_pairs={{0,24},{8,16},{16,8},{24,0},{1,25},{9,17},{17,9},{25,1},{2,26},{10... | collective-permute-start | bytes 1572872 | tf_op jit(solution)/shard_map/ppermute | solution.py:26
  476.5 60.7 %collective-permute-start.30 = (bf16[512,2048]{1,0:T(8,128)(2,1)}, bf16[512,2048]{1,0:T(8,128)(2,1)}, u32[]{:S(2)}, u32[]{:S(2)}) collective-permute-start(bf16[512,2048]{1,0:T(8,128)(2,1)} %collective-permute-done.29), channel_id=1, source_target_pairs={{0,8},{8,0},{16,24},{24,16},{1,9},{9,1},{17,25},{25,17},{2,10},{10... | collective-permute-start | bytes 6291464 | tf_op jit(solution)/shard_map/ppermute | solution.py:26
  476.9 114.4 %collective-permute-start.32 = (bf16[1024,1024]{1,0:T(8,128)(2,1)}, bf16[1024,1024]{1,0:T(8,128)(2,1)}, u32[]{:S(2)}, u32[]{:S(2)}) collective-permute-start(bf16[1024,1024]{1,0:T(8,128)(2,1)} %collective-permute-done.31), channel_id=1, source_target_pairs={{0,8},{8,0},{16,24},{24,16},{1,9},{9,1},{17,25},{25,17},{2,10},{10... | collective-permute-start | bytes 6291464 | tf_op jit(solution)/shard_map/ppermute | solution.py:26
  477.4 5.8 collective-permute-start.14
  477.9 14.8 %collective-permute-start.15 = (bf16[1,512,512]{2,1,0:T(8,128)(2,1)S(1)}, bf16[1,512,512]{2,1,0:T(8,128)(2,1)S(1)}, u32[]{:S(2)}, u32[]{:S(2)}) collective-permute-start(bf16[1,512,512]{2,1,0:T(8,128)(2,1)S(1)} %get-tuple-element.36), channel_id=1, source_target_pairs={{0,16},{8,24},{16,0},{24,8},{1,17},{9,25},{17,1},{25,9},{2,18},{10... | collective-permute-start | bytes 1572872 | tf_op jit(solution)/shard_map/ppermute | solution.py:26
  479.6 23.5 %collective-permute-start.16 = (bf16[1,512,512]{2,1,0:T(8,128)(2,1)S(1)}, bf16[1,512,512]{2,1,0:T(8,128)(2,1)S(1)}, u32[]{:S(2)}, u32[]{:S(2)}) collective-permute-start(bf16[1,512,512]{2,1,0:T(8,128)(2,1)S(1)} %get-tuple-element.37), channel_id=1, source_target_pairs={{0,24},{8,16},{16,8},{24,0},{1,25},{9,17},{17,9},{25,1},{2,26},{10... | collective-permute-start | bytes 1572872 | tf_op jit(solution)/shard_map/ppermute | solution.py:26
  483.3 38.4 %collective-permute-start.8 = (bf16[1,512,512]{2,1,0:T(8,128)(2,1)}, bf16[1,512,512]{2,1,0:T(8,128)(2,1)}, u32[]{:S(2)}, u32[]{:S(2)}) collective-permute-start(bf16[1,512,512]{2,1,0:T(8,128)(2,1)} %get-tuple-element.31), channel_id=1, source_target_pairs={{0,8},{8,0},{16,24},{24,16},{1,9},{9,1},{17,25},{25,17},{2,10},{10... | collective-permute-start | bytes 1572872 | tf_op jit(solution)/shard_map/ppermute | solution.py:26
  492.7 29.0 %collective-permute-start.9 = (bf16[1,512,512]{2,1,0:T(8,128)(2,1)}, bf16[1,512,512]{2,1,0:T(8,128)(2,1)}, u32[]{:S(2)}, u32[]{:S(2)}) collective-permute-start(bf16[1,512,512]{2,1,0:T(8,128)(2,1)} %get-tuple-element.32), channel_id=1, source_target_pairs={{0,16},{8,24},{16,0},{24,8},{1,17},{9,25},{17,1},{25,9},{2,18},{10... | collective-permute-start | bytes 1572872 | tf_op jit(solution)/shard_map/ppermute | solution.py:26
  503.2 21.7 %collective-permute-start.10 = (bf16[1,512,512]{2,1,0:T(8,128)(2,1)}, bf16[1,512,512]{2,1,0:T(8,128)(2,1)}, u32[]{:S(2)}, u32[]{:S(2)}) collective-permute-start(bf16[1,512,512]{2,1,0:T(8,128)(2,1)} %get-tuple-element.33), channel_id=1, source_target_pairs={{0,24},{8,16},{16,8},{24,0},{1,25},{9,17},{17,9},{25,1},{2,26},{10... | collective-permute-start | bytes 1572872 | tf_op jit(solution)/shard_map/ppermute | solution.py:26
  696.9 451.4 %reduce-scatter.3.cloned.1.call-start = ((), (), s32[]{:S(2)}) async-start(), calls=%async_computation.2 | async-start | bytes 10485760 | tf_op jit(solution)/shard_map/reduce_scatter | solution.py:318
  802.1 22.7 %collective-permute-start.34 = (bf16[512,1536]{1,0:T(8,128)(2,1)S(1)}, bf16[512,1536]{1,0:T(8,128)(2,1)}, u32[]{:S(2)}, u32[]{:S(2)}) collective-permute-start(bf16[512,1536]{1,0:T(8,128)(2,1)S(1)} %convolution_convert_fusion.2), channel_id=1, source_target_pairs={{0,8},{8,0},{16,24},{24,16},{1,9},{9,1},{17,25},{25,17},{2,10},{10... | collective-permute-start | bytes 4718600 | tf_op jit(solution)/shard_map/ppermute | solution.py:26
  815.9 15.6 %collective-permute-start.49 = (bf16[1024,1024]{1,0:T(8,128)(2,1)}, bf16[1024,1024]{1,0:T(8,128)(2,1)S(1)}, u32[]{:S(2)}, u32[]{:S(2)}) collective-permute-start(bf16[1024,1024]{1,0:T(8,128)(2,1)} %fusion.39), channel_id=1, source_target_pairs={{0,8},{8,0},{16,24},{24,16},{1,9},{9,1},{17,25},{25,17},{2,10},{10... | collective-permute-start | bytes 6291464 | tf_op jit(solution)/shard_map/ppermute | solution.py:26
  815.9 55.7 %collective-permute-start.48 = (bf16[1024,1024]{1,0:T(8,128)(2,1)}, bf16[1024,1024]{1,0:T(8,128)(2,1)}, u32[]{:S(2)}, u32[]{:S(2)}) collective-permute-start(bf16[1024,1024]{1,0:T(8,128)(2,1)} %fusion.36), channel_id=1, source_target_pairs={{0,8},{8,0},{16,24},{24,16},{1,9},{9,1},{17,25},{25,17},{2,10},{10... | collective-permute-start | bytes 6291464 | tf_op jit(solution)/shard_map/ppermute | solution.py:26
  816.4 24.8 %collective-permute-start.44 = (bf16[512,2048]{1,0:T(8,128)(2,1)}, bf16[512,2048]{1,0:T(8,128)(2,1)}, u32[]{:S(2)}, u32[]{:S(2)}) collective-permute-start(bf16[512,2048]{1,0:T(8,128)(2,1)} %convolution_convert_fusion), channel_id=1, source_target_pairs={{0,8},{8,0},{16,24},{24,16},{1,9},{9,1},{17,25},{25,17},{2,10},{10... | collective-permute-start | bytes 6291464 | tf_op jit(solution)/shard_map/ppermute | solution.py:26
  816.5 102.5 %collective-permute-start.43 = (bf16[512,2048]{1,0:T(8,128)(2,1)}, bf16[512,2048]{1,0:T(8,128)(2,1)}, u32[]{:S(2)}, u32[]{:S(2)}) collective-permute-start(bf16[512,2048]{1,0:T(8,128)(2,1)} %convolution_convert_fusion.1), channel_id=1, source_target_pairs={{0,8},{8,0},{16,24},{24,16},{1,9},{9,1},{17,25},{25,17},{2,10},{10... | collective-permute-start | bytes 6291464 | tf_op jit(solution)/shard_map/ppermute | solution.py:26
  824.8 26.5 %collective-permute-start.33 = (bf16[512,1536]{1,0:T(8,128)(2,1)}, bf16[512,1536]{1,0:T(8,128)(2,1)}, u32[]{:S(2)}, u32[]{:S(2)}) collective-permute-start(bf16[512,1536]{1,0:T(8,128)(2,1)} %convolution_convert_fusion.3), channel_id=1, source_target_pairs={{0,8},{8,0},{16,24},{24,16},{1,9},{9,1},{17,25},{25,17},{2,10},{10... | collective-permute-start | bytes 4718600 | tf_op jit(solution)/shard_map/ppermute | solution.py:26
  831.4 37.5 %collective-permute-start.35 = (bf16[512,1536]{1,0:T(8,128)(2,1)}, bf16[512,1536]{1,0:T(8,128)(2,1)}, u32[]{:S(2)}, u32[]{:S(2)}) collective-permute-start(bf16[512,1536]{1,0:T(8,128)(2,1)} %add_convert_fusion.16), channel_id=1, source_target_pairs={{0,1},{1,0},{2,3},{3,2},{4,5},{5,4},{6,7},{7,6},{8,9},{9,8},{10,11... | collective-permute-start | bytes 4718600 | tf_op jit(solution)/shard_map/ppermute | solution.py:26
  841.2 72.6 %collective-permute-start.50 = (bf16[1024,1024]{1,0:T(8,128)(2,1)}, bf16[1024,1024]{1,0:T(8,128)(2,1)}, u32[]{:S(2)}, u32[]{:S(2)}) collective-permute-start(bf16[1024,1024]{1,0:T(8,128)(2,1)} %add_convert_fusion.8), channel_id=1, source_target_pairs={{0,1},{1,0},{2,3},{3,2},{4,5},{5,4},{6,7},{7,6},{8,9},{9,8},{10,11... | collective-permute-start | bytes 6291464 | tf_op jit(solution)/shard_map/ppermute | solution.py:26
  851.4 107.1 %collective-permute-start.45 = (bf16[512,2048]{1,0:T(8,128)(2,1)}, bf16[512,2048]{1,0:T(8,128)(2,1)}, u32[]{:S(2)}, u32[]{:S(2)}) collective-permute-start(bf16[512,2048]{1,0:T(8,128)(2,1)} %add_convert_fusion.11), channel_id=1, source_target_pairs={{0,1},{1,0},{2,3},{3,2},{4,5},{5,4},{6,7},{7,6},{8,9},{9,8},{10,11... | collective-permute-start | bytes 6291464 | tf_op jit(solution)/shard_map/ppermute | solution.py:26
  868.9 94.6 %collective-permute-start.39 = (bf16[256,1024]{1,0:T(8,128)(2,1)S(1)}, bf16[256,1024]{1,0:T(8,128)(2,1)S(1)}, u32[]{:S(2)}, u32[]{:S(2)}) collective-permute-start(bf16[256,1024]{1,0:T(8,128)(2,1)S(1)} %fusion.65), channel_id=1, source_target_pairs={{0,8},{8,0},{16,24},{24,16},{1,9},{9,1},{17,25},{25,17},{2,10},{10... | collective-permute-start | bytes 1572872 | tf_op jit(solution)/shard_map/ppermute | solution.py:26
  871.6 96.8 %collective-permute-start.38 = (bf16[256,1024]{1,0:T(8,128)(2,1)S(1)}, bf16[256,1024]{1,0:T(8,128)(2,1)S(1)}, u32[]{:S(2)}, u32[]{:S(2)}) collective-permute-start(bf16[256,1024]{1,0:T(8,128)(2,1)S(1)} %fusion.62), channel_id=1, source_target_pairs={{0,8},{8,0},{16,24},{24,16},{1,9},{9,1},{17,25},{25,17},{2,10},{10... | collective-permute-start | bytes 1572872 | tf_op jit(solution)/shard_map/ppermute | solution.py:26
  913.9 65.0 %collective-permute-start.36 = (bf16[512,1536]{1,0:T(8,128)(2,1)S(1)}, bf16[512,1536]{1,0:T(8,128)(2,1)}, u32[]{:S(2)}, u32[]{:S(2)}) collective-permute-start(bf16[512,1536]{1,0:T(8,128)(2,1)S(1)} %add_convert_fusion.15), channel_id=1, source_target_pairs={{0,16},{8,24},{16,0},{24,8},{1,17},{9,25},{17,1},{25,9},{2,18},{10... | collective-permute-start | bytes 4718600 | tf_op jit(solution)/shard_map/ppermute | solution.py:26
  919.0 44.5 %copy-start.29 = (bf16[256,8,4,128]{3,1,2,0:T(8,128)(2,1)S(1)}, bf16[256,8,4,128]{3,1,2,0:T(8,128)(2,1)}, u32[]{:S(2)}) copy-start(bf16[256,8,4,128]{3,1,2,0:T(8,128)(2,1)} %copy-done.27) | copy-start | bytes 6291460
  919.1 77.1 %collective-permute-start.51 = (bf16[1024,1024]{1,0:T(8,128)(2,1)S(1)}, bf16[1024,1024]{1,0:T(8,128)(2,1)S(1)}, u32[]{:S(2)}, u32[]{:S(2)}) collective-permute-start(bf16[1024,1024]{1,0:T(8,128)(2,1)S(1)} %add_convert_fusion.7), channel_id=1, source_target_pairs={{0,16},{8,24},{16,0},{24,8},{1,17},{9,25},{17,1},{25,9},{2,18},{10... | collective-permute-start | bytes 6291464 | tf_op jit(solution)/shard_map/ppermute | solution.py:26
  961.8 79.3 %collective-permute-start.46 = (bf16[512,2048]{1,0:T(8,128)(2,1)S(1)}, bf16[512,2048]{1,0:T(8,128)(2,1)S(1)}, u32[]{:S(2)}, u32[]{:S(2)}) collective-permute-start(bf16[512,2048]{1,0:T(8,128)(2,1)S(1)} %add_convert_fusion.10), channel_id=1, source_target_pairs={{0,16},{8,24},{16,0},{24,8},{1,17},{9,25},{17,1},{25,9},{2,18},{10... | collective-permute-start | bytes 6291464 | tf_op jit(solution)/shard_map/ppermute | solution.py:26
  964.8 13.3 %collective-permute-start.40 = (bf16[256,1024]{1,0:T(8,128)(2,1)S(1)}, bf16[256,1024]{1,0:T(8,128)(2,1)S(1)}, u32[]{:S(2)}, u32[]{:S(2)}) collective-permute-start(bf16[256,1024]{1,0:T(8,128)(2,1)S(1)} %add_convert_fusion.19), channel_id=1, source_target_pairs={{0,1},{1,0},{2,3},{3,2},{4,5},{5,4},{6,7},{7,6},{8,9},{9,8},{10,11... | collective-permute-start | bytes 1572872 | tf_op jit(solution)/shard_map/ppermute | solution.py:26
  978.4 72.4 %collective-permute-start.41 = (bf16[256,1024]{1,0:T(8,128)(2,1)S(1)}, bf16[256,1024]{1,0:T(8,128)(2,1)}, u32[]{:S(2)}, u32[]{:S(2)}) collective-permute-start(bf16[256,1024]{1,0:T(8,128)(2,1)S(1)} %add_convert_fusion.18), channel_id=1, source_target_pairs={{0,16},{8,24},{16,0},{24,8},{1,17},{9,25},{17,1},{25,9},{2,18},{10... | collective-permute-start | bytes 1572872 | tf_op jit(solution)/shard_map/ppermute | solution.py:26
  978.9 64.4 %slice-start = ((s8[8388608]{0:T(1024)(128)(4,1)}), s8[4194304]{0:T(1024)(128)(4,1)S(1)}, s32[]{:S(2)}) async-start(s8[8388608]{0:T(1024)(128)(4,1)} %bitcast.136), calls=%async_computation.4 | async-start | bytes 8388608
  982.0 61.3 %slice-start.1 = ((s8[8388608]{0:T(1024)(128)(4,1)}), s8[4194304]{0:T(1024)(128)(4,1)S(1)}, s32[]{:S(2)}) async-start(s8[8388608]{0:T(1024)(128)(4,1)} %bitcast.136), calls=%async_computation.5 | async-start | bytes 8388608
  982.0 138.7 %collective-permute-start.37 = (bf16[512,1536]{1,0:T(8,128)(2,1)}, bf16[512,1536]{1,0:T(8,128)(2,1)}, u32[]{:S(2)}, u32[]{:S(2)}) collective-permute-start(bf16[512,1536]{1,0:T(8,128)(2,1)} %add_convert_fusion.14), channel_id=1, source_target_pairs={{0,8},{8,0},{16,24},{24,16},{1,9},{9,1},{17,25},{25,17},{2,10},{10... | collective-permute-start | bytes 4718600 | tf_op jit(solution)/shard_map/ppermute | solution.py:26
  997.1 128.6 %collective-permute-start.52 = (bf16[1024,1024]{1,0:T(8,128)(2,1)S(1)}, bf16[1024,1024]{1,0:T(8,128)(2,1)}, u32[]{:S(2)}, u32[]{:S(2)}) collective-permute-start(bf16[1024,1024]{1,0:T(8,128)(2,1)S(1)} %add_convert_fusion.6), channel_id=1, source_target_pairs={{0,8},{8,0},{16,24},{24,16},{1,9},{9,1},{17,25},{25,17},{2,10},{10... | collective-permute-start | bytes 6291464 | tf_op jit(solution)/shard_map/ppermute | solution.py:26
  1043.3 88.2 %collective-permute-start.47 = (bf16[512,2048]{1,0:T(8,128)(2,1)}, bf16[512,2048]{1,0:T(8,128)(2,1)}, u32[]{:S(2)}, u32[]{:S(2)}) collective-permute-start(bf16[512,2048]{1,0:T(8,128)(2,1)} %add_convert_fusion.9), channel_id=1, source_target_pairs={{0,8},{8,0},{16,24},{24,16},{1,9},{9,1},{17,25},{25,17},{2,10},{10... | collective-permute-start | bytes 6291464 | tf_op jit(solution)/shard_map/ppermute | solution.py:26
  1052.0 66.9 %collective-permute-start.42 = (bf16[256,1024]{1,0:T(8,128)(2,1)S(1)}, bf16[256,1024]{1,0:T(8,128)(2,1)S(1)}, u32[]{:S(2)}, u32[]{:S(2)}) collective-permute-start(bf16[256,1024]{1,0:T(8,128)(2,1)S(1)} %add_convert_fusion.17), channel_id=1, source_target_pairs={{0,8},{8,0},{16,24},{24,16},{1,9},{9,1},{17,25},{25,17},{2,10},{10... | collective-permute-start | bytes 1572872 | tf_op jit(solution)/shard_map/ppermute | solution.py:26
  1077.8 78.6 %copy-start.48 = (f32[1024]{0:T(1024)}, f32[1024]{0:T(1024)S(1)}, u32[]{:S(2)}) copy-start(f32[1024]{0:T(1024)S(1)} %get-tuple-element.250) | copy-start | bytes 12292
  (78 other events, 1105.3 us)
Sparse Core Ops, SparseCore 0:
  697.0 146.1 reduce-scatter.4
  845.6 145.1 reduce-scatter.2

commit v2 on v1

v2 whole, which is shorter than its diff:
```python
import functools
import math

import jax
import jax.numpy as jnp
import numpy as np
from jax import lax
from jax.experimental import pallas as pl
from jax.experimental.pallas import tpu as pltpu
from jax.sharding import PartitionSpec as P

HD = 128
ROT = 32
HALF_ROT = ROT // 2
EPS = 1e-05
F32 = jnp.float32
BF16 = jnp.bfloat16
NN = (((1,), (0,)), ((), ()))
NT = (((1,), (1,)), ((), ()))
TN = (((0,), (0,)), ((), ()))
WEIGHT = 0.1
GROUPS = (1, 3)
PIECES = {"down": 4, "up": 4, "qkv": 2, "dense": 1}
VMEM_LIMIT = 60 * 1024 * 1024
KEEP, SEND, KEEP_AT, SEND_AT, SEQ, TENSOR, ORDER = 4, 6, 8, 10, 12, 13, 14


def bit(value, b):
    return lax.rem(lax.div(value, jnp.int32(1 << b)), jnp.int32(2))


def xor(value, other):
    value, other = jnp.int32(value), jnp.int32(other)
    return sum((1 << b) * lax.rem(bit(value, b) + bit(other, b), jnp.int32(2)) for b in range(4))


class Places:
    def __init__(self, straight):
        self.straight = straight

    def __getitem__(self, key):
        s = lax.axis_index("seq")
        if key == SEQ:
            return s
        if key == TENSOR:
            return lax.axis_index("tensor")
        if key >= ORDER:
            return self.head(key - ORDER)
        core = lax.rem(s, jnp.int32(2))
        d = lax.axis_index("dp")
        places = (2 * d, 2 * d + 1, 2 * (1 - d) + core, 2 * (1 - d) + 1 - core)
        if key < KEEP:
            return places[key]
        if key < KEEP_AT:
            return (core, 2, 1 - core, 3)[key - KEEP]
        return (2 * d + core, places[2], 2 * d + 1 - core, places[3])[key - KEEP_AT]

    def head(self, slot):
        return xor(lax.axis_index("seq"), slot) if self.straight else slot

    def either(self, key, i):
        return (1 - i) * self[key] + i * self[key + 1]


class Ride:
    def __init__(self, source, axis, distance, first=0, rows=None, lead=None):
        self.source, self.axis, self.distance = source, axis, distance
        self.first, self.lead = first, lead
        self.rows = source.shape[-2] - first if rows is None else rows
        self.result = None

    @property
    def shape(self):
        return (self.rows, self.source.shape[-1])

    def target(self):
        return {self.axis: xor(lax.axis_index(self.axis), self.distance)}

    def copy(self, source, target, sent, got):
        at = pl.ds(self.first, self.rows)
        return pltpu.make_async_remote_copy(
            src_ref=source.at[at] if self.lead is None else source.at[self.lead, at],
            dst_ref=target,
            send_sem=sent,
            recv_sem=got,
            device_id=self.target(),
            device_id_type=pl.DeviceIdType.MESH,
        )


class Line:
    def __init__(self, first):
        self.last = [first]
        self.rides = []
        self.count = 0

    def ride(self, *args, **kwargs):
        self.rides.append(Ride(*args, **kwargs))
        return self.rides[-1]


def mm(a, b, dims=NN):
    return lax.dot_general(a, b, dims, preferred_element_type=F32)


def swap(block, axis, distance):
    return lax.ppermute(block, axis, [(i, i ^ distance) for i in range(lax.axis_size(axis))])


def spec(block, index):
    if block is None:
        return pl.BlockSpec(memory_space=pl.ANY)
    return pl.BlockSpec(block, index)


def call(line, kernel, w, grid, inputs, outputs, scratch=(), flops=0, nbytes=0, name=None, alias=None):
    before = list(line.last)
    rides, line.rides = line.rides, []
    skip = len(before) + len(rides)
    ends = len(inputs) + len(outputs)

    def at(index):
        return None if index is None else lambda *steps: index(*steps, w)

    def on_step(last, work):
        chosen = True
        for axis, size in enumerate(grid):
            if size > 1:
                step = pl.program_id(axis)
                chosen = jnp.logical_and(chosen, step == (size - 1 if last else 0))
        if chosen is True:
            work()
        else:
            pl.when(chosen)(work)

    def body(*refs):
        sources = refs[len(before) : skip]
        own = refs[skip : skip + ends]
        targets = refs[skip + ends : skip + ends + len(rides)]
        rest = refs[skip + ends + len(rides) :]
        if not rides:
            kernel(w, *own, *rest)
            return
        *rest, sent, got = rest
        copies = lambda: [
            ride.copy(source, target, sent.at[i], got.at[i])
            for i, (ride, source, target) in enumerate(zip(rides, sources, targets))
        ]

        def start():
            barrier = pltpu.get_barrier_semaphore()
            partners = {(ride.axis, ride.distance): ride for ride in rides}
            for ride in partners.values():
                pl.semaphore_signal(
                    barrier, inc=1, device_id=ride.target(), device_id_type=pl.DeviceIdType.MESH
                )
            pl.semaphore_wait(barrier, len(partners))
            for copy in copies():
                copy.start()

        def wait():
            for copy in copies():
                copy.wait()

        on_step(False, start)
        kernel(w, *own, *rest)
        on_step(True, wait)

    params = dict(
        vmem_limit_bytes=VMEM_LIMIT, dimension_semantics=("arbitrary",) * len(grid)
    )
    sems = []
    if rides:
        params.update(collective_id=line.count, has_side_effects=True)
        line.count += 1
        sems = [pltpu.SemaphoreType.DMA((len(rides),))] * 2
    anywhere = pl.BlockSpec(memory_space=pl.ANY)
    results = pl.pallas_call(
        body,
        grid=grid,
        in_specs=[anywhere] * skip + [spec(block, at(index)) for _, block, index in inputs],
        out_specs=[spec(block, at(index)) for _, _, block, index in outputs]
        + [anywhere] * len(rides),
        scratch_shapes=list(scratch) + sems,
        out_shape=[jax.ShapeDtypeStruct(shape, dtype) for shape, dtype, _, _ in outputs]
        + [jax.ShapeDtypeStruct(ride.shape, ride.source.dtype) for ride in rides],
        compiler_params=pltpu.CompilerParams(**params),
        cost_estimate=pl.CostEstimate(
            flops=int(flops * WEIGHT), bytes_accessed=int(nbytes * WEIGHT), transcendentals=0
        ),
        input_output_aliases={} if alias is None else {skip + alias: 0},
        name=name,
    )(*before, *[ride.source for ride in rides], *[array for array, _, _ in inputs])
    for ride, result in zip(rides, results[len(outputs) :]):
        ride.result = result
    results = results[: len(outputs)]
    line.last = [results[-1]]
    return results


def fixed(*index):
    return lambda *_: index


def groups(values):
    return jnp.sum(values.reshape(values.shape[0] // 8, 8, values.shape[1]), 0)


def columns_at(w, b, size):
    return pl.ds(pl.multiple_of(w[b] * size, size), size)


def norm_kernel(w, x, cot, vectors, one, two, total):
    quarter = x.shape[1] // 4

    @pl.when(pl.program_id(0) == 0)
    def _():
        total[...] = jnp.zeros_like(total)

    values = x[...].astype(F32)
    mean = jnp.mean(values, -1, keepdims=True)
    center = values - mean
    inverse = lax.rsqrt(jnp.mean(center * center, -1, keepdims=True) + EPS)
    for b in range(4):
        at = slice(b * quarter, (b + 1) * quarter)
        unit = (x[:, columns_at(w, b, quarter)].astype(F32) - mean) * inverse
        one[:, at] = (unit * vectors[0:1, at] + vectors[1:2, at]).astype(BF16)
        two[:, at] = (unit * vectors[2:3, at] + vectors[3:4, at]).astype(BF16)
    total[...] += groups(cot[...].astype(F32))


def norms(line, w, x, cot, vectors):
    tokens, features = x.shape
    size = min(256, tokens)
    row = (size, features)
    along = lambda i, w: (i, 0)
    return call(
        line,
        norm_kernel,
        w,
        (tokens // size,),
        [(x, row, along), (cot, row, along), (vectors, vectors.shape, fixed(0, 0))],
        [
            ((tokens, features), BF16, row, along),
            ((tokens, features), BF16, row, along),
            ((8, features), F32, (8, features), fixed(0, 0)),
        ],
        flops=30 * tokens * features,
        nbytes=8 * tokens * features,
        name="norms",
    )


def turned(values):
    lane = lax.broadcasted_iota(jnp.int32, values.shape, 1)
    return jnp.where(
        lane < HALF_ROT, pltpu.roll(values, HD - HALF_ROT, 1), pltpu.roll(values, HALF_ROT, 1)
    )


def turn_tables(length):
    frequency = 10000.0 ** (-np.arange(HALF_ROT) * 2.0 / ROT)
    angles = np.arange(length)[:, None] * frequency[None, :]
    cosine = np.ones((length, HD), np.float32)
    sine = np.zeros((length, HD), np.float32)
    cosine[:, :ROT] = np.tile(np.cos(angles), (1, 2))
    sine[:, :HALF_ROT] = np.sin(angles)
    sine[:, HALF_ROT:ROT] = -np.sin(angles)
    return jnp.asarray(cosine), jnp.asarray(sine)


def project_kernel(
    slots, w, one, q0, q1, q2, bias, cosine, sine, c0, c1, c2, c3, d0, d1, d2, *outs
):
    step = pl.program_id(0)
    quarter = c0.shape[1]
    u = (
        mm(one[:, : 2 * quarter], q0[...])
        + mm(one[:, 2 * quarter : 3 * quarter], q1[...])
        + mm(one[:, 3 * quarter :], q2[...])
        + bias[...]
    )
    g = (
        mm(c0[...], d0[:, :quarter], NT)
        + mm(c1[...], d0[:, quarter:], NT)
        + mm(c2[...], d1[...], NT)
        + mm(c3[...], d2[...], NT)
    )
    cos, sin = cosine[...], sine[...]
    rows = u.shape[0]
    at_rows = pl.ds(pl.multiple_of(pl.program_id(1) * rows, rows), rows)
    flip = lax.rem(w.head(2 * step), jnp.int32(2))
    blocks = []
    for head in range(2):
        at = head * 3 * HD
        query, key = u[:, at : at + HD], u[:, at + HD : at + 2 * HD]
        blocks.append(
            jnp.concatenate(
                [
                    (query * cos - turned(query) * sin).astype(BF16),
                    (key * cos - turned(key) * sin).astype(BF16),
                    u[:, at + 2 * HD : at + 3 * HD].astype(BF16),
                    g[:, head * HD : (head + 1) * HD].astype(BF16),
                ],
                1,
            )
        )
    for pair in range(slots // 2):
        for turn in range(2):

            @pl.when((step == pair) & (flip == turn))
            def _():
                outs[2 * pair + turn][at_rows, :] = blocks[0]
                outs[2 * pair + 1 - turn][at_rows, :] = blocks[1]


def projections(line, w, first, count, rows, one, qkv, bias, tables, cot, dense):
    features = one.shape[1]
    quarter = features // 4
    heads = dense[0][1] // HD
    wide = 6 * HD
    pair = lambda i, m, w: (0, lax.div(w.head(2 * i), jnp.int32(2)))
    own = lambda i, m, w: (w[SEQ], 0)
    inputs = [(one, (rows, features), lambda i, m, w: (m + first, 0))]
    inputs += [(array, (height, wide), pair) for array, height, _, _ in qkv]
    inputs += [(bias, (1, wide), pair)]
    inputs += [(table, (rows, HD), own) for table in tables]
    for b in range(4):
        inputs.append((cot, (rows, quarter), lambda i, m, w, b=b: (m + first, w[b])))
    for array, _, width, place in dense:
        inputs.append(
            (array, (2 * HD, width), lambda i, m, w, b=place: (lax.div(w.head(2 * i), jnp.int32(2)), b))
        )
    return call(
        line,
        functools.partial(project_kernel, heads),
        w,
        (heads // 2, count),
        inputs,
        [((count * rows, 4 * HD), BF16, (count * rows, 4 * HD), fixed(0, 0))] * heads,
        flops=2 * count * rows * features * heads * 4 * HD,
        nbytes=2 * features * (heads * 4 * HD + 2 * count * rows) + 8 * count * rows * heads * HD,
        name="projections",
    )


def attention_kernel(parts, scale, qsize, ksize, w, *refs):
    ins = refs[:parts]
    cos_ref, sin_ref = refs[parts : parts + 2]
    outs = refs[parts + 2 : 2 * parts + 2]
    q_s, k_s, v_s, g_s, kt_s, vt_s, prob_s, dk_s, dv_s, o_s, dq_s = refs[2 * parts + 2 :]
    rows = ins[0].shape[0]
    length = parts * rows
    places = []
    for k in range(parts):
        at = pl.ds(pl.multiple_of(xor(w[SEQ], k) * rows, rows), rows)
        places.append(at)
        q_s[at, :] = ins[k][:, 0:HD]
        k_s[at, :] = ins[k][:, HD : 2 * HD]
        v_s[at, :] = ins[k][:, 2 * HD : 3 * HD]
        g_s[at, :] = ins[k][:, 3 * HD : 4 * HD]
    for j in range(length // ksize):
        at = slice(j * ksize, (j + 1) * ksize)
        kt_s[:, at] = k_s[at, :].T
        vt_s[:, at] = v_s[at, :].T
    factor = scale * math.log2(math.e)
    for i in range(length // qsize):
        qat = slice(i * qsize, (i + 1) * qsize)
        q = q_s[qat, :]
        g = g_s[qat, :]
        chunks = []
        for first in range(0, (i + 1) * qsize, ksize):
            chunks.append((first, min(ksize, (i + 1) * qsize - first)))
        top = jnp.full((8, qsize), -1e30, F32)
        for first, size in chunks:
            s = mm(k_s[first : first + size, :], q, NT)
            if first + size > i * qsize:
                key = lax.broadcasted_iota(jnp.int32, s.shape, 0) + (first - i * qsize)
                query = lax.broadcasted_iota(jnp.int32, s.shape, 1)
                s = jnp.where(key <= query, s, -1e30)
            prob_s[first : first + size, :] = s
            top = jnp.maximum(top, jnp.max(s.reshape(size // 8, 8, qsize), 0))
        top = jnp.max(top, 0, keepdims=True)
        total = jnp.zeros((8, qsize), F32)
        acc = jnp.zeros((HD, qsize), F32)
        for first, size in chunks:
            e = jnp.exp2((prob_s[first : first + size, :] - top) * factor)
            prob_s[first : first + size, :] = e
            total = total + jnp.sum(e.reshape(size // 8, 8, qsize), 0)
            acc = acc + mm(vt_s[:, first : first + size], e.astype(BF16))
        inverse = 1.0 / jnp.sum(total, 0, keepdims=True)
        acc = acc * inverse
        delta = jnp.sum(acc * g.T.astype(F32), 0, keepdims=True)
        o_s[qat, :] = acc.T.astype(BF16)
        dqt = jnp.zeros((HD, qsize), F32)
        for first, size in chunks:
            at = slice(first, first + size)
            p = prob_s[at, :] * inverse
            ds = (p * (mm(v_s[at, :], g, NT) - delta)).astype(BF16)
            dv = mm(p.astype(BF16), g)
            dk = mm(ds, q)
            low = max(0, min(size, i * qsize - first))
            if low:
                old = slice(first, first + low)
                dv_s[old, :] += dv[:low]
                dk_s[old, :] += dk[:low]
            if low < size:
                new = slice(first + low, first + size)
                dv_s[new, :] = dv[low:]
                dk_s[new, :] = dk[low:]
            dqt = dqt + mm(kt_s[:, at], ds)
        dq_s[qat, :] = dqt.T
    for k in range(parts):
        at = places[k]
        cosine = cos_ref[at, :]
        sine = sin_ref[at, :]
        dq, dk = dq_s[at, :], dk_s[at, :]
        outs[k][:, 0:HD] = o_s[at, :]
        outs[k][:, HD : 2 * HD] = ((dq * cosine + turned(dq) * sine) * scale).astype(BF16)
        outs[k][:, 2 * HD : 3 * HD] = ((dk * cosine + turned(dk) * sine) * scale).astype(BF16)
        outs[k][:, 3 * HD : 4 * HD] = dv_s[at, :].astype(BF16)


def attention(line, w, rows, blocks, tables, qsize=512, ksize=512):
    parts = len(blocks)
    width = blocks[0][0].shape[1]
    count = 1
    length = parts * rows
    qsize, ksize = min(qsize, rows), min(ksize, rows)
    block = ((rows, width), lambda m, w: (m, 0))
    return call(
        line,
        functools.partial(attention_kernel, parts, HD ** (-0.5), qsize, ksize),
        w,
        (count,),
        [(array, (rows, width), fixed(place, 0)) for array, place in blocks] + [(table, (length, HD), fixed(0, 0)) for table in tables],
        [((count * rows, width), BF16, *block)] * parts,
        scratch=[pltpu.VMEM((length, HD), BF16)] * 4
        + [pltpu.VMEM((HD, length), BF16)] * 2
        + [pltpu.VMEM((length, qsize), F32)]
        + [pltpu.VMEM((length, HD), F32)] * 2
        + [pltpu.VMEM((length, HD), BF16)]
        + [pltpu.VMEM((length, HD), F32)],
        flops=14 * count * length * length * HD,
        nbytes=4 * count * length * width + 8 * length * HD,
        name="attention",
    )


def up_kernel(w, two, u0, u1, u2, bias, activated, slope):
    quarter = u1.shape[0]
    pre = (
        mm(two[:, : 2 * quarter], u0[...])
        + mm(two[:, 2 * quarter : 3 * quarter], u1[...])
        + mm(two[:, 3 * quarter :], u2[...])
        + bias[...]
    )
    tail = 0.5 + 0.5 * lax.erf(pre * math.sqrt(0.5))
    activated[...] = (pre * tail).astype(BF16)
    bell = jnp.exp2(pre * pre * (-0.5 * math.log2(math.e))) * (1.0 / math.sqrt(2.0 * math.pi))
    slope[...] = (tail + pre * bell).astype(BF16)


def feed_up(line, w, rows, two, up, bias):
    tokens, features = two.shape
    hidden = up[0][2]
    wide = min(1024, hidden)
    column = lambda j, m, w: (0, j)
    out = ((tokens, hidden), BF16, (rows, wide), lambda j, m, w: (m, j))
    return call(
        line,
        up_kernel,
        w,
        (hidden // wide, tokens // rows),
        [(two, (rows, features), lambda j, m, w: (m, 0))]
        + [(array, (height, wide), column) for array, height, _, _ in up]
        + [(bias, (1, wide), column)],
        [out, out],
        flops=2 * tokens * features * hidden,
        nbytes=2 * features * (hidden + 2 * tokens) + 4 * tokens * hidden,
        name="feed_up",
    )


def pre_grad_kernel(w, c0, c1, c2, c3, n0, n1, n2, slope, out, total):
    quarter = c0.shape[1]
    act_grad = (
        mm(c0[...], n0[:, :quarter], NT)
        + mm(c1[...], n0[:, quarter:], NT)
        + mm(c2[...], n1[...], NT)
        + mm(c3[...], n2[...], NT)
    )
    grad = (act_grad * slope[...].astype(F32)).astype(BF16)
    out[...] = grad

    @pl.when(pl.program_id(1) == 0)
    def _():
        total[...] = jnp.zeros_like(total)

    total[...] += groups(grad.astype(F32))


def pre_grads(line, w, rows, cot, down, slope):
    tokens, features = cot.shape
    hidden = slope.shape[1]
    wide = min(1024, hidden)
    quarter = features // 4
    inputs = []
    for b in range(4):
        inputs.append((cot, (rows, quarter), lambda j, m, w, b=b: (m, w[b])))
    inputs += [(array, (wide, width), lambda j, m, w: (j, 0)) for array, _, width, _ in down]
    tile = ((rows, wide), lambda j, m, w: (m, j))
    return call(
        line,
        pre_grad_kernel,
        w,
        (hidden // wide, tokens // rows),
        inputs + [(slope, *tile)],
        [
            ((tokens, hidden), BF16, *tile),
            ((8, hidden), F32, (8, wide), lambda j, m, w: (0, j)),
        ],
        flops=2 * tokens * features * hidden,
        nbytes=2 * features * (hidden + 2 * tokens) + 4 * tokens * hidden,
        name="pre_grads",
    )


def back_kernel(more, w, grad, w0, w1, w2, x, gain, *refs):
    if more:
        before, out, sums, e = refs
    else:
        out, sums, e = refs
    features = x.shape[1]
    quarter = features // 4
    rows = x.shape[0]

    @pl.when(pl.program_id(0) == 0)
    def _():
        sums[...] = jnp.zeros_like(sums)

    e[:, : 2 * quarter] = mm(grad[...], w0[...], NT)
    e[:, 2 * quarter : 3 * quarter] = mm(grad[...], w1[...], NT)
    e[:, 3 * quarter :] = mm(grad[...], w2[...], NT)
    values = x[...].astype(F32)
    mean = jnp.mean(values, -1, keepdims=True)
    center = values - mean
    inverse = lax.rsqrt(jnp.mean(center * center, -1, keepdims=True) + EPS)
    middle = jnp.zeros((rows, 1), F32)
    slant = jnp.zeros((rows, 1), F32)
    for b in range(4):
        at = slice(b * quarter, (b + 1) * quarter)
        unit = (x[:, columns_at(w, b, quarter)].astype(F32) - mean) * inverse
        found = e[:, at]
        sums[0:8, at] += groups(found * unit)
        sums[8:16, at] += groups(found)
        scaled = found * gain[:, at]
        middle += jnp.sum(scaled, -1, keepdims=True)
        slant += jnp.sum(scaled * unit, -1, keepdims=True)
    middle = middle * (1.0 / features)
    slant = slant * (1.0 / features)
    for b in range(4):
        at = slice(b * quarter, (b + 1) * quarter)
        place = columns_at(w, b, quarter)
        unit = (x[:, place].astype(F32) - mean) * inverse
        part = inverse * (e[:, at] * gain[:, at] - middle - unit * slant)
        if more:
            part = part + before[:, place].astype(F32)
        out[:, place] = part.astype(BF16)


def backs(line, w, rows, first, count, grad, weight, x, gain, before=None):
    features = x.shape[1]
    width = grad.shape[1]
    row = (rows, features)
    shift = lambda m, w: (m + first, 0)
    along = lambda m, w: (m, 0)
    inputs = [(grad, (rows, width), along)]
    inputs += [(array, (height, wide), fixed(0, place)) for array, height, wide, place in weight]
    inputs += [(x, row, shift), (gain, gain.shape, fixed(0, 0))]
    if before is not None:
        inputs.append((before, row, shift))
    return call(
        line,
        functools.partial(back_kernel, before is not None),
        w,
        (count,),
        inputs,
        [
            ((count * rows, features), BF16, row, along),
            ((16, features), F32, (16, features), fixed(0, 0)),
        ],
        scratch=[pltpu.VMEM(row, F32)],
        flops=2 * count * rows * features * width,
        nbytes=2 * (features * width + count * rows * (width + 3 * features)),
        name="backs",
    )


def output_kernel(heads, w, act, n0, n1, n2, d0, d1, d2, *refs):
    blocks = refs[:heads]
    part, attended, qkv_grad, total = refs[heads:]
    quarter = n1.shape[1]

    @pl.when(pl.program_id(0) == 0)
    def _():
        total[...] = jnp.zeros_like(total)

    for i in range(heads):
        head = w[ORDER + i]
        attended[:, pl.ds(pl.multiple_of(head * HD, HD), HD)] = blocks[i][:, :HD]
        at = pl.ds(pl.multiple_of(head * 3 * HD, HD), 3 * HD)
        qkv_grad[:, at] = blocks[i][:, HD:]
        total[:, at] += groups(blocks[i][:, HD:].astype(F32))
    pieces = [(n0, d0, 0), (n0, d0, 1), (n1, d1, 0), (n2, d2, 0)]
    for b, (down, dense, half) in enumerate(pieces):
        at = slice(half * quarter, (half + 1) * quarter)
        part[:, columns_at(w, b, quarter)] = (
            mm(attended[...], dense[:, at]) + mm(act[...], down[:, at])
        ).astype(BF16)


def outputs(line, w, first, rows, act, down, dense, blocks):
    hidden = act.shape[1]
    inner = dense[0][1]
    features = 2 * dense[0][2]
    heads = len(blocks)
    count = 1
    along = lambda m, w: (m, 0)
    inputs = [(act, (rows, hidden), lambda m, w: (m + first, 0))]
    for array, height, width, place in (*down, *dense):
        inputs.append((array, (height, width), fixed(0, place)))
    inputs += [(block, block.shape, fixed(0, 0)) for block in blocks]
    wide = lambda size: ((count * rows, size), BF16, (rows, size), along)
    return call(
        line,
        functools.partial(output_kernel, heads),
        w,
        (count,),
        inputs,
        [
            wide(features),
            wide(inner),
            wide(3 * inner),
            ((8, 3 * inner), F32, (8, 3 * inner), fixed(0, 0)),
        ],
        flops=2 * count * rows * features * (hidden + inner),
        nbytes=2 * features * (hidden + inner)
        + 2 * count * rows * (hidden + features + 8 * inner),
        name="outputs",
    )


def grad_kernel(pieces, count, at_left, adds, w, *refs):
    sides, swept = refs[: (1 if at_left else count)], refs[1 if at_left else count :]
    rest = swept[pieces:]
    swept = swept[:pieces]
    out = rest[-1]
    for i, side in enumerate(sides):
        value = 0.0
        start = 0
        for ref in swept:
            part = side[start : start + ref.shape[0], :]
            start += ref.shape[0]
            value = value + (mm(part, ref[...], TN) if at_left else mm(ref[...], part, TN))
        if adds:
            value = value + rest[0][i].astype(F32)
        out[i] = value.astype(BF16)


def weight_grad(line, w, at, at_left, side, swept, adds=None):
    tokens = side.shape[0]
    quarter = side.shape[1] // 4
    size = swept[0].shape[1]
    tile = min(256, quarter, size)
    heights = [piece.shape[0] for piece in swept]
    if at_left:
        split = quarter // tile
        grid = (2, split)
        inputs = [(side, (tokens, tile), lambda i, j, w: (0, w.either(at, i) * split + j))]
        inputs += [(piece, piece.shape, fixed(0, 0)) for piece in swept]
        out = ((2, quarter, size), BF16, (1, tile, size), lambda i, j, w: (i, j, 0))
    else:
        grid = (size // tile,)
        inputs = []
        for i in range(2):
            inputs.append((side, (tokens, quarter), lambda j, w, i=i: (0, w[at + i])))
        inputs += [(piece, (piece.shape[0], tile), lambda j, w: (0, j)) for piece in swept]
        out = ((2, size, quarter), BF16, (2, tile, quarter), lambda j, w: (0, j, 0))
    if adds is not None:
        inputs.append((adds, out[2], out[3]))
    return call(
        line,
        functools.partial(grad_kernel, len(swept), 2, at_left, adds is not None),
        w,
        grid,
        inputs,
        [out],
        flops=4 * tokens * quarter * size,
        nbytes=2 * tokens * (2 * quarter + size) + 8 * quarter * size,
        name="weight_grad",
    )[0]


def join(pieces):
    return [(piece, piece.shape, fixed(0, 0)) for piece in pieces]


def add_kernel(w, mine, *refs):
    *pieces, out = refs
    first = 0
    for piece in pieces:
        at = slice(first, first + piece.shape[0])
        out[at, :] = (mine[at, :].astype(F32) + piece[...].astype(F32)).astype(BF16)
        first += piece.shape[0]


def add(line, w, mine, pieces):
    shape = mine.shape[-2:]
    first = (mine, (None,) + shape, fixed(0, 0, 0)) if mine.ndim == 3 else (mine, shape, fixed(0, 0))
    return call(
        line,
        add_kernel,
        w,
        (1,),
        [first] + join(pieces),
        [(shape, BF16, shape, fixed(0, 0))],
        nbytes=6 * shape[0] * shape[1],
        name="add",
    )[0]


def first_half_kernel(w, mine, *refs):
    *pieces, wide, total = refs
    first = 0
    for piece in pieces:
        at = slice(first, first + piece.shape[0])
        value = (mine[at, :].astype(F32) + piece[...].astype(F32)).astype(BF16)
        total[at, :] = value
        wide[at, :] = value.astype(F32)
        first += piece.shape[0]


def first_half(line, w, at_left, mine, pieces):
    height, width = mine.shape
    if at_left:
        whole, place = (2 * height, width), lambda i, w: (w[KEEP], 0)
    else:
        whole, place = (height, 2 * width), lambda i, w: (0, w[KEEP])
    return call(
        line,
        first_half_kernel,
        w,
        (1,),
        [(mine, mine.shape, fixed(0, 0))] + join(pieces),
        [(whole, F32, mine.shape, place), (mine.shape, BF16, mine.shape, fixed(0, 0))],
        nbytes=10 * height * width,
        name="first_half",
    )


def second_half_kernel(w, held, other, wide):
    wide[...] = other[...].astype(F32)


def second_half(line, w, at_left, held, other):
    height, width = other.shape
    size = height // 2
    if at_left:
        whole, place = (2 * height, width), lambda i, w: (2 * w[SEND] + i, 0)
    else:
        whole, place = (height, 2 * width), lambda i, w: (i, w[SEND])
    return call(
        line,
        second_half_kernel,
        w,
        (2,),
        [(held, None, None), (other, (size, width), lambda i, w: (i, 0))],
        [(whole, F32, (size, width), place)],
        nbytes=6 * height * width,
        name="second_half",
        alias=0,
    )[0]


def gate_kernel(w, source, target):
    pass


def gate(line, w, array):
    return call(
        line,
        gate_kernel,
        w,
        (1,),
        [(array, None, None)],
        [(array.shape, array.dtype, None, None)],
        name="gate",
        alias=0,
    )[0]


def finish_kernel(more, w, kept, cols, *refs):
    refs = refs[1:] if more == "held" else refs
    *bias, out = refs
    value = kept[...].astype(F32) + cols[...].astype(F32)
    for ref in bias:
        value = value + ref[...]
    out[...] = value.astype(out.dtype)


def finish(line, w, m, held, kept, cols, bias, shape, dtype):
    count, rows, columns = shape
    block = (rows, columns)
    inputs = [
        (kept, (None,) + block, lambda i, w: (m, 0, w[TENSOR])),
        (cols, block, fixed(0, 0)),
    ]
    if held is not None:
        inputs.append((held, None, None))
    if bias is not None:
        inputs.append((bias, (1, columns), lambda i, w: (0, w[TENSOR])))
    return call(
        line,
        functools.partial(finish_kernel, None if held is None else "held"),
        w,
        (1,),
        inputs,
        [(shape, dtype, (None,) + block, fixed(m, 0, 0))],
        nbytes=8 * rows * columns,
        name="finish",
        alias=None if held is None else 2,
    )[0]


def pick_kernel(joint, w, by_rows, by_columns, *targets):
    if joint:
        width = by_columns.shape[1]
        targets[0][:, : by_rows.shape[1]] = by_rows[...]
        targets[0][: by_columns.shape[0], targets[0].shape[1] - width :] = by_columns[...]
    else:
        targets[0][...] = by_rows[...]
        targets[1][...] = by_columns[...]


def pick(line, w, by_rows, by_columns, joint):
    height, width = by_rows.shape[0] // 2, by_columns.shape[1] // 2
    first = (height, by_rows.shape[1])
    second = (by_columns.shape[0], width)
    if joint:
        shapes = [(max(first[0], second[0]), pl.cdiv(first[1], width) * width + width)]
    else:
        shapes = [first, second]
    return call(
        line,
        functools.partial(pick_kernel, joint),
        w,
        (1,),
        [
            (by_rows, first, lambda i, w: (w[KEEP], 0)),
            (by_columns, second, lambda i, w: (0, w[KEEP])),
        ],
        [(shape, BF16, shape, fixed(0, 0)) for shape in shapes],
        nbytes=4 * (first[0] * first[1] + second[0] * second[1]),
        name="pick",
    )


def on_device(
    states,
    ln1_gain,
    ln1_bias,
    ln2_gain,
    ln2_bias,
    qkv_weight,
    qkv_bias,
    dense_weight,
    dense_bias,
    up_weight,
    up_bias,
    down_weight,
    out_bias,
    out_grad,
):
    micros, rows, features = states.shape
    heads = qkv_weight.shape[1] // (3 * HD)
    tokens = micros * rows
    n = lax.axis_size("seq")
    pairs = heads * micros // n
    straight = heads == n
    s = lax.axis_index("seq")
    core = s % 2
    d = lax.axis_index("dp")
    columns = features // lax.axis_size("tensor")
    first = lax.axis_index("tensor") * columns
    w = Places(straight)

    def absolute(own, other):
        return jnp.where(d == 1, jnp.concatenate([other, own]), jnp.concatenate([own, other]))

    x = states.reshape(tokens, features)
    cot = out_grad.reshape(tokens, features)

    small = (ln1_gain, ln1_bias, ln2_gain, ln2_bias, dense_bias, out_bias, qkv_bias, up_bias)
    small_got = swap(jnp.concatenate(small, 0), "dp", 1)
    line = Line(small_got)
    joint_half = swap(pick(line, w, qkv_weight, dense_weight, True)[0], "dp", 1)
    own, other = [], []
    place = 0
    for vector in small:
        own.append(vector.astype(F32))
        other.append(small_got[place : place + vector.shape[0]].astype(F32))
        place += vector.shape[0]
    half = features // 4
    vectors = jnp.stack(
        [
            jnp.concatenate(
                [
                    own[i],
                    lax.dynamic_slice_in_dim(other[i], core * half, half),
                    lax.dynamic_slice_in_dim(other[i], (1 - core) * half, half),
                ]
            )
            for i in range(4)
        ]
    )
    tables = turn_tables(n * rows)

    one, two, cot_total = norms(line, w, x, cot, vectors)
    halves = pick(line, w, up_weight, down_weight, False)
    up_got = swap(halves[0], "dp", 1)
    down_got = swap(halves[1], "dp", 1)
    got = gate(line, w, joint_half)
    joint = (got, swap(got, "seq", 1))
    height, width = qkv_weight.shape[0], qkv_weight.shape[1]
    qkv = [(qkv_weight, height, width, 0)] + [(half, height // 2, width, 0) for half in joint]
    height, width = dense_weight.shape[0], dense_weight.shape[1]
    dense = [(dense_weight, height, width, 0)] + [
        (half, height, width // 2, half.shape[1] // (width // 2) - 1) for half in joint
    ]
    qkv_shift = absolute(own[6], other[6])[None]
    up_shift = absolute(own[7], other[7])[None]
    bias = absolute(own[4] + own[5], other[4] + other[5])[None]
    payload, arrived, results, attended, qkv_grad = {}, {}, {}, {}, {}
    branch, back_cols, held = {}, {}, {"output": None, "input_grad": None}
    out_shape = (micros, rows, columns)
    totals = {"qkv": 0.0, "one": 0.0}
    sizes = GROUPS if micros == sum(GROUPS) else (1,) * micros
    starts = [sum(sizes[:i]) for i in range(len(sizes))]

    def project(group):
        found = projections(
            line, w, starts[group], sizes[group], rows, one, qkv, qkv_shift, tables, cot, dense
        )
        for i in range(sizes[group]):
            payload[starts[group] + i] = [(array, i) for array in found]

    def bring(m, *distances):
        for k in distances if straight else ():
            array, place = payload[m][k]
            arrived[m, k] = line.ride(array, "seq", k, place * rows, rows)

    def attend(m):
        if straight:
            blocks = [payload[m][0]] + [(arrived[m, k].result, 0) for k in range(1, n)]
            results[m] = list(attention(line, w, rows, blocks, tables))

    def give(m, *distances):
        for k in distances if straight else ():
            results[m][k] = line.ride(results[m][k], "seq", k)

    def attend_pairs():
        blocks = []
        for h in range(heads):
            for m in range(micros):
                array, place = payload[m][h]
                blocks.append(array[place * rows : (place + 1) * rows])
        stacked = jnp.stack(blocks).reshape(n, pairs, rows, 4 * HD)
        found = []
        for pair in range(pairs):
            sent = [
                lax.dynamic_index_in_dim(stacked[:, pair], s ^ k, 0, False) for k in range(n)
            ]
            sent = [sent[0]] + [swap(sent[k], "seq", k) for k in range(1, n)]
            back = attention(line, w, rows, [(array, 0) for array in sent], tables)
            found.append(jnp.stack([back[0]] + [swap(back[k], "seq", k) for k in range(1, n)]))
        for m in range(micros):
            results[m] = []
            for h in range(heads):
                device, pair = divmod(h * micros + m, pairs)
                results[m].append(
                    lax.dynamic_index_in_dim(found[pair], s ^ device, 0, False)
                )

    def both_cores(shard, got, by_rows):
        got = gate(line, w, got)
        return [(shard, *shard.shape, 0)] + [
            (half, *half.shape, 0) for half in (got, swap(got, "seq", 1))
        ]

    def put_out(m):
        if not straight and not results:
            attend_pairs()
        blocks = [block.result if isinstance(block, Ride) else block for block in results[m]]
        partial, attended[m], qkv_grad[m], total = outputs(
            line, w, m, rows, activated, down, dense, blocks
        )
        totals["qkv"] = totals["qkv"] + total
        branch[m] = lax.psum_scatter(partial, "tensor", scatter_dimension=1, tiled=True)

    def go_back(m):
        part, sums = backs(line, w, rows, m, 1, qkv_grad[m], qkv, x, vectors[0:1], part_two)
        totals["one"] = totals["one"] + sums
        back_cols[m] = lax.psum_scatter(part, "tensor", scatter_dimension=1, tiled=True)

    def finish_out(m):
        held["output"] = finish(
            line, w, m, held["output"], states, branch[m], bias, out_shape, BF16
        )

    def finish_back(m):
        held["input_grad"] = finish(
            line, w, m, held["input_grad"], out_grad, back_cols[m], None, out_shape, F32
        )

    grads, terms = {}, {
        "down": (False, cot, None),
        "up": (True, two, None),
        "dense": (False, cot, None),
        "qkv": (True, one, None),
    }
    steps = {}

    found, rides = {}, {}

    def send(name, swept):
        at_left, side, _ = terms[name]
        terms[name] = (at_left, side, swept)
        at = SEND if at_left else SEND_AT
        sent = weight_grad(line, w, at, at_left, side, swept)
        found[name] = sent.reshape(-1, sent.shape[2])

    def to_sibling(name):
        rides[name] = line.ride(found[name], "seq", 1)

    def keep(name):
        at_left, side, swept = terms[name]
        at = KEEP if at_left else KEEP_AT
        added = rides[name].result
        added = added.reshape(2, added.shape[0] // 2, added.shape[1])
        found[name] = weight_grad(line, w, at, at_left, side, swept, added)
        rides[name] = []

    def parts(name, count):
        height = found[name].shape[-2]
        size = height // PIECES[name]
        first = sum(ride.rows for ride in rides[name])
        return [(first + i * size, size) for i in range(count)]

    def over_y(name, count):
        for first, size in parts(name, count):
            rides[name].append(line.ride(found[name], "dp", 1, first, size, lead=1))

    def over_x(name, count):
        for first, size in parts(name, count):
            rides[name].append(line.ride(found[name], "seq", steps[name], first, size))

    def all_over_y(name):
        rides[name] = [swap(found[name][1], "dp", 1)]

    def all_over_x(name):
        rides[name] = [swap(found[name], "seq", steps[name])]

    def landed(name):
        return [ride.result if isinstance(ride, Ride) else ride for ride in rides[name]]

    def add_up(name):
        found[name] = add(line, w, found[name], landed(name))
        rides[name] = []
        steps[name] = 2
        while 2 * steps[name] < n:
            found[name] = add(
                line, w, found[name], [swap(found[name], "seq", steps[name])]
            )
            steps[name] *= 2
            rides[name] = []

    def mine_done(name):
        held[name], found[name] = first_half(
            line, w, terms[name][0], found[name], landed(name)
        )

    def sibling_swap(name):
        rides[name] = swap(found[name], "seq", 1)

    def all_done(name):
        ride = rides[name]
        other = ride.result if isinstance(ride, Ride) else ride
        grads[name] = second_half(line, w, terms[name][0], held[name], other)

    def all_terms():
        one_sums, qkv_total = totals["one"], totals["qkv"]
        sums = jnp.concatenate([one_sums, two_sums], 0).reshape(4, 8, features).sum(1)
        norm_own, norm_oth = sums[:, : 2 * half], sums[:, 2 * half :]
        norm_oth = jnp.where(
            core == 1,
            jnp.concatenate([norm_oth[:, half:], norm_oth[:, :half]], 1),
            norm_oth,
        )
        norm_terms = jnp.where(
            d == 1,
            jnp.concatenate([norm_oth, norm_own], 1),
            jnp.concatenate([norm_own, norm_oth], 1),
        ).reshape(-1)
        rest = jnp.concatenate([qkv_total.sum(0), up_total.sum(0), cot_total.sum(0)])
        return norm_terms, rest

    def hop(vector, axis, step):
        vector = gate(line, w, vector)
        return vector + swap(vector, axis, step)

    project(0)
    bring(0, 1, 2, 3)
    project(1)
    bring(1, 1, 2)
    attend(0)
    up = both_cores(up_weight, up_got, True)
    bring(1, 3)
    give(0, 1, 2, 3)
    activated, slope = feed_up(line, w, rows, two, up, up_shift)
    down = both_cores(down_weight, down_got, False)
    put_out(0)
    bring(2, 1, 2)
    attend(1)
    send("down", [activated])
    give(1, 1, 2, 3)
    pre_grad, up_total = pre_grads(line, w, rows, cot, down, slope)
    to_sibling("down")
    put_out(1)
    bring(2, 3)
    keep("down")
    bring(3, 1, 2, 3)
    over_y("down", 3)
    part_two, two_sums = backs(line, w, rows, 0, micros, pre_grad, up, x, vectors[2:3])
    go_back(0)
    over_y("down", 1)
    attend(2)
    give(2, 1, 2)
    attend(3)
    give(2, 3)
    give(3, 1)
    send("up", [pre_grad])
    to_sibling("up")
    put_out(2)
    add_up("down")
    give(3, 2)
    keep("up")
    give(3, 3)
    over_y("up", 1)
    go_back(1)
    finish_out(0)
    over_x("down", 1)
    over_y("up", 1)
    put_out(3)
    over_x("down", 1)
    over_y("up", 1)
    go_back(2)
    heads_out = [attended[m] for m in range(micros)]
    heads_grad = [qkv_grad[m] for m in range(micros)]
    over_x("down", 1)
    over_y("up", 1)
    send("qkv", heads_grad)
    finish_out(1)
    add_up("up")
    over_x("down", 1)
    to_sibling("qkv")
    go_back(3)
    over_x("up", 1)
    keep("qkv")
    mine_done("down")
    finish_back(0)
    all_over_y("qkv")
    to_sibling("down")
    over_x("up", 1)
    send("dense", heads_out)
    to_sibling("dense")
    over_x("up", 2)
    norm_terms, rest = all_terms()
    step = 1
    while step < lax.axis_size("tensor"):
        norm_terms, step = hop(norm_terms, "tensor", step), 2 * step
    keep("dense")
    all_over_y("dense")
    mine_done("up")
    add_up("qkv")
    all_over_x("qkv")
    sibling_swap("up")
    finish_out(2)
    vector = hop(jnp.concatenate([norm_terms, rest]), "dp", 1)
    add_up("dense")
    all_over_x("dense")
    all_done("down")
    all_done("up")
    finish_back(1)
    finish_out(3)
    step = 1
    while step < n:
        vector, step = hop(vector, "seq", step), 2 * step
    mine_done("qkv")
    sibling_swap("qkv")
    mine_done("dense")
    sibling_swap("dense")
    finish_back(2)
    all_done("qkv")
    all_done("dense")
    finish_back(3)
    norm_terms = vector[: 4 * features].reshape(4, features)
    rest = vector[4 * features :]
    count = columns // 2
    norm_mine = lax.dynamic_slice_in_dim(norm_terms, first + d * count, count, 1)
    vector_grads = []
    place = 0
    for size in (3 * HD * heads, up_total.shape[1], features):
        vector_grads.append(lax.dynamic_slice_in_dim(rest, place + d * (size // 2), size // 2, 0))
        place += size

    return (
        held["output"],
        held["input_grad"],
        norm_mine[0],
        norm_mine[1],
        norm_mine[2],
        norm_mine[3],
        grads["qkv"],
        vector_grads[0],
        grads["dense"],
        vector_grads[2],
        grads["up"],
        vector_grads[1],
        grads["down"],
        vector_grads[2],
    )


def solution(mesh):
    placed = (
        P("dp", "seq", None),
        P("dp"),
        P("dp"),
        P("dp"),
        P("dp"),
        P("dp", "tensor"),
        P(("tensor", "dp")),
        P("tensor", "dp"),
        P("dp"),
        P("dp", "tensor"),
        P(("tensor", "dp")),
        P("tensor", "dp"),
        P("dp"),
        P("dp", "seq", None),
    )
    return jax.shard_map(
        on_device,
        mesh=mesh,
        in_specs=placed,
        out_specs=(
            P("dp", "seq", "tensor"),
            P("dp", "seq", "tensor"),
            P(("tensor", "dp")),
            P(("tensor", "dp")),
            P(("tensor", "dp")),
            P(("tensor", "dp")),
            P("dp", "tensor"),
            P(("tensor", "dp")),
            P("tensor", "dp"),
            P("dp"),
            P("dp", "tensor"),
            P(("tensor", "dp")),
            P("tensor", "dp"),
            P("dp"),
        ),
        check_vma=False,
    )
```

time: 1180 us -> 746 us (0.63)
  Pallas kernels: 123 us -> 608 us
  matrix products: 315 us -> 0 us
  local copies, waits for them, and re-layouts: 243 us -> 20 us
  waiting for transfers between devices: 237 us -> 61.7 us
  other arithmetic: 126 us -> 11.9 us
  blocking collectives: 64.7 us -> 0 us
  starting transfers between devices: 39.3 us -> 20.9 us
    pallas_call x4 -> x56, Pallas kernels: 123 us -> 608 us  [call(): pl.pallas_call(body, grid=grid, in_specs=[anywhere] * skip + [spec(block,...]
    dot_general x32 -> x0, matrix products: 315 us -> none  [mm(): return lax.dot_general(a, b, dims, preferred_element_type=F32)]
    ppermute x53 -> x19, waiting for transfers between devices: 237 us -> 61.5 us  [swap(): lax.ppermute(block, axis, [(i, i ^ distance) for i in range(lax.axis_size...]
    dynamic_slice x31 -> x4, local copies, waits for them, and re-layouts: 103 us -> 1.49 us  [the longest x2 1.34 us: on_device(): lax.dynamic_slice_in_dim(rest, place + d * (size // 2), size // 2, 0)]
    convert_element_type x23 -> x4, other arithmetic: 69.3 us -> 3.05 us  [on_device(): own.append(vector.astype(F32))]
    psum x2 -> x0, blocking collectives: 64.7 us -> none  [the longest x1 39.7 us: on_device(): norm_terms = lax.psum(norm_terms, ('seq', 'dp', 'tensor'))]
    unnamed x194 -> x69, local copies, waits for them, and re-layouts: 48.2 us -> 14.2 us
    reshape x3 -> x1, local copies, waits for them, and re-layouts: 24.2 us -> 0.02 us  [on_device(): norm_terms = vector[:4 * features].reshape(4, features)]
  transfers between devices with their start and end apart: 55 -> 27, of which waited for: 11 -> 13; matrix products, arithmetic and copies ran while one was open for 48% -> 2% of each run, Pallas kernels for 11% -> 80%
where the time goes in v2:
time: 746 us; the launch traced here: 737 us
  Pallas kernels  608 us (82%)
  waiting for transfers between devices  61.7 us (8%)
  starting transfers between devices  20.9 us (3%)
  local copies, waits for them, and re-layouts  20 us (3%)
  between operations  14.9 us (2%)
  other arithmetic  11.9 us (2%)
    pallas_call x56, Pallas kernels, call(): pl.pallas_call(body, grid=grid, in_specs=[anywhere] * skip + [spec(block,...  608 us
    ppermute x19, waiting for transfers between devices, swap(): lax.ppermute(block, axis, [(i, i ^ distance) for i in range(lax.axis_size...  61.5 us
    ppermute x19, starting transfers between devices, swap(): lax.ppermute(block, axis, [(i, i ^ distance) for i in range(lax.axis_size...  20 us
  transfers between devices with their start and end apart: 27, of which 13 were waited for; matrix products, arithmetic and copies ran while one was open for 2% of the time, Pallas kernels for 80%

profile of v2, /device:TPU:0, one launch (start us, length us, event | category | flops | bytes accessed | tf_op | source)
XLA Modules:
  0.0 737.3 jit_solution(6257009874265060067)
XLA Ops:
  13.4 3.0 collective-permute-start
  18.7 3.0 pick.2.refs_0_
  21.6 2.0 collective-permute-start.1
  25.2 18.1 %norms.1 = (bf16[2048,2048]{1,0:T(8,128)(2,1)}, bf16[2048,2048]{1,0:T(8,128)(2,1)}, f32[8,2048]{1,0:T(8,128)}) custom-call(bf16[512,2048]{1,0:T(8,128)(2,1)} %pick.2.refs_0_, bf16[2048,2048]{1,0:T(8,128)(2,1)} %bitcast.54, bf16[2048,2048]{1,0:T(8,128)(2,1)} %bitcast.33, f32[4,2048]{1,0:T(4,128)} %pad_maximum_fusion.1.refs_3_), custom_call_target="tpu_custom_call" | custom-call | flops 12582912 | bytes 3355443 | tf_op jit(solution)/shard_map/norms/pallas_call | solution.py:178
  43.4 4.4 pick.3
  47.8 20.6 %collective-permute-done.1.refs_1_ = bf16[512,2048]{1,0:T(8,128)(2,1)S(1)} collective-permute-done((bf16[512,2048]{1,0:T(8,128)(2,1)}, bf16[512,2048]{1,0:T(8,128)(2,1)S(1)}, u32[]{:S(2)}, u32[]{:S(2)}) %collective-permute-start.1) | collective-permute-done | bytes 2097184 | tf_op jit(solution)/shard_map/ppermute | solution.py:107
  69.7 1.7 collective-permute-start.3
  75.4 10.7 %projections.2 = (bf16[512,512]{1,0:T(8,128)(2,1)}, bf16[512,512]{1,0:T(8,128)(2,1)}, bf16[512,512]{1,0:T(8,128)(2,1)}, bf16[512,512]{1,0:T(8,128)(2,1)}) custom-call(bf16[512,2048]{1,0:T(8,128)(2,1)} %gate.8.refs_0_.refs_3_.refs_13_.refs_6_.refs_16_.refs_7_.refs_5_.refs_8_, bf16[2048,2048]{1,0:T(8,128)(2,1)} %get-tuple-element.135.refs_1_.refs_4_.refs_3_.refs_2_, ...), custom_call_target="tpu_custom_call" | custom-call | flops 429496736 | bytes 1468006 | tf_op jit(solution)/shard_map/projections/pallas_call | solution.py:178
  86.1 32.2 %projections.3 = (bf16[1536,512]{1,0:T(8,128)(2,1)}, bf16[1536,512]{1,0:T(8,128)(2,1)}, bf16[1536,512]{1,0:T(8,128)(2,1)}, bf16[1536,512]{1,0:T(8,128)(2,1)}, bf...) custom-call(bf16[512,512]{1,0:T(8,128)(2,1)} %get-tuple-element.136.refs_0_.refs_3_, ...), custom_call_target="tpu_custom_call" | custom-call | flops 1288490240 | bytes 2726297 | tf_op jit(solution)/shard_map/projections/pallas_call | solution.py:178
  118.2 18.2 %attention.4 = (bf16[512,512]{1,0:T(8,128)(2,1)}, bf16[512,512]{1,0:T(8,128)(2,1)}, bf16[512,512]{1,0:T(8,128)(2,1)}, bf16[512,512]{1,0:T(8,128)(2,1)}, bf16[512...) custom-call(bf16[1536,512]{1,0:T(8,128)(2,1)} %get-tuple-element.139.refs_0_.refs_1_.refs_3_, ...), custom_call_target="tpu_custom_call" | custom-call | flops 751619264 | bytes 629145 | tf_op jit(solution)/shard_map/attention/pallas_call | solution.py:178
  136.6 1.8 collective-permute-start.5
  138.9 2.1 collective-permute-done.4.refs_8_.refs_10_
  141.0 41.0 %feed_up.1 = (bf16[2048,2048]{1,0:T(8,128)(2,1)}, bf16[2048,2048]{1,0:T(8,128)(2,1)}, bf16[512,512]{1,0:T(8,128)(2,1)}, bf16[512,512]{1,0:T(8,128)(2,1)}, bf16[5...) custom-call(bf16[512,2048]{1,0:T(8,128)(2,1)} %gate.9.refs_0_.refs_7_.refs_9_, ...), custom_call_target="tpu_custom_call" | custom-call | flops 1717986944 | bytes 4194304 | tf_op jit(solution)/shard_map/feed_up/pallas_call | solution.py:178
  182.0 2.8 collective-permute-done.5.refs_1_
  186.2 4.4 collective-permute-done.6.refs_4_.refs_10_.refs_5_.refs_6_
  191.9 12.8 %outputs.4 = (bf16[512,2048]{1,0:T(8,128)(2,1)}, bf16[512,512]{1,0:T(8,128)(2,1)}, bf16[512,1536]{1,0:T(8,128)(2,1)}, f32[8,1536]{1,0:T(8,128)}) custom-call(bf16[2048,512]{1,0:T(8,128)(2,1)} %gate.10.refs_0_.refs_3_.refs_9_.refs_4_.refs_5_, bf16[2048,2048]{1,0:T(8,128)(2,1)} %get-tuple-element.152.refs_1_.refs_3_.refs_2_.refs_4_, ...), custom_call_target="tpu_custom_call" | custom-call | flops 536870912 | bytes 1887436 | tf_op jit(solution)/shard_map/outputs/pallas_call | solution.py:178
  204.8 18.1 %attention.5 = (bf16[512,512]{1,0:T(8,128)(2,1)}, bf16[512,512]{1,0:T(8,128)(2,1)}, bf16[512,512]{1,0:T(8,128)(2,1)}, bf16[512,512]{1,0:T(8,128)(2,1)}, bf16[512...) custom-call(f32[8,1536]{1,0:T(8,128)} %get-tuple-element.157.refs_0_, bf16[1536,512]{1,0:T(8,128)(2,1)} %get-tuple-element.140.refs_1_, ...), custom_call_target="tpu_custom_call" | custom-call | flops 751619264 | bytes 629145 | tf_op jit(solution)/shard_map/attention/pallas_call | solution.py:178
  222.9 15.0 %weight_grad.8.refs_0_ = bf16[2,2048,512]{2,1,0:T(8,128)(2,1)} custom-call(bf16[512,512]{1,0:T(8,128)(2,1)} %get-tuple-element.162.refs_0_.refs_3_, bf16[2048,2048]{1,0:T(8,128)(2,1)} %bitcast.42, bf16[2048,2048]{1,0:T(8,128)(2,1)} %bitcast.43, bf16[2048,2048]{1,0:T(8,128)(2,1)} %get-tuple-element.152.refs_1_.refs_3_.refs_2_.refs_4_), custom_call_target="tpu_custom_call" | custom-call | flops 858993472 | bytes 2097152 | tf_op jit(solution)/shard_map/weight_grad/pallas_call | solution.py:178
  237.9 29.6 %pre_grads.1 = (bf16[2048,2048]{1,0:T(8,128)(2,1)}, f32[8,2048]{1,0:T(8,128)}, bf16[512,512]{1,0:T(8,128)(2,1)}, bf16[512,512]{1,0:T(8,128)(2,1)}, bf16[512,512]{1,0:T(8,128)(2,1)}) custom-call(bf16[2,2048,512]{2,1,0:T(8,128)(2,1)} %weight_grad.8.refs_0_, bf16[512,512]{1,0:T(8,128)(2,1)} %get-tuple-element.163.refs_1_, ...), custom_call_target="tpu_custom_call" | custom-call | flops 1717986944 | bytes 4194304 | tf_op jit(solution)/shard_map/pre_grads/pallas_call | solution.py:178
  267.6 15.0 %outputs.5 = (bf16[512,2048]{1,0:T(8,128)(2,1)}, bf16[512,512]{1,0:T(8,128)(2,1)}, bf16[512,1536]{1,0:T(8,128)(2,1)}, f32[8,1536]{1,0:T(8,128)}, bf16[4096,512]{1,0:T(8,128)(2,1)}) custom-call(f32[8,2048]{1,0:T(8,128)} %get-tuple-element.165.refs_0_, bf16[4096,512]{1,0:T(8,128)(2,1)} %bitcast.60, ...), custom_call_target="tpu_custom_call" | custom-call | flops 536870912 | bytes 1887436 | tf_op jit(solution)/shard_map/outputs/pallas_call | solution.py:178
  282.6 18.0 %weight_grad.9 = (bf16[2,2048,512]{2,1,0:T(8,128)(2,1)}, bf16[512,512]{1,0:T(8,128)(2,1)}) custom-call(f32[8,1536]{1,0:T(8,128)} %get-tuple-element.170.refs_0_, bf16[1536,512]{1,0:T(8,128)(2,1)} %get-tuple-element.139.refs_0_.refs_1_.refs_3_, bf16[2048,2048]{1,0:T(8,128)(2,1)} %bitcast.48, bf16[2048,2048]{1,0:T(8,128)(2,1)} %bitcast.49, ...), custom_call_target="tpu_custom_call" | custom-call | flops 858993472 | bytes 2097152 | tf_op jit(solution)/shard_map/weight_grad/pallas_call | solution.py:178
  300.6 44.3 %backs.5 = (bf16[2048,2048]{1,0:T(8,128)(2,1)}, f32[16,2048]{1,0:T(8,128)}, bf16[512,512]{1,0:T(8,128)(2,1)}, bf16[512,512]{1,0:T(8,128)(2,1)}, bf16[512,512]{1,...) custom-call(bf16[2,2048,512]{2,1,0:T(8,128)(2,1)} %get-tuple-element.172.refs_0_.refs_, ...), custom_call_target="tpu_custom_call" | custom-call | flops 1717986944 | bytes 4194304 | tf_op jit(solution)/shard_map/backs/pallas_call | solution.py:178
  344.9 12.2 %backs.6 = (bf16[512,2048]{1,0:T(8,128)(2,1)}, f32[16,2048]{1,0:T(8,128)}) custom-call(f32[16,2048]{1,0:T(8,128)} %get-tuple-element.174.refs_0_, bf16[512,1536]{1,0:T(8,128)(2,1)} %get-tuple-element.175.refs_1_.refs_4_.refs_3_, bf16[1024,1536]{1,0:T(8,128)(2,1)} %refs_4_.7, ...), custom_call_target="tpu_custom_call" | custom-call | flops 322122560 | bytes 1415577 | tf_op jit(solution)/shard_map/backs/pallas_call | solution.py:178
  357.5 17.3 %attention.6 = (bf16[512,512]{1,0:T(8,128)(2,1)}, bf16[512,512]{1,0:T(8,128)(2,1)}, bf16[512,512]{1,0:T(8,128)(2,1)}, bf16[512,512]{1,0:T(8,128)(2,1)}, bf16[512,512]{1,0:T(8,128)(2,1)}) custom-call(f32[16,2048]{1,0:T(8,128)} %get-tuple-element.177.refs_0_, bf16[2,2048,512]{2,1,0:T(8,128)(2,1)} %get-tuple-element.172.refs_0_.refs_4_.refs_5_.refs_6_.refs_1_, ...), custom_call_target="tpu_custom_call" | custom-call | flops 751619264 | bytes 629145 | tf_op jit(solution)/shard_map/attention/pallas_call | solution.py:178
  374.8 17.1 %attention.7 = (bf16[512,512]{1,0:T(8,128)(2,1)}, bf16[512,512]{1,0:T(8,128)(2,1)}, bf16[512,512]{1,0:T(8,128)(2,1)}, bf16[512,512]{1,0:T(8,128)(2,1)}, bf16[512...) custom-call(bf16[512,512]{1,0:T(8,128)(2,1)} %get-tuple-element.181.refs_0_.refs_1_, ...), custom_call_target="tpu_custom_call" | custom-call | flops 751619264 | bytes 629145 | tf_op jit(solution)/shard_map/attention/pallas_call | solution.py:178
  392.0 19.4 %weight_grad.10 = (bf16[2,512,2048]{2,1,0:T(8,128)(2,1)}, bf16[512,512]{1,0:T(8,128)(2,1)}, bf16[512,512]{1,0:T(8,128)(2,1)}) custom-call(bf16[512,512]{1,0:T(8,128)(2,1)} %get-tuple-element.187.refs_0_.refs_1_, bf16[512,512]{1,0:T(8,128)(2,1)} %get-tuple-element.181.refs_0_.refs_1_, bf16[512,512]{1,0:T(8,128)(2,1)} %get-tuple-element.188.refs_2_, ...), custom_call_target="tpu_custom_call" | custom-call | flops 858993472 | bytes 2097152 | tf_op jit(solution)/shard_map/weight_grad/pallas_call | solution.py:178
  411.3 14.7 %outputs.6 = (bf16[512,2048]{1,0:T(8,128)(2,1)}, bf16[512,512]{1,0:T(8,128)(2,1)}, bf16[512,1536]{1,0:T(8,128)(2,1)}, f32[8,1536]{1,0:T(8,128)}, bf16[1024,2048]{1,0:T(8,128)(2,1)}) custom-call(bf16[2,512,2048]{2,1,0:T(8,128)(2,1)} %get-tuple-element.189.refs_0_, bf16[1024,2048]{1,0:T(8,128)(2,1)} %bitcast.61, ...), custom_call_target="tpu_custom_call" | custom-call | flops 536870912 | bytes 1887436 | tf_op jit(solution)/shard_map/outputs/pallas_call | solution.py:178
  426.1 3.9 add.134.refs_0_.refs_1_
  430.0 20.2 %weight_grad.11 = (bf16[2,512,2048]{2,1,0:T(8,128)(2,1)}, bf16[512,512]{1,0:T(8,128)(2,1)}) custom-call(bf16[2048,512]{1,0:T(8,128)(2,1)} %add.134.refs_0_.refs_1_, bf16[512,512]{1,0:T(8,128)(2,1)} %get-tuple-element.199.refs_1_, bf16[2048,2048]{1,0:T(8,128)(2,1)} %get-tuple-element.150.refs_5_.refs_3_.refs_2_, ...), custom_call_target="tpu_custom_call" | custom-call | flops 858993472 | bytes 2097152 | tf_op jit(solution)/shard_map/weight_grad/pallas_call | solution.py:178
  450.2 20.7 %backs.7 = (bf16[512,2048]{1,0:T(8,128)(2,1)}, f32[16,2048]{1,0:T(8,128)}, bf16[512,512]{1,0:T(8,128)(2,1)}, bf16[128,2048]{1,0:T(8,128)(2,1)}) custom-call(bf16[2,512,2048]{2,1,0:T(8,128)(2,1)} %get-tuple-element.201.refs_0_.refs_2_.refs_1_, bf16[512,512]{1,0:T(8,128)(2,1)} %get-tuple-element.187.refs_0_.refs_1_, ...), custom_call_target="tpu_custom_call" | custom-call | flops 322122560 | bytes 1415577 | tf_op jit(solution)/shard_map/backs/pallas_call | solution.py:178
  473.0 2.1 finish.8.refs_0_.refs_3_
  475.1 22.0 %outputs.7 = (bf16[512,2048]{1,0:T(8,128)(2,1)}, bf16[512,512]{1,0:T(8,128)(2,1)}, bf16[512,1536]{1,0:T(8,128)(2,1)}, f32[8,1536]{1,0:T(8,128)}, bf16[512,512]{1,0:T(8,128)(2,1)}, /*index=5*/bf16[128,2048]{1,0:T(8,128)(2,1)}) custom-call(bf16[4,512,512]{2,1,0:T(8,128)(2,1)} %finish.8.refs_0_.refs_3_, bf16[2048,512]{1,0:T(8,128)(2,1)} %add.134.refs_0_.refs_1_, ...), custom_call_target="tpu_custom_call" | custom-call | flops 536870912 | bytes 1887436 | tf_op jit(solution)/shard_map/outputs/pallas_call | solution.py:178
  497.4 19.5 %backs.8 = (bf16[512,2048]{1,0:T(8,128)(2,1)}, f32[16,2048]{1,0:T(8,128)}, bf16[512,512]{1,0:T(8,128)(2,1)}, bf16[128,2048]{1,0:T(8,128)(2,1)}) custom-call(f32[8,1536]{1,0:T(8,128)} %get-tuple-element.209.refs_0_, bf16[2048,512]{1,0:T(8,128)(2,1)} %add.134.refs_0_.refs_1_, bf16[2,512,2048]{2,1,0:T(8,128)(2,1)} %get-tuple-element.201.refs_0_.refs_2_.refs_1_, ...), custom_call_target="tpu_custom_call" | custom-call | flops 322122560 | bytes 1415577 | tf_op jit(solution)/shard_map/backs/pallas_call | solution.py:178
  517.0 16.7 %weight_grad.12 = (bf16[2,512,1536]{2,1,0:T(8,128)(2,1)}, bf16[512,512]{1,0:T(8,128)(2,1)}, bf16[128,2048]{1,0:T(8,128)(2,1)}) custom-call(f32[16,2048]{1,0:T(8,128)} %get-tuple-element.211.refs_0_, bf16[2048,512]{1,0:T(8,128)(2,1)} %add.134.refs_0_.refs_1_, bf16[2,512,2048]{2,1,0:T(8,128)(2,1)} %get-tuple-element.201.refs_0_.refs_2_.refs_1_, ...), custom_call_target="tpu_custom_call" | custom-call | flops 644245120 | bytes 1677721 | tf_op jit(solution)/shard_map/weight_grad/pallas_call | solution.py:178
  533.7 2.2 finish.9.refs_0_.refs_3_
  535.9 4.0 add.135.refs_0_.refs_1_.refs_2_.refs_3_
  539.9 20.1 %backs.9 = (bf16[512,2048]{1,0:T(8,128)(2,1)}, f32[16,2048]{1,0:T(8,128)}, bf16[512,512]{1,0:T(8,128)(2,1)}, bf16[1024,1536]{1,0:T(8,128)(2,1)}) custom-call(bf16[512,2048]{1,0:T(8,128)(2,1)} %add.135.refs_0_.refs_1_.refs_2_.refs_3_, bf16[2048,512]{1,0:T(8,128)(2,1)} %add.134.refs_0_.refs_1_, bf16[1024,1536]{1,0:T(8,128)(2,1)} %bitcast.62, ...), custom_call_target="tpu_custom_call" | custom-call | flops 322122560 | bytes 1415577 | tf_op jit(solution)/shard_map/backs/pallas_call | solution.py:178
  560.0 17.5 %weight_grad.13 = (bf16[2,512,1536]{2,1,0:T(8,128)(2,1)}, bf16[128,2048]{1,0:T(8,128)(2,1)}) custom-call(f32[16,2048]{1,0:T(8,128)} %get-tuple-element.219.refs_0_, bf16[512,2048]{1,0:T(8,128)(2,1)} %add.135.refs_0_.refs_1_.refs_2_.refs_3_, bf16[2048,2048]{1,0:T(8,128)(2,1)} %get-tuple-element.135.refs_1_.refs_4_.refs_3_.refs_2_, ...), custom_call_target="tpu_custom_call" | custom-call | flops 644245120 | bytes 1677721 | tf_op jit(solution)/shard_map/weight_grad/pallas_call | solution.py:178
  577.6 2.7 slice_bitcast_fusion
  582.0 5.5 first_half.4
  587.6 2.3 finish.10.refs_0_.refs_3_
  589.8 17.7 %weight_grad.14 = (bf16[2,512,512]{2,1,0:T(8,128)(2,1)}, bf16[2048,512]{1,0:T(8,128)(2,1)}, bf16[128,2048]{1,0:T(8,128)(2,1)}) custom-call(f32[4,512,512]{2,1,0:T(8,128)} %finish.10.refs_0_.refs_3_, bf16[2048,512]{1,0:T(8,128)(2,1)} %get-tuple-element.226.refs_0_.refs_1_, bf16[512,2048]{1,0:T(8,128)(2,1)} %add.135.refs_0_.refs_1_.refs_2_.refs_3_, ...), custom_call_target="tpu_custom_call" | custom-call | flops 214748368 | bytes 838860 | tf_op jit(solution)/shard_map/weight_grad/pallas_call | solution.py:178
  607.6 25.2 %gate.11 = (f32[8192]{0:T(1024)}, bf16[1024,512]{1,0:T(8,128)(2,1)}, bf16[128,2048]{1,0:T(8,128)(2,1)}, bf16[128,2048]{1,0:T(8,128)(2,1)}) custom-call(bf16[2,512,512]{2,1,0:T(8,128)(2,1)} %get-tuple-element.232.refs_0_, bf16[1024,512]{1,0:T(8,128)(2,1)} %bitcast.65, ...), custom_call_target="tpu_custom_call", output_to_operand_aliasing={{0}: (4, {})} | custom-call | tf_op jit(solution)/shard_map/gate/pallas_call | solution.py:178
  634.1 3.9 collective-permute-done.7
  639.5 6.5 weight_grad.15.refs_0_.refs_1_
  645.9 5.6 first_half.5
  651.6 3.5 add.136.refs_0_.refs_1_
  658.3 2.2 collective-permute-start.9
  660.5 2.7 collective-permute-done.9
  663.8 2.1 finish.11.refs_0_.refs_3_
  666.6 4.9 collective-permute-done.10.refs_2_
  671.5 2.1 add.137.refs_0_.refs_1_
  673.6 3.4 second_half.4.refs_0_
  678.9 3.4 second_half.5.refs_0_
  682.3 2.3 finish.12.refs_0_.refs_3_
  684.6 2.1 finish.13.refs_0_
  689.6 2.5 collective-permute-done.14.refs_2_
  692.1 4.4 first_half.6
  698.2 12.7 %collective-permute-done.15.refs_2_ = bf16[512,512]{1,0:T(8,128)(2,1)S(1)} collective-permute-done((bf16[512,512]{1,0:T(8,128)(2,1)S(1)}, bf16[512,512]{1,0:T(8,128)(2,1)S(1)}, u32[]{:S(2)}, u32[]{:S(2)}) %collective-permute-start.15) | collective-permute-done | bytes 524320 | tf_op jit(solution)/shard_map/ppermute | solution.py:107
  711.7 2.5 first_half.7
  715.8 2.3 finish.14.refs_0_.refs_3_
  721.8 2.9 second_half.6.refs_0_
  725.5 2.0 second_half.7.refs_0_
  727.4 2.3 finish.15
  (167 shorter events, 44.5 us)
Async XLA Ops:
  7.2 465.8 %reduce-scatter.9.cloned.1.call-start = ((), (), s32[]{:S(2)}) async-start(), calls=%async_computation.8 | async-start | bytes 2621440 | tf_op jit(solution)/shard_map/reduce_scatter | solution.py:1009
  13.4 4.7 collective-permute-start
  18.1 0.6 copy-start.26
  21.6 46.7 %collective-permute-start.1 = (bf16[512,2048]{1,0:T(8,128)(2,1)}, bf16[512,2048]{1,0:T(8,128)(2,1)S(1)}, u32[]{:S(2)}, u32[]{:S(2)}) collective-permute-start(bf16[512,2048]{1,0:T(8,128)(2,1)} %pick.2.refs_0_), channel_id=1, source_target_pairs={{0,1},{1,0},{2,3},{3,2},{4,5},{5,4},{6,7},{7,6},{8,9},{9,8},{10,11... | collective-permute-start | bytes 6291464 | tf_op jit(solution)/shard_map/ppermute | solution.py:107
  24.5 18.9 %copy-start.18 = (f32[2048]{0:T(1024)}, f32[2048]{0:T(1024)S(1)}, u32[]{:S(2)}) copy-start(f32[2048]{0:T(1024)S(1)} %pad_maximum_fusion.2) | copy-start | bytes 24580
  24.5 18.8 %copy-start.25 = (f32[2048]{0:T(1024)}, f32[2048]{0:T(1024)S(1)}, u32[]{:S(2)}) copy-start(f32[2048]{0:T(1024)S(1)} %pad_maximum_fusion.4) | copy-start | bytes 24580
  68.4 1.3 copy-start
  69.7 1.7 copy-start.29
  69.7 4.4 collective-permute-start.2
  69.7 66.8 %collective-permute-start.3 = (bf16[512,2048]{1,0:T(8,128)(2,1)}, bf16[512,2048]{1,0:T(8,128)(2,1)}, u32[]{:S(2)}, u32[]{:S(2)}) collective-permute-start(bf16[512,2048]{1,0:T(8,128)(2,1)} %get-tuple-element.147), channel_id=1, source_target_pairs={{0,1},{1,0},{2,3},{3,2},{4,5},{5,4},{6,7},{7,6},{8,9},{9,8},{10,11... | collective-permute-start | bytes 6291464 | tf_op jit(solution)/shard_map/ppermute | solution.py:107
  74.0 1.3 copy-start.1
  136.5 1.9 copy-start.28
  136.5 4.6 collective-permute-start.4
  136.6 48.3 %collective-permute-start.5 = (bf16[2048,512]{1,0:T(8,128)(2,1)}, bf16[2048,512]{1,0:T(8,128)(2,1)S(1)}, u32[]{:S(2)}, u32[]{:S(2)}) collective-permute-start(bf16[2048,512]{1,0:T(8,128)(2,1)} %get-tuple-element.134.refs_0_), channel_id=1, source_target_pairs={{0,1},{1,0},{2,3},{3,2},{4,5},{5,4},{6,7},{7,6},{8,9},{9,8},{10,11... | collective-permute-start | bytes 6291464 | tf_op jit(solution)/shard_map/ppermute | solution.py:107
  184.8 1.4 copy-start.2
  186.2 4.4 collective-permute-start.6
  190.6 1.4 copy-start.3
  204.7 329.0 %reduce-scatter.11.cloned.1.call-start = ((), (), s32[]{:S(2)}) async-start(), calls=%async_computation.9 | async-start | bytes 2621440 | tf_op jit(solution)/shard_map/reduce_scatter | solution.py:1009
  282.5 305.0 %reduce-scatter.13.cloned.1.call-start = ((), (), s32[]{:S(2)}) async-start(), calls=%async_computation.10 | async-start | bytes 2621440 | tf_op jit(solution)/shard_map/reduce_scatter | solution.py:1014
  357.1 306.7 %reduce-scatter.15.cloned.1.call-start = ((), (), s32[]{:S(2)}) async-start(), calls=%async_computation.11 | async-start | bytes 2621440 | tf_op jit(solution)/shard_map/reduce_scatter | solution.py:1009
  426.0 256.3 %reduce-scatter.17.cloned.1.call-start = ((), (), s32[]{:S(2)}) async-start(), calls=%async_computation.12 | async-start | bytes 2621440 | tf_op jit(solution)/shard_map/reduce_scatter | solution.py:1014
  471.0 0.7 copy-start.30
  471.0 0.7 copy-start.31
  471.0 213.5 %reduce-scatter.19.cloned.1.call-start = ((), (), s32[]{:S(2)}) async-start(), calls=%async_computation.13 | async-start | bytes 2621440 | tf_op jit(solution)/shard_map/reduce_scatter | solution.py:1009
  497.2 218.7 %reduce-scatter.21.cloned.1.call-start = ((), (), s32[]{:S(2)}) async-start(), calls=%async_computation.14 | async-start | bytes 2621440 | tf_op jit(solution)/shard_map/reduce_scatter | solution.py:1014
  517.0 210.5 %reduce-scatter.23.cloned.1.call-start = ((), (), s32[]{:S(2)}) async-start(), calls=%async_computation.15 | async-start | bytes 2621440 | tf_op jit(solution)/shard_map/reduce_scatter | solution.py:1014
  577.5 3.7 copy-start.10
  577.5 3.7 copy-start.11
  577.5 3.7 copy-start.12
  577.6 3.7 copy-start.13
  580.3 1.0 copy-start.14
  580.3 71.3 %collective-permute-start.8 = (bf16[512,1536]{1,0:T(8,128)(2,1)}, bf16[512,1536]{1,0:T(8,128)(2,1)}, u32[]{:S(2)}, u32[]{:S(2)}) collective-permute-start(bf16[512,1536]{1,0:T(8,128)(2,1)} %slice_bitcast_fusion), channel_id=1, source_target_pairs={{0,1},{1,0},{2,3},{3,2},{4,5},{5,4},{6,7},{7,6},{8,9},{9,8},{10,11... | collective-permute-start | bytes 4718600 | tf_op jit(solution)/shard_map/ppermute | solution.py:107
  632.8 5.3 collective-permute-start.7
  651.5 5.3 copy-start.4
  651.5 6.7 copy-start.19
  651.5 6.7 copy-start.20
  651.5 6.8 copy-start.15
  651.5 8.9 %copy-start.21 = (f32[8,1536]{1,0:T(8,128)S(1)}, f32[8,1536]{1,0:T(8,128)}, u32[]{:S(2)}) copy-start(f32[8,1536]{1,0:T(8,128)} %get-tuple-element.157.refs_0_) | copy-start | bytes 147460
  651.5 8.9 %copy-start.22 = (f32[8,1536]{1,0:T(8,128)S(1)}, f32[8,1536]{1,0:T(8,128)}, u32[]{:S(2)}) copy-start(f32[8,1536]{1,0:T(8,128)} %get-tuple-element.170.refs_0_) | copy-start | bytes 147460
  651.5 8.9 %copy-start.23 = (f32[8,1536]{1,0:T(8,128)S(1)}, f32[8,1536]{1,0:T(8,128)}, u32[]{:S(2)}) copy-start(f32[8,1536]{1,0:T(8,128)} %get-tuple-element.194.refs_0_) | copy-start | bytes 147460
  651.5 8.9 %copy-start.24 = (f32[8,1536]{1,0:T(8,128)S(1)}, f32[8,1536]{1,0:T(8,128)}, u32[]{:S(2)}) copy-start(f32[8,1536]{1,0:T(8,128)} %get-tuple-element.209.refs_0_) | copy-start | bytes 147460
  651.5 26.1 %collective-permute-start.11 = (bf16[512,2048]{1,0:T(8,128)(2,1)}, bf16[512,2048]{1,0:T(8,128)(2,1)S(1)}, u32[]{:S(2)}, u32[]{:S(2)}) collective-permute-start(bf16[512,2048]{1,0:T(8,128)(2,1)} %get-tuple-element.239.refs_0_), channel_id=1, source_target_pairs={{0,8},{8,0},{16,24},{24,16},{1,9},{9,1},{17,25},{25,17},{2,10},{10... | collective-permute-start | bytes 6291464 | tf_op jit(solution)/shard_map/ppermute | solution.py:107
  655.1 37.0 %collective-permute-start.14 = (bf16[512,1536]{1,0:T(8,128)(2,1)}, bf16[512,1536]{1,0:T(8,128)(2,1)}, u32[]{:S(2)}, u32[]{:S(2)}) collective-permute-start(bf16[512,1536]{1,0:T(8,128)(2,1)} %add.136.refs_0_.refs_1_), channel_id=1, source_target_pairs={{0,16},{8,24},{16,0},{24,8},{1,17},{9,25},{17,1},{25,9},{2,18},{10... | collective-permute-start | bytes 4718600 | tf_op jit(solution)/shard_map/ppermute | solution.py:107
  656.8 14.7 %collective-permute-start.10 = (bf16[512,512]{1,0:T(8,128)(2,1)S(1)}, bf16[512,512]{1,0:T(8,128)(2,1)}, u32[]{:S(2)}, u32[]{:S(2)}) collective-permute-start(bf16[512,512]{1,0:T(8,128)(2,1)S(1)} %slice_bitcast_fusion.1), channel_id=1, source_target_pairs={{0,1},{1,0},{2,3},{3,2},{4,5},{5,4},{6,7},{7,6},{8,9},{9,8},{10,11... | collective-permute-start | bytes 1572872 | tf_op jit(solution)/shard_map/ppermute | solution.py:107
  658.3 4.9 collective-permute-start.9
  665.9 11.0 %collective-permute-start.12 = (f32[13824]{0:T(1024)}, f32[13824]{0:T(1024)S(1)}, u32[]{:S(2)}, u32[]{:S(2)}) collective-permute-start(f32[13824]{0:T(1024)} %gate.13.refs_0_), channel_id=1, source_target_pairs={{0,1},{1,0},{2,3},{3,2},{4,5},{5,4},{6,7},{7,6},{8,9},{9,8},{10,11... | collective-permute-start | bytes 165896 | tf_op jit(solution)/shard_map/ppermute | solution.py:107
  673.6 3.4 copy-start.8
  677.6 1.3 copy-start.6
  686.7 9.9 %copy-start.5 = (bf16[512,512]{1,0:T(8,128)(2,1)S(1)}, bf16[512,512]{1,0:T(8,128)(2,1)}, u32[]{:S(2)}) copy-start(bf16[512,512]{1,0:T(8,128)(2,1)} %add.137.refs_0_.refs_1_) | copy-start | bytes 1572868
  686.7 1.5 collective-permute-start.13
  696.6 17.6 %copy-start.9 = (f32[13824]{0:T(1024)S(1)}, f32[13824]{0:T(1024)}, u32[]{:S(2)}) copy-start(f32[13824]{0:T(1024)} %gate.15.refs_0_) | copy-start | bytes 165892
  696.6 24.0 %collective-permute-start.16 = (bf16[512,1536]{1,0:T(8,128)(2,1)}, bf16[512,1536]{1,0:T(8,128)(2,1)S(1)}, u32[]{:S(2)}, u32[]{:S(2)}) collective-permute-start(bf16[512,1536]{1,0:T(8,128)(2,1)} %get-tuple-element.246.refs_0_), channel_id=1, source_target_pairs={{0,8},{8,0},{16,24},{24,16},{1,9},{9,1},{17,25},{25,17},{2,10},{10... | collective-permute-start | bytes 4718600 | tf_op jit(solution)/shard_map/ppermute | solution.py:107
  696.6 14.3 %collective-permute-start.15 = (bf16[512,512]{1,0:T(8,128)(2,1)S(1)}, bf16[512,512]{1,0:T(8,128)(2,1)S(1)}, u32[]{:S(2)}, u32[]{:S(2)}) collective-permute-start(bf16[512,512]{1,0:T(8,128)(2,1)S(1)} %copy-done.5), channel_id=1, source_target_pairs={{0,16},{8,24},{16,0},{24,8},{1,17},{9,25},{17,1},{25,9},{2,18},{10... | collective-permute-start | bytes 1572872 | tf_op jit(solution)/shard_map/ppermute | solution.py:107
  710.9 0.8 copy-start.16
  714.2 10.4 %collective-permute-start.17 = (bf16[512,512]{1,0:T(8,128)(2,1)}, bf16[512,512]{1,0:T(8,128)(2,1)S(1)}, u32[]{:S(2)}, u32[]{:S(2)}) collective-permute-start(bf16[512,512]{1,0:T(8,128)(2,1)} %get-tuple-element.247.refs_0_), channel_id=1, source_target_pairs={{0,8},{8,0},{16,24},{24,16},{1,9},{9,1},{17,25},{25,17},{2,10},{10... | collective-permute-start | bytes 1572872 | tf_op jit(solution)/shard_map/ppermute | solution.py:107
  714.2 4.3 collective-permute-start.18
  719.9 9.7 %copy-start.27 = (f32[1024]{0:T(1024)}, f32[1024]{0:T(1024)S(1)}, u32[]{:S(2)}) copy-start(f32[1024]{0:T(1024)S(1)} %get-tuple-element.314) | copy-start | bytes 12292
  720.6 1.2 copy-start.7
  724.7 0.8 copy-start.17
Sparse Core Ops, SparseCore 0:
  204.9 45.2 reduce-scatter.8
  282.7 44.9 reduce-scatter.10
  357.2 44.0 reduce-scatter.12
  426.2 44.2 reduce-scatter.14
  472.6 43.1 reduce-scatter.16
  518.0 43.1 reduce-scatter.18
  563.6 43.1 reduce-scatter.20
  609.2 43.8 reduce-scatter.22

commit v3 on v2

--- a/solution.py
+++ b/solution.py
@@ -114,10 +114,25 @@
 
 
 def call(line, kernel, w, grid, inputs, outputs, scratch=(), flops=0, nbytes=0, name=None, alias=None):
-    before = list(line.last)
+    before = [token for token in line.last if alias is None or token is not inputs[alias][0]]
     rides, line.rides = line.rides, []
     skip = len(before) + len(rides)
     ends = len(inputs) + len(outputs)
+    steps = 1
+    for size in grid:
+        steps *= size
+    staged = [i for i in range(len(inputs)) if rides and steps == 1 and inputs[i][1] is not None]
+
+    def stage(ref, block, index):
+        cut = []
+        for size, place in zip(block, index(*[0] * len(grid), w)):
+            if size is None:
+                cut.append(place)
+            elif isinstance(place, int):
+                cut.append(slice(place * size, (place + 1) * size))
+            else:
+                cut.append(pl.ds(pl.multiple_of(place * size, size), size))
+        return ref.at[tuple(cut)]
 
     def at(index):
         return None if index is None else lambda *steps: index(*steps, w)
@@ -142,6 +157,16 @@
             kernel(w, *own, *rest)
             return
         *rest, sent, got = rest
+        own = list(own)
+        loads = []
+        if staged:
+            *rest, loaded = rest
+            buffers = rest[len(rest) - len(staged) :]
+            rest = rest[: len(rest) - len(staged)]
+            for k, i in enumerate(staged):
+                part = stage(own[i], *inputs[i][1:])
+                loads.append(pltpu.make_async_copy(part, buffers[k], loaded.at[k]))
+                own[i] = buffers[k]
         copies = lambda: [
             ride.copy(source, target, sent.at[i], got.at[i])
             for i, (ride, source, target) in enumerate(zip(rides, sources, targets))
@@ -162,7 +187,11 @@
             for copy in copies():
                 copy.wait()
 
+        for load in loads:
+            load.start()
         on_step(False, start)
+        for load in loads:
+            load.wait()
         kernel(w, *own, *rest)
         on_step(True, wait)
 
@@ -173,12 +202,22 @@
     if rides:
         params.update(collective_id=line.count, has_side_effects=True)
         line.count += 1
-        sems = [pltpu.SemaphoreType.DMA((len(rides),))] * 2
+        for i in staged:
+            array, block, _ = inputs[i]
+            shape = tuple(size for size in block if size is not None)
+            sems.append(pltpu.VMEM(shape, array.dtype))
+        if staged:
+            sems.append(pltpu.SemaphoreType.DMA((len(staged),)))
+        sems += [pltpu.SemaphoreType.DMA((len(rides),))] * 2
     anywhere = pl.BlockSpec(memory_space=pl.ANY)
     results = pl.pallas_call(
         body,
         grid=grid,
-        in_specs=[anywhere] * skip + [spec(block, at(index)) for _, block, index in inputs],
+        in_specs=[anywhere] * skip
+        + [
+            anywhere if i in staged else spec(block, at(index))
+            for i, (_, block, index) in enumerate(inputs)
+        ],
         out_specs=[spec(block, at(index)) for _, _, block, index in outputs]
         + [anywhere] * len(rides),
         scratch_shapes=list(scratch) + sems,
@@ -800,36 +839,37 @@
     )[0]
 
 
-def finish_kernel(more, w, kept, cols, *refs):
-    refs = refs[1:] if more == "held" else refs
+def finish_kernel(count, more, w, kept, *refs):
+    cols, refs = refs[:count], refs[count:]
+    refs = refs[1:] if more else refs
     *bias, out = refs
-    value = kept[...].astype(F32) + cols[...].astype(F32)
-    for ref in bias:
-        value = value + ref[...]
-    out[...] = value.astype(out.dtype)
-
-
-def finish(line, w, m, held, kept, cols, bias, shape, dtype):
-    count, rows, columns = shape
-    block = (rows, columns)
-    inputs = [
-        (kept, (None,) + block, lambda i, w: (m, 0, w[TENSOR])),
-        (cols, block, fixed(0, 0)),
-    ]
+    for i in range(count):
+        value = kept[i].astype(F32) + cols[i][...].astype(F32)
+        for ref in bias:
+            value = value + ref[...]
+        out[i] = value.astype(out.dtype)
+
+
+def finish(line, w, place, held, kept, cols, bias, shape, dtype):
+    _, rows, columns = shape
+    count = len(cols)
+    block = (count, rows, columns)
+    inputs = [(kept, block, lambda i, w: (place, 0, w[TENSOR]))]
+    inputs += [(part, (rows, columns), fixed(0, 0)) for part in cols]
     if held is not None:
         inputs.append((held, None, None))
     if bias is not None:
         inputs.append((bias, (1, columns), lambda i, w: (0, w[TENSOR])))
     return call(
         line,
-        functools.partial(finish_kernel, None if held is None else "held"),
+        functools.partial(finish_kernel, count, held is not None),
         w,
         (1,),
         inputs,
-        [(shape, dtype, (None,) + block, fixed(m, 0, 0))],
-        nbytes=8 * rows * columns,
+        [(shape, dtype, block, fixed(place, 0, 0))],
+        nbytes=8 * count * rows * columns,
         name="finish",
-        alias=None if held is None else 2,
+        alias=None if held is None else 1 + count,
     )[0]
 
 
@@ -1013,15 +1053,42 @@
         totals["one"] = totals["one"] + sums
         back_cols[m] = lax.psum_scatter(part, "tensor", scatter_dimension=1, tiled=True)
 
-    def finish_out(m):
+    def finish_out(first, count):
         held["output"] = finish(
-            line, w, m, held["output"], states, branch[m], bias, out_shape, BF16
+            line,
+            w,
+            first // count,
+            held["output"],
+            states,
+            [branch[m] for m in range(first, first + count)],
+            bias,
+            out_shape,
+            BF16,
         )
 
-    def finish_back(m):
+    def finish_back(first, count):
         held["input_grad"] = finish(
-            line, w, m, held["input_grad"], out_grad, back_cols[m], None, out_shape, F32
+            line,
+            w,
+            first // count,
+            held["input_grad"],
+            out_grad,
+            [back_cols[m] for m in range(first, first + count)],
+            None,
+            out_shape,
+            F32,
         )
+
+    def spread(vector, axis):
+        size = -(-vector.size // 1024) * 1024
+        vector = jnp.pad(vector, (0, size - vector.size)).reshape(8, size // 8)
+        return [vector] + [line.ride(vector, axis, k) for k in range(1, lax.axis_size(axis))]
+
+    def summed(parts, size):
+        parts = landed(parts)
+        while len(parts) > 1:
+            parts = [one + two for one, two in zip(parts[::2], parts[1::2])]
+        return parts[0].reshape(-1)[:size]
 
     grads, terms = {}, {
         "down": (False, cot, None),
@@ -1071,11 +1138,15 @@
     def all_over_x(name):
         rides[name] = [swap(found[name], "seq", steps[name])]
 
-    def landed(name):
-        return [ride.result if isinstance(ride, Ride) else ride for ride in rides[name]]
+    def rest_over_x(name):
+        for first, size in parts(name, PIECES[name] - len(rides[name])):
+            rides[name].append(swap(found[name][first : first + size], "seq", steps[name]))
+
+    def landed(parts):
+        return [part.result if isinstance(part, Ride) else part for part in parts]
 
     def add_up(name):
-        found[name] = add(line, w, found[name], landed(name))
+        found[name] = add(line, w, found[name], landed(rides[name]))
         rides[name] = []
         steps[name] = 2
         while 2 * steps[name] < n:
@@ -1087,7 +1158,7 @@
 
     def mine_done(name):
         held[name], found[name] = first_half(
-            line, w, terms[name][0], found[name], landed(name)
+            line, w, terms[name][0], found[name], landed(rides[name])
         )
 
     def sibling_swap(name):
@@ -1115,10 +1186,6 @@
         rest = jnp.concatenate([qkv_total.sum(0), up_total.sum(0), cot_total.sum(0)])
         return norm_terms, rest
 
-    def hop(vector, axis, step):
-        vector = gate(line, w, vector)
-        return vector + swap(vector, axis, step)
-
     project(0)
     bring(0, 1, 2, 3)
     project(1)
@@ -1129,91 +1196,93 @@
     give(0, 1, 2, 3)
     activated, slope = feed_up(line, w, rows, two, up, up_shift)
     down = both_cores(down_weight, down_got, False)
+    bring(2, 1, 2)
     put_out(0)
-    bring(2, 1, 2)
+    bring(2, 3)
     attend(1)
+    give(1, 1, 2)
     send("down", [activated])
-    give(1, 1, 2, 3)
+    give(1, 3)
+    bring(3, 1, 2)
+    to_sibling("down")
     pre_grad, up_total = pre_grads(line, w, rows, cot, down, slope)
-    to_sibling("down")
+    bring(3, 3)
     put_out(1)
-    bring(2, 3)
-    keep("down")
-    bring(3, 1, 2, 3)
-    over_y("down", 3)
-    part_two, two_sums = backs(line, w, rows, 0, micros, pre_grad, up, x, vectors[2:3])
-    go_back(0)
-    over_y("down", 1)
     attend(2)
     give(2, 1, 2)
+    keep("down")
+    give(2, 3)
+    over_y("down", 1)
     attend(3)
-    give(2, 3)
-    give(3, 1)
+    give(3, 1, 2)
+    over_y("down", 1)
+    put_out(2)
+    give(3, 3)
+    over_y("down", 1)
     send("up", [pre_grad])
+    over_y("down", 1)
     to_sibling("up")
-    put_out(2)
+    put_out(3)
     add_up("down")
-    give(3, 2)
+    over_x("down", 1)
     keep("up")
-    give(3, 3)
+    over_x("down", 3)
+    over_y("up", 3)
+    part_two, two_sums = backs(line, w, rows, 0, micros, pre_grad, up, x, vectors[2:3])
     over_y("up", 1)
-    go_back(1)
-    finish_out(0)
-    over_x("down", 1)
-    over_y("up", 1)
-    put_out(3)
-    over_x("down", 1)
-    over_y("up", 1)
-    go_back(2)
+    go_back(0)
+    add_up("up")
     heads_out = [attended[m] for m in range(micros)]
     heads_grad = [qkv_grad[m] for m in range(micros)]
-    over_x("down", 1)
-    over_y("up", 1)
+    over_x("up", 1)
     send("qkv", heads_grad)
-    finish_out(1)
-    add_up("up")
-    over_x("down", 1)
+    over_x("up", 1)
     to_sibling("qkv")
-    go_back(3)
+    send("dense", heads_out)
+    over_x("up", 1)
+    to_sibling("dense")
+    go_back(1)
     over_x("up", 1)
     keep("qkv")
+    over_y("qkv", 1)
+    go_back(2)
+    over_y("qkv", 1)
+    keep("dense")
+    add_up("qkv")
+    over_x("qkv", 1)
+    over_y("dense", 1)
+    go_back(3)
+    norm_terms, rest = all_terms()
+    size = norm_terms.size
+    spreads = spread(norm_terms, "tensor")
+    add_up("dense")
+    norm_terms = summed(spreads, size)
+    vector = jnp.concatenate([norm_terms, rest])
+    size = vector.size
+    spreads = spread(vector, "seq")
+    one_sums = gate(line, w, totals["one"])
+    vector = summed(spreads, size)
+    found["qkv"] = gate(line, w, found["qkv"])
+    rest_over_x("qkv")
     mine_done("down")
-    finish_back(0)
-    all_over_y("qkv")
-    to_sibling("down")
-    over_x("up", 1)
-    send("dense", heads_out)
-    to_sibling("dense")
-    over_x("up", 2)
-    norm_terms, rest = all_terms()
-    step = 1
-    while step < lax.axis_size("tensor"):
-        norm_terms, step = hop(norm_terms, "tensor", step), 2 * step
-    keep("dense")
-    all_over_y("dense")
+    sibling_swap("down")
     mine_done("up")
-    add_up("qkv")
-    all_over_x("qkv")
     sibling_swap("up")
-    finish_out(2)
-    vector = hop(jnp.concatenate([norm_terms, rest]), "dp", 1)
-    add_up("dense")
-    all_over_x("dense")
+    finish_out(0, micros)
+    mine_done("qkv")
+    sibling_swap("qkv")
+    rest_over_x("dense")
+    spreads = spread(vector, "dp")
+    one_sums = gate(line, w, one_sums)
+    vector = summed(spreads, size)
     all_done("down")
     all_done("up")
-    finish_back(1)
-    finish_out(3)
-    step = 1
-    while step < n:
-        vector, step = hop(vector, "seq", step), 2 * step
-    mine_done("qkv")
-    sibling_swap("qkv")
     mine_done("dense")
     sibling_swap("dense")
-    finish_back(2)
+    finish_back(0, micros - 1)
     all_done("qkv")
     all_done("dense")
-    finish_back(3)
+    finish_back(micros - 1, 1)
     norm_terms = vector[: 4 * features].reshape(4, features)
     rest = vector[4 * features :]
     count = columns // 2

time: 746 us -> 704 us (0.944)
  waiting for transfers between devices: 61.7 us -> 45.3 us
  Pallas kernels: 608 us -> 592 us
    ppermute x19 -> x13, waiting for transfers between devices: 61.5 us -> 45.1 us  [swap(): lax.ppermute(block, axis, [(i, i ^ distance) for i in range(lax.axis_size...]
    pallas_call x56 -> x49, Pallas kernels: 608 us -> 592 us  [call(): pl.pallas_call(body, grid=grid, in_specs=[anywhere] * skip + [anywhere if...]
    ppermute x19 -> x13, starting transfers between devices: 20 us -> 12.5 us  [swap(): lax.ppermute(block, axis, [(i, i ^ distance) for i in range(lax.axis_size...]
  transfers between devices with their start and end apart: 27 -> 21, of which waited for: 13 -> 7; matrix products, arithmetic and copies ran while one was open for 2% -> 2% of each run, Pallas kernels for 80% -> 82%
where the time goes in v3:
time: 704 us; the launch traced here: 696 us
  Pallas kernels  592 us (84%)
  waiting for transfers between devices  45.3 us (6%)
  local copies, waits for them, and re-layouts  20.1 us (3%)
  between operations  15.2 us (2%)
  starting transfers between devices  13.5 us (2%)
  other arithmetic  9.29 us (1%)
    pallas_call x49, Pallas kernels, call(): pl.pallas_call(body, grid=grid, in_specs=[anywhere] * skip + [anywhere if...  592 us
    ppermute x13, waiting for transfers between devices, swap(): lax.ppermute(block, axis, [(i, i ^ distance) for i in range(lax.axis_size...  45.1 us
    unnamed x79, local copies, waits for them, and re-layouts  14.9 us
  transfers between devices with their start and end apart: 21, of which 7 were waited for; matrix products, arithmetic and copies ran while one was open for 2% of the time, Pallas kernels for 82%

profile of v3, /device:TPU:0, one launch (start us, length us, event | category | flops | bytes accessed | tf_op | source)
XLA Modules:
  0.0 695.6 jit_solution(8575048418258626675)
XLA Ops:
  13.4 3.0 collective-permute-start
  16.3 1.7 collective-permute-done.refs_0_
  18.7 3.0 pick.2.refs_0_
  21.6 2.0 collective-permute-start.1
  25.8 18.1 %norms.1 = (bf16[2048,2048]{1,0:T(8,128)(2,1)}, bf16[2048,2048]{1,0:T(8,128)(2,1)}, f32[8,2048]{1,0:T(8,128)}) custom-call(bf16[512,2048]{1,0:T(8,128)(2,1)} %pick.2.refs_0_, bf16[2048,2048]{1,0:T(8,128)(2,1)} %bitcast.52, bf16[2048,2048]{1,0:T(8,128)(2,1)} %bitcast.31, f32[4,2048]{1,0:T(4,128)} %pad_maximum_fusion.refs_3_), custom_call_target="tpu_custom_call" | custom-call | flops 12582912 | bytes 3355443 | tf_op jit(solution)/shard_map/norms/pallas_call | solution.py:213
  43.9 4.4 pick.3
  48.3 20.0 %collective-permute-done.1.refs_1_ = bf16[512,2048]{1,0:T(8,128)(2,1)S(1)} collective-permute-done((bf16[512,2048]{1,0:T(8,128)(2,1)}, bf16[512,2048]{1,0:T(8,128)(2,1)S(1)}, u32[]{:S(2)}, u32[]{:S(2)}) %collective-permute-start.1) | collective-permute-done | bytes 2097184 | tf_op jit(solution)/shard_map/ppermute | solution.py:107
  68.4 1.3 copy-done
  69.7 1.7 collective-permute-start.3
  72.7 1.3 collective-permute-done.2.refs_4_.refs_14_.refs_7_.refs_17_.refs_9_.refs_8_.refs_10_.refs_5_.refs_6_
  74.0 1.3 copy-done.1
  75.4 10.6 %projections.2 = (bf16[512,512]{1,0:T(8,128)(2,1)}, bf16[512,512]{1,0:T(8,128)(2,1)}, bf16[512,512]{1,0:T(8,128)(2,1)}, bf16[512,512]{1,0:T(8,128)(2,1)}) custom-call(bf16[512,2048]{1,0:T(8,128)(2,1)} %gate.6.refs_0_.refs_3_.refs_13_.refs_6_.refs_16_.refs_8_.refs_7_.refs_9_.refs_4_.refs_5_, bf16[2048,2048]{1,0:T(8,128)(2,1)} %get-tuple-element.149.refs_1_.refs_4_.refs_2_, ...), custom_call_target="tpu_custom_call" | custom-call | flops 429496736 | bytes 1468006 | tf_op jit(solution)/shard_map/projections/pallas_call | solution.py:213
  86.0 32.5 %projections.3 = (bf16[1536,512]{1,0:T(8,128)(2,1)}, bf16[1536,512]{1,0:T(8,128)(2,1)}, bf16[1536,512]{1,0:T(8,128)(2,1)}, bf16[1536,512]{1,0:T(8,128)(2,1)}, bf...) custom-call(bf16[512,512]{1,0:T(8,128)(2,1)} %get-tuple-element.150.refs_0_.refs_3_, ...), custom_call_target="tpu_custom_call" | custom-call | flops 1288490240 | bytes 2726297 | tf_op jit(solution)/shard_map/projections/pallas_call | solution.py:213
  118.5 16.2 %attention.4 = (bf16[512,512]{1,0:T(8,128)(2,1)}, bf16[512,512]{1,0:T(8,128)(2,1)}, bf16[512,512]{1,0:T(8,128)(2,1)}, bf16[512,512]{1,0:T(8,128)(2,1)}, bf16[512...) custom-call(bf16[1536,512]{1,0:T(8,128)(2,1)} %get-tuple-element.153.refs_0_.refs_1_, ...), custom_call_target="tpu_custom_call" | custom-call | flops 751619264 | bytes 629145 | tf_op jit(solution)/shard_map/attention/pallas_call | solution.py:213
  134.8 1.8 collective-permute-start.5
  137.2 2.1 collective-permute-done.4.refs_8_.refs_10_
  139.3 41.0 %feed_up.1 = (bf16[2048,2048]{1,0:T(8,128)(2,1)}, bf16[2048,2048]{1,0:T(8,128)(2,1)}, bf16[512,512]{1,0:T(8,128)(2,1)}, bf16[512,512]{1,0:T(8,128)(2,1)}, bf16[5...) custom-call(bf16[512,2048]{1,0:T(8,128)(2,1)} %gate.7.refs_0_.refs_7_.refs_9_, ...), custom_call_target="tpu_custom_call" | custom-call | flops 1717986944 | bytes 4194304 | tf_op jit(solution)/shard_map/feed_up/pallas_call | solution.py:213
  180.3 2.7 collective-permute-done.5.refs_1_
  183.1 1.3 copy-done.2
  184.4 4.4 collective-permute-done.6.refs_6_.refs_11_.refs_5_.refs_7_
  188.8 1.3 copy-done.4
  190.1 16.7 %outputs.4 = (bf16[512,2048]{1,0:T(8,128)(2,1)}, bf16[512,512]{1,0:T(8,128)(2,1)}, bf16[512,1536]{1,0:T(8,128)(2,1)}, f32[8,1536]{1,0:T(8,128)}, bf16[512,512]{1,0:T(8,128)(2,1)}, /*index=5*/bf16[512,512]{1,0:T(8,128)(2,1)}) custom-call(bf16[2048,512]{1,0:T(8,128)(2,1)} %gate.8.refs_0_.refs_5_.refs_10_.refs_4_.refs_6_, ...), custom_call_target="tpu_custom_call" | custom-call | flops 536870912 | bytes 1887436 | tf_op jit(solution)/shard_map/outputs/pallas_call | solution.py:213
  207.1 16.0 %attention.5 = (bf16[512,512]{1,0:T(8,128)(2,1)}, bf16[512,512]{1,0:T(8,128)(2,1)}, bf16[512,512]{1,0:T(8,128)(2,1)}, bf16[512,512]{1,0:T(8,128)(2,1)}, bf16[512,512]{1,0:T(8,128)(2,1)}) custom-call(f32[8,1536]{1,0:T(8,128)} %get-tuple-element.171.refs_0_, bf16[1536,512]{1,0:T(8,128)(2,1)} %get-tuple-element.153.refs_0_.refs_1_, ...), custom_call_target="tpu_custom_call" | custom-call | flops 751619264 | bytes 629145 | tf_op jit(solution)/shard_map/attention/pallas_call | solution.py:213
  223.1 18.3 %weight_grad.8 = (bf16[2,2048,512]{2,1,0:T(8,128)(2,1)}, bf16[512,512]{1,0:T(8,128)(2,1)}, bf16[512,512]{1,0:T(8,128)(2,1)}) custom-call(bf16[512,512]{1,0:T(8,128)(2,1)} %get-tuple-element.176.refs_0_.refs_1_, bf16[512,512]{1,0:T(8,128)(2,1)} %get-tuple-element.177.refs_1_, bf16[512,512]{1,0:T(8,128)(2,1)} %get-tuple-element.178.refs_2_, ...), custom_call_target="tpu_custom_call" | custom-call | flops 858993472 | bytes 2097152 | tf_op jit(solution)/shard_map/weight_grad/pallas_call | solution.py:213
  241.5 30.2 %pre_grads.1 = (bf16[2048,2048]{1,0:T(8,128)(2,1)}, f32[8,2048]{1,0:T(8,128)}, bf16[512,512]{1,0:T(8,128)(2,1)}, bf16[512,512]{1,0:T(8,128)(2,1)}, bf16[512,512]{1,0:T(8,128)(2,1)}, /*index=5*/bf16[4096,512]{1,0:T(8,128)(2,1)}) custom-call(bf16[2,2048,512]{2,1,0:T(8,128)(2,1)} %get-tuple-element.179.refs_0_, ...), custom_call_target="tpu_custom_call" | custom-call | flops 1717986944 | bytes 4194304 | tf_op jit(solution)/shard_map/pre_grads/pallas_call | solution.py:213
  271.6 16.5 %outputs.5 = (bf16[512,2048]{1,0:T(8,128)(2,1)}, bf16[512,512]{1,0:T(8,128)(2,1)}, bf16[512,1536]{1,0:T(8,128)(2,1)}, f32[8,1536]{1,0:T(8,128)}, bf16[512,512]{1,0:T(8,128)(2,1)}) custom-call(f32[8,2048]{1,0:T(8,128)} %get-tuple-element.180.refs_0_, bf16[1536,512]{1,0:T(8,128)(2,1)} %get-tuple-element.153.refs_0_.refs_1_, ...), custom_call_target="tpu_custom_call" | custom-call | flops 536870912 | bytes 1887436 | tf_op jit(solution)/shard_map/outputs/pallas_call | solution.py:213
  288.6 13.1 %attention.6 = (bf16[512,512]{1,0:T(8,128)(2,1)}, bf16[512,512]{1,0:T(8,128)(2,1)}, bf16[512,512]{1,0:T(8,128)(2,1)}, bf16[512,512]{1,0:T(8,128)(2,1)}) custom-call(f32[8,1536]{1,0:T(8,128)} %get-tuple-element.185.refs_0_, bf16[1536,512]{1,0:T(8,128)(2,1)} %get-tuple-element.172.refs_2_.refs_1_.refs_3_, bf16[512,512]{1,0:T(8,128)(2,1)} %get-tuple-element.186.refs_2_, ...), custom_call_target="tpu_custom_call" | custom-call | flops 751619264 | bytes 629145 | tf_op jit(solution)/shard_map/attention/pallas_call | solution.py:213
  301.7 17.8 %weight_grad.9 = (bf16[2,2048,512]{2,1,0:T(8,128)(2,1)}, bf16[512,512]{1,0:T(8,128)(2,1)}, bf16[512,512]{1,0:T(8,128)(2,1)}) custom-call(bf16[512,512]{1,0:T(8,128)(2,1)} %get-tuple-element.189.refs_0_.refs_1_, bf16[512,512]{1,0:T(8,128)(2,1)} %get-tuple-element.190.refs_1_, bf16[512,512]{1,0:T(8,128)(2,1)} %get-tuple-element.191.refs_2_, ...), custom_call_target="tpu_custom_call" | custom-call | flops 858993472 | bytes 2097152 | tf_op jit(solution)/shard_map/weight_grad/pallas_call | solution.py:213
  319.5 16.5 %attention.7 = (bf16[512,512]{1,0:T(8,128)(2,1)}, bf16[512,512]{1,0:T(8,128)(2,1)}, bf16[512,512]{1,0:T(8,128)(2,1)}, bf16[512,512]{1,0:T(8,128)(2,1)}, bf16[512...) custom-call(bf16[2,2048,512]{2,1,0:T(8,128)(2,1)} %get-tuple-element.193.refs_0_.refs_2_.refs_3_.refs_1_, ...), custom_call_target="tpu_custom_call" | custom-call | flops 751619264 | bytes 629145 | tf_op jit(solution)/shard_map/attention/pallas_call | solution.py:213
  336.0 16.4 %outputs.6 = (bf16[512,2048]{1,0:T(8,128)(2,1)}, bf16[512,512]{1,0:T(8,128)(2,1)}, bf16[512,1536]{1,0:T(8,128)(2,1)}, f32[8,1536]{1,0:T(8,128)}, bf16[512,512]{1...) custom-call(bf16[512,512]{1,0:T(8,128)(2,1)} %get-tuple-element.197.refs_0_.refs_1_, ...), custom_call_target="tpu_custom_call" | custom-call | flops 536870912 | bytes 1887436 | tf_op jit(solution)/shard_map/outputs/pallas_call | solution.py:213
  352.4 19.4 %weight_grad.10 = (bf16[2,512,2048]{2,1,0:T(8,128)(2,1)}, bf16[512,512]{1,0:T(8,128)(2,1)}, bf16[512,512]{1,0:T(8,128)(2,1)}) custom-call(f32[8,1536]{1,0:T(8,128)} %get-tuple-element.204.refs_0_, bf16[512,512]{1,0:T(8,128)(2,1)} %get-tuple-element.197.refs_0_.refs_1_, bf16[2,2048,512]{2,1,0:T(8,128)(2,1)} %get-tuple-element.193.refs_0_.refs_2_.refs_3_.refs_1_, ...), custom_call_target="tpu_custom_call" | custom-call | flops 858993472 | bytes 2097152 | tf_op jit(solution)/shard_map/weight_grad/pallas_call | solution.py:213
  371.9 16.5 %outputs.7 = (bf16[512,2048]{1,0:T(8,128)(2,1)}, bf16[512,512]{1,0:T(8,128)(2,1)}, bf16[512,1536]{1,0:T(8,128)(2,1)}, f32[8,1536]{1,0:T(8,128)}, bf16[512,512]{1,0:T(8,128)(2,1)}, /*index=5*/bf16[1024,2048]{1,0:T(8,128)(2,1)}) custom-call(bf16[2,512,2048]{2,1,0:T(8,128)(2,1)} %get-tuple-element.206.refs_0_, ...), custom_call_target="tpu_custom_call" | custom-call | flops 536870912 | bytes 1887436 | tf_op jit(solution)/shard_map/outputs/pallas_call | solution.py:213
  388.4 3.9 add.150.refs_0_.refs_1_.refs_2_.refs_3_
  392.4 18.8 %weight_grad.11 = (bf16[2,512,2048]{2,1,0:T(8,128)(2,1)}, bf16[512,512]{1,0:T(8,128)(2,1)}) custom-call(bf16[2048,512]{1,0:T(8,128)(2,1)} %add.150.refs_0_.refs_1_.refs_2_.refs_3_, bf16[2048,512]{1,0:T(8,128)(2,1)} %add.150.refs_0_.refs_1_.refs_2_.refs_3_, bf16[2048,2048]{1,0:T(8,128)(2,1)} %get-tuple-element.164.refs_5_.refs_3_.refs_2_, ...), custom_call_target="tpu_custom_call" | custom-call | flops 858993472 | bytes 2097152 | tf_op jit(solution)/shard_map/weight_grad/pallas_call | solution.py:213
  411.2 41.8 %backs.5 = (bf16[2048,2048]{1,0:T(8,128)(2,1)}, f32[16,2048]{1,0:T(8,128)}, bf16[512,512]{1,0:T(8,128)(2,1)}, bf16[512,512]{1,0:T(8,128)(2,1)}, bf16[512,512]{1,...) custom-call(bf16[2,512,2048]{2,1,0:T(8,128)(2,1)} %get-tuple-element.217.refs_0_.re, ...), custom_call_target="tpu_custom_call" | custom-call | flops 1717986944 | bytes 4194304 | tf_op jit(solution)/shard_map/backs/pallas_call | solution.py:213
  452.9 13.1 %backs.6 = (bf16[512,2048]{1,0:T(8,128)(2,1)}, f32[16,2048]{1,0:T(8,128)}, bf16[128,2048]{1,0:T(8,128)(2,1)}) custom-call(f32[16,2048]{1,0:T(8,128)} %get-tuple-element.218.refs_0_, bf16[2,512,2048]{2,1,0:T(8,128)(2,1)} %get-tuple-element.217.refs_0_.refs_4_.refs_5_.refs_6_.refs_1_, bf16[512,1536]{1,0:T(8,128)(2,1)} %get-tuple-element.219.refs_2_.refs_3_, ...), custom_call_target="tpu_custom_call" | custom-call | flops 322122560 | bytes 1415577 | tf_op jit(solution)/shard_map/backs/pallas_call | solution.py:213
  466.1 3.9 add.151.refs_0_.refs_1_
  470.0 14.9 %weight_grad.12 = (bf16[2,512,1536]{2,1,0:T(8,128)(2,1)}, bf16[128,2048]{1,0:T(8,128)(2,1)}) custom-call(bf16[512,2048]{1,0:T(8,128)(2,1)} %add.151.refs_0_.refs_1_, bf16[512,2048]{1,0:T(8,128)(2,1)} %add.151.refs_0_.refs_1_, bf16[2048,2048]{1,0:T(8,128)(2,1)} %get-tuple-element.149.refs_1_.refs_4_.refs_2_, ...), custom_call_target="tpu_custom_call" | custom-call | flops 644245120 | bytes 1677721 | tf_op jit(solution)/shard_map/weight_grad/pallas_call | solution.py:213
  485.0 18.0 %weight_grad.13 = (bf16[2,512,512]{2,1,0:T(8,128)(2,1)}, bf16[128,2048]{1,0:T(8,128)(2,1)}, bf16[1024,1536]{1,0:T(8,128)(2,1)}) custom-call(bf16[2,512,1536]{2,1,0:T(8,128)(2,1)} %get-tuple-element.229.refs_0_, bf16[512,2048]{1,0:T(8,128)(2,1)} %add.151.refs_0_.refs_1_, bf16[1024,1536]{1,0:T(8,128)(2,1)} %bitcast.60, bf16[2048,2048]{1,0:T(8,128)(2,1)} %bitcast.48, ...), custom_call_target="tpu_custom_call" | custom-call | flops 214748368 | bytes 838860 | tf_op jit(solution)/shard_map/weight_grad/pallas_call | solution.py:213
  502.9 15.3 %backs.7 = (bf16[512,2048]{1,0:T(8,128)(2,1)}, f32[16,2048]{1,0:T(8,128)}, bf16[128,2048]{1,0:T(8,128)(2,1)}, bf16[1024,512]{1,0:T(8,128)(2,1)}) custom-call(bf16[2,512,512]{2,1,0:T(8,128)(2,1)} %get-tuple-element.234.refs_0_, bf16[512,2048]{1,0:T(8,128)(2,1)} %add.151.refs_0_.refs_1_, bf16[1024,512]{1,0:T(8,128)(2,1)} %bitcast.61, ...), custom_call_target="tpu_custom_call" | custom-call | flops 322122560 | bytes 1415577 | tf_op jit(solution)/shard_map/backs/pallas_call | solution.py:213
  518.3 17.4 %weight_grad.14 = (bf16[2,512,1536]{2,1,0:T(8,128)(2,1)}, bf16[128,2048]{1,0:T(8,128)(2,1)}) custom-call(f32[16,2048]{1,0:T(8,128)} %get-tuple-element.235.refs_0_, bf16[512,2048]{1,0:T(8,128)(2,1)} %add.151.refs_0_.refs_1_, bf16[2048,2048]{1,0:T(8,128)(2,1)} %get-tuple-element.149.refs_1_.refs_4_.refs_2_, ...), custom_call_target="tpu_custom_call" | custom-call | flops 644245120 | bytes 1677721 | tf_op jit(solution)/shard_map/weight_grad/pallas_call | solution.py:213
  535.7 19.4 %backs.8 = (bf16[512,2048]{1,0:T(8,128)(2,1)}, f32[16,2048]{1,0:T(8,128)}, bf16[256,1536]{1,0:T(8,128)(2,1)}) custom-call(bf16[2,512,1536]{2,1,0:T(8,128)(2,1)} %get-tuple-element.237.refs_0_.refs_1_, bf16[2,512,1536]{2,1,0:T(8,128)(2,1)} %get-tuple-element.237.refs_0_.refs_1_, bf16[512,1536]{1,0:T(8,128)(2,1)} %get-tuple-element.227.refs_5_.refs_2_, ...), custom_call_target="tpu_custom_call" | custom-call | flops 322122560 | bytes 1415577 | tf_op jit(solution)/shard_map/backs/pallas_call | solution.py:213
  556.1 21.0 %weight_grad.15 = (bf16[2,512,512]{2,1,0:T(8,128)(2,1)}, bf16[256,1536]{1,0:T(8,128)(2,1)}) custom-call(f32[16,2048]{1,0:T(8,128)} %get-tuple-element.238.refs_0_, bf16[2,512,1536]{2,1,0:T(8,128)(2,1)} %get-tuple-element.237.refs_0_.refs_1_, bf16[2048,2048]{1,0:T(8,128)(2,1)} %bitcast.50, bf16[2048,2048]{1,0:T(8,128)(2,1)} %bitcast.51, ...), custom_call_target="tpu_custom_call" | custom-call | flops 214748368 | bytes 838860 | tf_op jit(solution)/shard_map/weight_grad/pallas_call | solution.py:213
  577.0 3.4 add.152.refs_0_.refs_1_
  580.4 17.8 %backs.9 = (bf16[512,2048]{1,0:T(8,128)(2,1)}, f32[16,2048]{1,0:T(8,128)}, bf16[256,1536]{1,0:T(8,128)(2,1)}, bf16[512,512]{1,0:T(8,128)(2,1)}) custom-call(bf16[512,1536]{1,0:T(8,128)(2,1)} %add.152.refs_0_.refs_1_, bf16[512,1536]{1,0:T(8,128)(2,1)} %add.152.refs_0_.refs_1_, bf16[2,512,512]{2,1,0:T(8,128)(2,1)} %get-tuple-element.240.refs_0_.refs_2_.refs_4_, ...), custom_call_target="tpu_custom_call" | custom-call | flops 322122560 | bytes 1415577 | tf_op jit(solution)/shard_map/backs/pallas_call | solution.py:213
  600.2 9.9 %add.153 = (bf16[512,512]{1,0:T(8,128)(2,1)}, f32[8,1024]{1,0:T(8,128)}, f32[8,1024]{1,0:T(8,128)}, f32[8,1024]{1,0:T(8,128)}) custom-call(f32[16,2048]{1,0:T(8,128)} %get-tuple-element.243.refs_0_, f32[8,1024]{1,0:T(8,128)} %select_n.103.refs_1_.refs_2_.refs_3_, f32[8,1024]{1,0:T(8,128)} %select_n.103.refs_1_.refs_2_.refs_3_, ...), custom_call_target="tpu_custom_call" | custom-call | bytes 157286 | tf_op jit(solution)/shard_map/add/pallas_call | solution.py:213
  611.7 5.5 gate.9
  617.1 5.8 first_half.4
  623.2 5.7 first_half.5
  629.1 0.9 slice.100
  630.1 1.7 collective-permute-start.7
  633.1 4.2 finish.3.refs_0_
  637.2 12.8 %collective-permute-done.7.refs_3_ = bf16[256,1536]{1,0:T(8,128)(2,1)S(1)} collective-permute-done((bf16[256,1536]{1,0:T(8,128)(2,1)}, bf16[256,1536]{1,0:T(8,128)(2,1)S(1)}, u32[]{:S(2)}, u32[]{:S(2)}) %collective-permute-start.7) | collective-permute-done | bytes 786464 | tf_op jit(solution)/shard_map/ppermute | solution.py:107
  650.9 4.5 first_half.6
  655.5 1.8 collective-permute-start.10
  657.9 4.5 gate.11
  662.4 1.3 copy-done.6
  663.7 3.4 second_half.4.refs_0_
  667.1 3.4 second_half.5.refs_0_
  671.3 2.5 first_half.7
  675.3 3.9 finish.4.refs_0_.refs_3_
  679.8 2.9 second_half.6.refs_0_
  683.5 2.0 second_half.7.refs_0_
  685.5 2.3 finish.5
  (158 shorter events, 23.7 us)
Async XLA Ops:
  7.2 625.9 %reduce-scatter.9.cloned.1.call-start = ((), (), s32[]{:S(2)}) async-start(), calls=%async_computation.8 | async-start | bytes 2621440 | tf_op jit(solution)/shard_map/reduce_scatter | solution.py:1049
  13.4 4.7 collective-permute-start
  18.1 0.6 copy-start.26
  21.6 46.7 %collective-permute-start.1 = (bf16[512,2048]{1,0:T(8,128)(2,1)}, bf16[512,2048]{1,0:T(8,128)(2,1)S(1)}, u32[]{:S(2)}, u32[]{:S(2)}) collective-permute-start(bf16[512,2048]{1,0:T(8,128)(2,1)} %pick.2.refs_0_), channel_id=1, source_target_pairs={{0,1},{1,0},{2,3},{3,2},{4,5},{5,4},{6,7},{7,6},{8,9},{9,8},{10,11... | collective-permute-start | bytes 6291464 | tf_op jit(solution)/shard_map/ppermute | solution.py:107
  24.5 0.6 copy-start.18
  24.5 19.4 %copy-start.25 = (f32[2048]{0:T(1024)}, f32[2048]{0:T(1024)S(1)}, u32[]{:S(2)}) copy-start(f32[2048]{0:T(1024)S(1)} %pad_maximum_fusion.3) | copy-start | bytes 24580
  68.4 1.3 copy-start
  69.7 1.7 copy-start.34
  69.7 4.4 collective-permute-start.2
  69.7 65.0 %collective-permute-start.3 = (bf16[512,2048]{1,0:T(8,128)(2,1)}, bf16[512,2048]{1,0:T(8,128)(2,1)}, u32[]{:S(2)}, u32[]{:S(2)}) collective-permute-start(bf16[512,2048]{1,0:T(8,128)(2,1)} %get-tuple-element.161), channel_id=1, source_target_pairs={{0,1},{1,0},{2,3},{3,2},{4,5},{5,4},{6,7},{7,6},{8,9},{9,8},{10,11... | collective-permute-start | bytes 6291464 | tf_op jit(solution)/shard_map/ppermute | solution.py:107
  74.0 1.3 copy-start.1
  134.7 1.9 copy-start.33
  134.7 4.6 collective-permute-start.4
  134.8 48.3 %collective-permute-start.5 = (bf16[2048,512]{1,0:T(8,128)(2,1)}, bf16[2048,512]{1,0:T(8,128)(2,1)S(1)}, u32[]{:S(2)}, u32[]{:S(2)}) collective-permute-start(bf16[2048,512]{1,0:T(8,128)(2,1)} %get-tuple-element.148.refs_0_), channel_id=1, source_target_pairs={{0,1},{1,0},{2,3},{3,2},{4,5},{5,4},{6,7},{7,6},{8,9},{9,8},{10,11... | collective-permute-start | bytes 6291464 | tf_op jit(solution)/shard_map/ppermute | solution.py:107
  183.1 1.3 copy-start.2
  184.4 4.4 collective-permute-start.6
  188.8 1.3 copy-start.4
  206.8 426.2 %reduce-scatter.11.cloned.1.call-start = ((), (), s32[]{:S(2)}) async-start(), calls=%async_computation.9 | async-start | bytes 2621440 | tf_op jit(solution)/shard_map/reduce_scatter | solution.py:1049
  288.1 344.9 %reduce-scatter.13.cloned.1.call-start = ((), (), s32[]{:S(2)}) async-start(), calls=%async_computation.10 | async-start | bytes 2621440 | tf_op jit(solution)/shard_map/reduce_scatter | solution.py:1049
  352.4 280.7 %reduce-scatter.15.cloned.1.call-start = ((), (), s32[]{:S(2)}) async-start(), calls=%async_computation.11 | async-start | bytes 2621440 | tf_op jit(solution)/shard_map/reduce_scatter | solution.py:1049
  388.4 286.8 %reduce-scatter.17.cloned.1.call-start = ((), (), s32[]{:S(2)}) async-start(), calls=%async_computation.12 | async-start | bytes 2621440 | tf_op jit(solution)/shard_map/reduce_scatter | solution.py:1054
  466.0 209.2 %reduce-scatter.19.cloned.1.call-start = ((), (), s32[]{:S(2)}) async-start(), calls=%async_computation.13 | async-start | bytes 2621440 | tf_op jit(solution)/shard_map/reduce_scatter | solution.py:1054
  518.2 157.0 %reduce-scatter.21.cloned.1.call-start = ((), (), s32[]{:S(2)}) async-start(), calls=%async_computation.14 | async-start | bytes 2621440 | tf_op jit(solution)/shard_map/reduce_scatter | solution.py:1054
  555.2 0.8 copy-start.19
  555.2 0.9 copy-start.20
  555.2 130.3 %reduce-scatter.23.cloned.1.call-start = ((), (), s32[]{:S(2)}) async-start(), calls=%async_computation.15 | async-start | bytes 2621440 | tf_op jit(solution)/shard_map/reduce_scatter | solution.py:1054
  598.3 0.9 copy-start.10
  598.3 1.0 copy-start.11
  598.3 1.0 copy-start.12
  598.3 1.1 copy-start.15
  598.3 1.1 copy-start.13
  598.4 12.6 %copy-start.21 = (f32[8,1536]{1,0:T(8,128)S(1)}, f32[8,1536]{1,0:T(8,128)}, u32[]{:S(2)}) copy-start(f32[8,1536]{1,0:T(8,128)} %get-tuple-element.171.refs_0_) | copy-start | bytes 147460
  598.4 12.6 %copy-start.22 = (f32[8,1536]{1,0:T(8,128)S(1)}, f32[8,1536]{1,0:T(8,128)}, u32[]{:S(2)}) copy-start(f32[8,1536]{1,0:T(8,128)} %get-tuple-element.185.refs_0_) | copy-start | bytes 147460
  598.4 12.6 %copy-start.23 = (f32[8,1536]{1,0:T(8,128)S(1)}, f32[8,1536]{1,0:T(8,128)}, u32[]{:S(2)}) copy-start(f32[8,1536]{1,0:T(8,128)} %get-tuple-element.204.refs_0_) | copy-start | bytes 147460
  598.4 12.6 %copy-start.24 = (f32[8,1536]{1,0:T(8,128)S(1)}, f32[8,1536]{1,0:T(8,128)}, u32[]{:S(2)}) copy-start(f32[8,1536]{1,0:T(8,128)} %get-tuple-element.211.refs_0_) | copy-start | bytes 147460
  599.5 12.2 %copy-start.5 = (f32[16,2048]{1,0:T(8,128)}, f32[16,2048]{1,0:T(8,128)S(1)}, u32[]{:S(2)}) copy-start(f32[16,2048]{1,0:T(8,128)S(1)} %add_add_fusion.refs_4_) | copy-start | bytes 393220
  622.9 39.5 %collective-permute-start.8 = (bf16[2048,512]{1,0:T(8,128)(2,1)}, bf16[2048,512]{1,0:T(8,128)(2,1)S(1)}, u32[]{:S(2)}, u32[]{:S(2)}) collective-permute-start(bf16[2048,512]{1,0:T(8,128)(2,1)} %get-tuple-element.254.refs_0_), channel_id=1, source_target_pairs={{0,8},{8,0},{16,24},{24,16},{1,9},{9,1},{17,25},{25,17},{2,10},{10... | collective-permute-start | bytes 6291464 | tf_op jit(solution)/shard_map/ppermute | solution.py:107
  623.2 5.9 copy-start.3
  623.2 8.5 %copy-start.35 = (bf16[1024]{0:T(1024)(128)(2,1)S(1)}, bf16[1024]{0:T(1024)(128)(2,1)}, u32[]{:S(2)}) copy-start(bf16[1024]{0:T(1024)(128)(2,1)} %param.24) | copy-start | bytes 6148
  623.2 8.5 %copy-start.36 = (bf16[1024]{0:T(1024)(128)(2,1)S(1)}, bf16[1024]{0:T(1024)(128)(2,1)}, u32[]{:S(2)}) copy-start(bf16[1024]{0:T(1024)(128)(2,1)} %param.28) | copy-start | bytes 6148
  628.9 38.2 %collective-permute-start.9 = (bf16[512,2048]{1,0:T(8,128)(2,1)}, bf16[512,2048]{1,0:T(8,128)(2,1)}, u32[]{:S(2)}, u32[]{:S(2)}) collective-permute-start(bf16[512,2048]{1,0:T(8,128)(2,1)} %get-tuple-element.259.refs_0_), channel_id=1, source_target_pairs={{0,8},{8,0},{16,24},{24,16},{1,9},{9,1},{17,25},{25,17},{2,10},{10... | collective-permute-start | bytes 6291464 | tf_op jit(solution)/shard_map/ppermute | solution.py:107
  630.1 20.0 %collective-permute-start.7 = (bf16[256,1536]{1,0:T(8,128)(2,1)}, bf16[256,1536]{1,0:T(8,128)(2,1)S(1)}, u32[]{:S(2)}, u32[]{:S(2)}) collective-permute-start(bf16[256,1536]{1,0:T(8,128)(2,1)} %slice.100), channel_id=1, source_target_pairs={{0,16},{8,24},{16,0},{24,8},{1,17},{9,25},{17,1},{25,9},{2,18},{10... | collective-permute-start | bytes 2359304 | tf_op jit(solution)/shard_map/ppermute | solution.py:107
  650.0 0.9 copy-start.9
  650.9 4.6 copy-start.7
  650.9 6.3 copy-start.8
  650.9 6.3 copy-start.27
  650.9 6.3 copy-start.28
  650.9 6.3 copy-start.29
  650.9 6.3 copy-start.32
  655.5 24.3 %collective-permute-start.11 = (bf16[512,1536]{1,0:T(8,128)(2,1)}, bf16[512,1536]{1,0:T(8,128)(2,1)}, u32[]{:S(2)}, u32[]{:S(2)}) collective-permute-start(bf16[512,1536]{1,0:T(8,128)(2,1)} %get-tuple-element.265.refs_0_), channel_id=1, source_target_pairs={{0,8},{8,0},{16,24},{24,16},{1,9},{9,1},{17,25},{25,17},{2,10},{10... | collective-permute-start | bytes 4718600 | tf_op jit(solution)/shard_map/ppermute | solution.py:107
  655.5 15.0 %collective-permute-start.10 = (bf16[512,512]{1,0:T(8,128)(2,1)S(1)}, bf16[512,512]{1,0:T(8,128)(2,1)S(1)}, u32[]{:S(2)}, u32[]{:S(2)}) collective-permute-start(bf16[512,512]{1,0:T(8,128)(2,1)S(1)} %copy-done.7), channel_id=1, source_target_pairs={{0,16},{8,24},{16,0},{24,8},{1,17},{9,25},{17,1},{25,9},{2,18},{10... | collective-permute-start | bytes 1572872 | tf_op jit(solution)/shard_map/ppermute | solution.py:107
  662.4 1.3 copy-start.6
  670.5 3.3 copy-start.17
  670.5 3.3 copy-start.30
  670.5 0.8 copy-start.14
  673.7 8.9 %collective-permute-start.12 = (bf16[512,512]{1,0:T(8,128)(2,1)}, bf16[512,512]{1,0:T(8,128)(2,1)S(1)}, u32[]{:S(2)}, u32[]{:S(2)}) collective-permute-start(bf16[512,512]{1,0:T(8,128)(2,1)} %get-tuple-element.272.refs_0_), channel_id=1, source_target_pairs={{0,8},{8,0},{16,24},{24,16},{1,9},{9,1},{17,25},{25,17},{2,10},{10... | collective-permute-start | bytes 1572872 | tf_op jit(solution)/shard_map/ppermute | solution.py:107
  675.2 12.6 %copy-start.31 = (f32[1024]{0:T(1024)}, f32[1024]{0:T(1024)S(1)}, u32[]{:S(2)}) copy-start(f32[1024]{0:T(1024)S(1)} %get-tuple-element.342) | copy-start | bytes 12292
  682.7 0.8 copy-start.16
Sparse Core Ops, SparseCore 0:
  207.0 44.9 reduce-scatter.8
  288.2 44.4 reduce-scatter.10
  352.5 44.0 reduce-scatter.12
  398.8 43.2 reduce-scatter.14
  466.2 44.1 reduce-scatter.16
  518.4 44.1 reduce-scatter.18
  564.8 45.1 reduce-scatter.20
  612.4 43.3 reduce-scatter.22

commit v4 on v3

--- a/solution.py
+++ b/solution.py
@@ -943,7 +943,7 @@
 
     small = (ln1_gain, ln1_bias, ln2_gain, ln2_bias, dense_bias, out_bias, qkv_bias, up_bias)
     small_got = swap(jnp.concatenate(small, 0), "dp", 1)
-    line = Line(small_got)
+    line = Line(qkv_bias)
     joint_half = swap(pick(line, w, qkv_weight, dense_weight, True)[0], "dp", 1)
     own, other = [], []
     place = 0
@@ -1268,17 +1268,17 @@
     sibling_swap("down")
     mine_done("up")
     sibling_swap("up")
-    finish_out(0, micros)
     mine_done("qkv")
     sibling_swap("qkv")
     rest_over_x("dense")
+    finish_out(0, micros)
     spreads = spread(vector, "dp")
     one_sums = gate(line, w, one_sums)
     vector = summed(spreads, size)
     all_done("down")
-    all_done("up")
     mine_done("dense")
     sibling_swap("dense")
+    all_done("up")
     finish_back(0, micros - 1)
     all_done("qkv")
     all_done("dense")

time: 704 us -> 718 us (1.020)
  waiting for transfers between devices: 45.3 us -> 69.3 us
    ppermute x13, waiting for transfers between devices: 45.1 us -> 69.1 us  [swap(): lax.ppermute(block, axis, [(i, i ^ distance) for i in range(lax.axis_size...]
    unnamed x79 -> x93, local copies, waits for them, and re-layouts: 14.9 us -> 12.4 us
  transfers between devices with their start and end apart: 21 -> 21, of which waited for: 7 -> 6; matrix products, arithmetic and copies ran while one was open for 2% -> 1% of each run, Pallas kernels for 82% -> 80%
where the time goes in v4:
time: 718 us; the launch traced here: 710 us
  Pallas kernels  592 us (82%)
  waiting for transfers between devices  69.3 us (10%)
  local copies, waits for them, and re-layouts  16.9 us (2%)
  between operations  15.4 us (2%)
  starting transfers between devices  11.1 us (2%)
    pallas_call x49, Pallas kernels, call(): pl.pallas_call(body, grid=grid, in_specs=[anywhere] * skip + [anywhere if...  592 us
    ppermute x13, waiting for transfers between devices, swap(): lax.ppermute(block, axis, [(i, i ^ distance) for i in range(lax.axis_size...  69.1 us
  transfers between devices with their start and end apart: 21, of which 6 were waited for; matrix products, arithmetic and copies ran while one was open for 1% of the time, Pallas kernels for 80%

profile of v4, /device:TPU:0, one launch (start us, length us, event | category | flops | bytes accessed | tf_op | source)
XLA Modules:
  0.0 709.9 jit_solution(6514059968460544686)
XLA Ops:
  7.3 3.0 pick.2.refs_0_
  10.3 3.0 collective-permute-start.1
  13.9 45.6 %collective-permute-done = bf16[7936]{0:T(1024)(128)(2,1)S(1)} collective-permute-done((bf16[7936]{0:T(1024)(128)(2,1)S(1)}, bf16[7936]{0:T(1024)(128)(2,1)S(1)}, u32[]{:S(2)}, u32[]{:S(2)}) %collective-permute-start) | collective-permute-done | bytes 15904 | tf_op jit(solution)/shard_map/ppermute | solution.py:107
  60.9 18.1 %norms.1 = (bf16[2048,2048]{1,0:T(8,128)(2,1)}, bf16[2048,2048]{1,0:T(8,128)(2,1)}, f32[8,2048]{1,0:T(8,128)}) custom-call(bf16[512,2048]{1,0:T(8,128)(2,1)} %pick.2.refs_0_, bf16[2048,2048]{1,0:T(8,128)(2,1)} %bitcast.52, bf16[2048,2048]{1,0:T(8,128)(2,1)} %bitcast.31, f32[4,2048]{1,0:T(4,128)} %pad_maximum_fusion.refs_3_), custom_call_target="tpu_custom_call" | custom-call | flops 12582912 | bytes 3355443 | tf_op jit(solution)/shard_map/norms/pallas_call | solution.py:213
  79.0 4.4 pick.3
  83.4 1.3 copy-done
  84.7 1.7 collective-permute-start.3
  87.1 2.0 collective-permute-done.2.refs_4_.refs_14_.refs_7_.refs_17_.refs_9_.refs_8_.refs_10_.refs_5_.refs_6_
  89.1 1.3 copy-done.1
  90.4 10.6 %projections.2 = (bf16[512,512]{1,0:T(8,128)(2,1)}, bf16[512,512]{1,0:T(8,128)(2,1)}, bf16[512,512]{1,0:T(8,128)(2,1)}, bf16[512,512]{1,0:T(8,128)(2,1)}) custom-call(bf16[512,2048]{1,0:T(8,128)(2,1)} %gate.6.refs_0_.refs_3_.refs_13_.refs_6_.refs_16_.refs_8_.refs_7_.refs_9_.refs_4_.refs_5_, bf16[2048,2048]{1,0:T(8,128)(2,1)} %get-tuple-element.149.refs_1_.refs_4_.refs_2_, ...), custom_call_target="tpu_custom_call" | custom-call | flops 429496736 | bytes 1468006 | tf_op jit(solution)/shard_map/projections/pallas_call | solution.py:213
  101.1 32.2 %projections.3 = (bf16[1536,512]{1,0:T(8,128)(2,1)}, bf16[1536,512]{1,0:T(8,128)(2,1)}, bf16[1536,512]{1,0:T(8,128)(2,1)}, bf16[1536,512]{1,0:T(8,128)(2,1)}, bf...) custom-call(bf16[512,512]{1,0:T(8,128)(2,1)} %get-tuple-element.150.refs_0_.refs_3_, ...), custom_call_target="tpu_custom_call" | custom-call | flops 1288490240 | bytes 2726297 | tf_op jit(solution)/shard_map/projections/pallas_call | solution.py:213
  133.3 16.2 %attention.4 = (bf16[512,512]{1,0:T(8,128)(2,1)}, bf16[512,512]{1,0:T(8,128)(2,1)}, bf16[512,512]{1,0:T(8,128)(2,1)}, bf16[512,512]{1,0:T(8,128)(2,1)}, bf16[512...) custom-call(bf16[1536,512]{1,0:T(8,128)(2,1)} %get-tuple-element.153.refs_0_.refs_1_, ...), custom_call_target="tpu_custom_call" | custom-call | flops 751619264 | bytes 629145 | tf_op jit(solution)/shard_map/attention/pallas_call | solution.py:213
  149.6 1.8 collective-permute-start.5
  151.9 2.1 collective-permute-done.4.refs_8_.refs_10_
  154.1 41.3 %feed_up.1 = (bf16[2048,2048]{1,0:T(8,128)(2,1)}, bf16[2048,2048]{1,0:T(8,128)(2,1)}, bf16[512,512]{1,0:T(8,128)(2,1)}, bf16[512,512]{1,0:T(8,128)(2,1)}, bf16[5...) custom-call(bf16[512,2048]{1,0:T(8,128)(2,1)} %gate.7.refs_0_.refs_7_.refs_9_, ...), custom_call_target="tpu_custom_call" | custom-call | flops 1717986944 | bytes 4194304 | tf_op jit(solution)/shard_map/feed_up/pallas_call | solution.py:213
  195.4 2.4 collective-permute-done.5.refs_1_
  197.8 1.3 copy-done.2
  199.2 4.4 collective-permute-done.6.refs_6_.refs_11_.refs_5_.refs_7_
  203.5 1.3 copy-done.4
  204.8 16.7 %outputs.4 = (bf16[512,2048]{1,0:T(8,128)(2,1)}, bf16[512,512]{1,0:T(8,128)(2,1)}, bf16[512,1536]{1,0:T(8,128)(2,1)}, f32[8,1536]{1,0:T(8,128)}, bf16[512,512]{1,0:T(8,128)(2,1)}, /*index=5*/bf16[512,512]{1,0:T(8,128)(2,1)}) custom-call(bf16[2048,512]{1,0:T(8,128)(2,1)} %gate.8.refs_0_.refs_5_.refs_10_.refs_4_.refs_6_, ...), custom_call_target="tpu_custom_call" | custom-call | flops 536870912 | bytes 1887436 | tf_op jit(solution)/shard_map/outputs/pallas_call | solution.py:213
  221.8 16.0 %attention.5 = (bf16[512,512]{1,0:T(8,128)(2,1)}, bf16[512,512]{1,0:T(8,128)(2,1)}, bf16[512,512]{1,0:T(8,128)(2,1)}, bf16[512,512]{1,0:T(8,128)(2,1)}, bf16[512,512]{1,0:T(8,128)(2,1)}) custom-call(f32[8,1536]{1,0:T(8,128)} %get-tuple-element.171.refs_0_, bf16[1536,512]{1,0:T(8,128)(2,1)} %get-tuple-element.153.refs_0_.refs_1_, ...), custom_call_target="tpu_custom_call" | custom-call | flops 751619264 | bytes 629145 | tf_op jit(solution)/shard_map/attention/pallas_call | solution.py:213
  237.8 18.3 %weight_grad.8 = (bf16[2,2048,512]{2,1,0:T(8,128)(2,1)}, bf16[512,512]{1,0:T(8,128)(2,1)}, bf16[512,512]{1,0:T(8,128)(2,1)}) custom-call(bf16[512,512]{1,0:T(8,128)(2,1)} %get-tuple-element.176.refs_0_.refs_1_, bf16[512,512]{1,0:T(8,128)(2,1)} %get-tuple-element.177.refs_1_, bf16[512,512]{1,0:T(8,128)(2,1)} %get-tuple-element.178.refs_2_, ...), custom_call_target="tpu_custom_call" | custom-call | flops 858993472 | bytes 2097152 | tf_op jit(solution)/shard_map/weight_grad/pallas_call | solution.py:213
  256.0 30.2 %pre_grads.1 = (bf16[2048,2048]{1,0:T(8,128)(2,1)}, f32[8,2048]{1,0:T(8,128)}, bf16[512,512]{1,0:T(8,128)(2,1)}, bf16[512,512]{1,0:T(8,128)(2,1)}, bf16[512,512]{1,0:T(8,128)(2,1)}, /*index=5*/bf16[4096,512]{1,0:T(8,128)(2,1)}) custom-call(bf16[2,2048,512]{2,1,0:T(8,128)(2,1)} %get-tuple-element.179.refs_0_, ...), custom_call_target="tpu_custom_call" | custom-call | flops 1717986944 | bytes 4194304 | tf_op jit(solution)/shard_map/pre_grads/pallas_call | solution.py:213
  286.2 16.4 %outputs.5 = (bf16[512,2048]{1,0:T(8,128)(2,1)}, bf16[512,512]{1,0:T(8,128)(2,1)}, bf16[512,1536]{1,0:T(8,128)(2,1)}, f32[8,1536]{1,0:T(8,128)}, bf16[512,512]{1,0:T(8,128)(2,1)}) custom-call(f32[8,2048]{1,0:T(8,128)} %get-tuple-element.180.refs_0_, bf16[1536,512]{1,0:T(8,128)(2,1)} %get-tuple-element.153.refs_0_.refs_1_, ...), custom_call_target="tpu_custom_call" | custom-call | flops 536870912 | bytes 1887436 | tf_op jit(solution)/shard_map/outputs/pallas_call | solution.py:213
  303.2 13.1 %attention.6 = (bf16[512,512]{1,0:T(8,128)(2,1)}, bf16[512,512]{1,0:T(8,128)(2,1)}, bf16[512,512]{1,0:T(8,128)(2,1)}, bf16[512,512]{1,0:T(8,128)(2,1)}) custom-call(f32[8,1536]{1,0:T(8,128)} %get-tuple-element.185.refs_0_, bf16[1536,512]{1,0:T(8,128)(2,1)} %get-tuple-element.172.refs_2_.refs_1_.refs_3_, bf16[512,512]{1,0:T(8,128)(2,1)} %get-tuple-element.186.refs_2_, ...), custom_call_target="tpu_custom_call" | custom-call | flops 751619264 | bytes 629145 | tf_op jit(solution)/shard_map/attention/pallas_call | solution.py:213
  316.2 17.8 %weight_grad.9 = (bf16[2,2048,512]{2,1,0:T(8,128)(2,1)}, bf16[512,512]{1,0:T(8,128)(2,1)}, bf16[512,512]{1,0:T(8,128)(2,1)}) custom-call(bf16[512,512]{1,0:T(8,128)(2,1)} %get-tuple-element.189.refs_0_.refs_1_, bf16[512,512]{1,0:T(8,128)(2,1)} %get-tuple-element.190.refs_1_, bf16[512,512]{1,0:T(8,128)(2,1)} %get-tuple-element.191.refs_2_, ...), custom_call_target="tpu_custom_call" | custom-call | flops 858993472 | bytes 2097152 | tf_op jit(solution)/shard_map/weight_grad/pallas_call | solution.py:213
  334.0 16.5 %attention.7 = (bf16[512,512]{1,0:T(8,128)(2,1)}, bf16[512,512]{1,0:T(8,128)(2,1)}, bf16[512,512]{1,0:T(8,128)(2,1)}, bf16[512,512]{1,0:T(8,128)(2,1)}, bf16[512...) custom-call(bf16[2,2048,512]{2,1,0:T(8,128)(2,1)} %get-tuple-element.193.refs_0_.refs_2_.refs_3_.refs_1_, ...), custom_call_target="tpu_custom_call" | custom-call | flops 751619264 | bytes 629145 | tf_op jit(solution)/shard_map/attention/pallas_call | solution.py:213
  350.5 16.4 %outputs.6 = (bf16[512,2048]{1,0:T(8,128)(2,1)}, bf16[512,512]{1,0:T(8,128)(2,1)}, bf16[512,1536]{1,0:T(8,128)(2,1)}, f32[8,1536]{1,0:T(8,128)}, bf16[512,512]{1...) custom-call(bf16[512,512]{1,0:T(8,128)(2,1)} %get-tuple-element.197.refs_0_.refs_1_, ...), custom_call_target="tpu_custom_call" | custom-call | flops 536870912 | bytes 1887436 | tf_op jit(solution)/shard_map/outputs/pallas_call | solution.py:213
  367.0 19.4 %weight_grad.10 = (bf16[2,512,2048]{2,1,0:T(8,128)(2,1)}, bf16[512,512]{1,0:T(8,128)(2,1)}, bf16[512,512]{1,0:T(8,128)(2,1)}) custom-call(f32[8,1536]{1,0:T(8,128)} %get-tuple-element.204.refs_0_, bf16[512,512]{1,0:T(8,128)(2,1)} %get-tuple-element.197.refs_0_.refs_1_, bf16[2,2048,512]{2,1,0:T(8,128)(2,1)} %get-tuple-element.193.refs_0_.refs_2_.refs_3_.refs_1_, ...), custom_call_target="tpu_custom_call" | custom-call | flops 858993472 | bytes 2097152 | tf_op jit(solution)/shard_map/weight_grad/pallas_call | solution.py:213
  386.4 16.5 %outputs.7 = (bf16[512,2048]{1,0:T(8,128)(2,1)}, bf16[512,512]{1,0:T(8,128)(2,1)}, bf16[512,1536]{1,0:T(8,128)(2,1)}, f32[8,1536]{1,0:T(8,128)}, bf16[512,512]{1,0:T(8,128)(2,1)}, /*index=5*/bf16[1024,2048]{1,0:T(8,128)(2,1)}) custom-call(bf16[2,512,2048]{2,1,0:T(8,128)(2,1)} %get-tuple-element.206.refs_0_, ...), custom_call_target="tpu_custom_call" | custom-call | flops 536870912 | bytes 1887436 | tf_op jit(solution)/shard_map/outputs/pallas_call | solution.py:213
  403.0 3.9 add.150.refs_0_.refs_1_.refs_2_.refs_3_
  406.9 18.8 %weight_grad.11 = (bf16[2,512,2048]{2,1,0:T(8,128)(2,1)}, bf16[512,512]{1,0:T(8,128)(2,1)}) custom-call(bf16[2048,512]{1,0:T(8,128)(2,1)} %add.150.refs_0_.refs_1_.refs_2_.refs_3_, bf16[2048,512]{1,0:T(8,128)(2,1)} %add.150.refs_0_.refs_1_.refs_2_.refs_3_, bf16[2048,2048]{1,0:T(8,128)(2,1)} %get-tuple-element.164.refs_5_.refs_3_.refs_2_, ...), custom_call_target="tpu_custom_call" | custom-call | flops 858993472 | bytes 2097152 | tf_op jit(solution)/shard_map/weight_grad/pallas_call | solution.py:213
  425.8 41.8 %backs.5 = (bf16[2048,2048]{1,0:T(8,128)(2,1)}, f32[16,2048]{1,0:T(8,128)}, bf16[512,512]{1,0:T(8,128)(2,1)}, bf16[512,512]{1,0:T(8,128)(2,1)}, bf16[512,512]{1,...) custom-call(bf16[2,512,2048]{2,1,0:T(8,128)(2,1)} %get-tuple-element.217.refs_0_.re, ...), custom_call_target="tpu_custom_call" | custom-call | flops 1717986944 | bytes 4194304 | tf_op jit(solution)/shard_map/backs/pallas_call | solution.py:213
  467.6 13.1 %backs.6 = (bf16[512,2048]{1,0:T(8,128)(2,1)}, f32[16,2048]{1,0:T(8,128)}, bf16[128,2048]{1,0:T(8,128)(2,1)}) custom-call(f32[16,2048]{1,0:T(8,128)} %get-tuple-element.218.refs_0_, bf16[2,512,2048]{2,1,0:T(8,128)(2,1)} %get-tuple-element.217.refs_0_.refs_4_.refs_5_.refs_6_.refs_1_, bf16[512,1536]{1,0:T(8,128)(2,1)} %get-tuple-element.219.refs_2_.refs_3_, ...), custom_call_target="tpu_custom_call" | custom-call | flops 322122560 | bytes 1415577 | tf_op jit(solution)/shard_map/backs/pallas_call | solution.py:213
  480.8 3.9 add.151.refs_0_.refs_1_
  484.7 14.9 %weight_grad.12 = (bf16[2,512,1536]{2,1,0:T(8,128)(2,1)}, bf16[128,2048]{1,0:T(8,128)(2,1)}) custom-call(bf16[512,2048]{1,0:T(8,128)(2,1)} %add.151.refs_0_.refs_1_, bf16[512,2048]{1,0:T(8,128)(2,1)} %add.151.refs_0_.refs_1_, bf16[2048,2048]{1,0:T(8,128)(2,1)} %get-tuple-element.149.refs_1_.refs_4_.refs_2_, ...), custom_call_target="tpu_custom_call" | custom-call | flops 644245120 | bytes 1677721 | tf_op jit(solution)/shard_map/weight_grad/pallas_call | solution.py:213
  499.7 18.0 %weight_grad.13 = (bf16[2,512,512]{2,1,0:T(8,128)(2,1)}, bf16[128,2048]{1,0:T(8,128)(2,1)}, bf16[1024,1536]{1,0:T(8,128)(2,1)}) custom-call(bf16[2,512,1536]{2,1,0:T(8,128)(2,1)} %get-tuple-element.229.refs_0_, bf16[512,2048]{1,0:T(8,128)(2,1)} %add.151.refs_0_.refs_1_, bf16[1024,1536]{1,0:T(8,128)(2,1)} %bitcast.60, bf16[2048,2048]{1,0:T(8,128)(2,1)} %bitcast.48, ...), custom_call_target="tpu_custom_call" | custom-call | flops 214748368 | bytes 838860 | tf_op jit(solution)/shard_map/weight_grad/pallas_call | solution.py:213
  517.6 15.2 %backs.7 = (bf16[512,2048]{1,0:T(8,128)(2,1)}, f32[16,2048]{1,0:T(8,128)}, bf16[128,2048]{1,0:T(8,128)(2,1)}, bf16[1024,512]{1,0:T(8,128)(2,1)}) custom-call(bf16[2,512,512]{2,1,0:T(8,128)(2,1)} %get-tuple-element.234.refs_0_, bf16[512,2048]{1,0:T(8,128)(2,1)} %add.151.refs_0_.refs_1_, bf16[1024,512]{1,0:T(8,128)(2,1)} %bitcast.61, ...), custom_call_target="tpu_custom_call" | custom-call | flops 322122560 | bytes 1415577 | tf_op jit(solution)/shard_map/backs/pallas_call | solution.py:213
  532.9 17.4 %weight_grad.14 = (bf16[2,512,1536]{2,1,0:T(8,128)(2,1)}, bf16[128,2048]{1,0:T(8,128)(2,1)}) custom-call(f32[16,2048]{1,0:T(8,128)} %get-tuple-element.235.refs_0_, bf16[512,2048]{1,0:T(8,128)(2,1)} %add.151.refs_0_.refs_1_, bf16[2048,2048]{1,0:T(8,128)(2,1)} %get-tuple-element.149.refs_1_.refs_4_.refs_2_, ...), custom_call_target="tpu_custom_call" | custom-call | flops 644245120 | bytes 1677721 | tf_op jit(solution)/shard_map/weight_grad/pallas_call | solution.py:213
  550.4 19.4 %backs.8 = (bf16[512,2048]{1,0:T(8,128)(2,1)}, f32[16,2048]{1,0:T(8,128)}, bf16[256,1536]{1,0:T(8,128)(2,1)}) custom-call(bf16[2,512,1536]{2,1,0:T(8,128)(2,1)} %get-tuple-element.237.refs_0_.refs_1_, bf16[2,512,1536]{2,1,0:T(8,128)(2,1)} %get-tuple-element.237.refs_0_.refs_1_, bf16[512,1536]{1,0:T(8,128)(2,1)} %get-tuple-element.227.refs_5_.refs_2_, ...), custom_call_target="tpu_custom_call" | custom-call | flops 322122560 | bytes 1415577 | tf_op jit(solution)/shard_map/backs/pallas_call | solution.py:213
  570.7 21.0 %weight_grad.15 = (bf16[2,512,512]{2,1,0:T(8,128)(2,1)}, bf16[256,1536]{1,0:T(8,128)(2,1)}) custom-call(f32[16,2048]{1,0:T(8,128)} %get-tuple-element.238.refs_0_, bf16[2,512,1536]{2,1,0:T(8,128)(2,1)} %get-tuple-element.237.refs_0_.refs_1_, bf16[2048,2048]{1,0:T(8,128)(2,1)} %bitcast.50, bf16[2048,2048]{1,0:T(8,128)(2,1)} %bitcast.51, ...), custom_call_target="tpu_custom_call" | custom-call | flops 214748368 | bytes 838860 | tf_op jit(solution)/shard_map/weight_grad/pallas_call | solution.py:213
  591.7 3.4 add.152.refs_0_.refs_1_
  595.1 17.9 %backs.9 = (bf16[512,2048]{1,0:T(8,128)(2,1)}, f32[16,2048]{1,0:T(8,128)}, bf16[256,1536]{1,0:T(8,128)(2,1)}, bf16[512,512]{1,0:T(8,128)(2,1)}) custom-call(bf16[512,1536]{1,0:T(8,128)(2,1)} %add.152.refs_0_.refs_1_, bf16[512,1536]{1,0:T(8,128)(2,1)} %add.152.refs_0_.refs_1_, bf16[2,512,512]{2,1,0:T(8,128)(2,1)} %get-tuple-element.240.refs_0_.refs_2_.refs_4_, ...), custom_call_target="tpu_custom_call" | custom-call | flops 322122560 | bytes 1415577 | tf_op jit(solution)/shard_map/backs/pallas_call | solution.py:213
  614.8 9.9 %add.153 = (bf16[512,512]{1,0:T(8,128)(2,1)}, f32[8,1024]{1,0:T(8,128)}, f32[8,1024]{1,0:T(8,128)}, f32[8,1024]{1,0:T(8,128)}) custom-call(f32[16,2048]{1,0:T(8,128)} %get-tuple-element.243.refs_0_, f32[8,1024]{1,0:T(8,128)} %select_n.103.refs_1_.refs_2_.refs_3_, f32[8,1024]{1,0:T(8,128)} %select_n.103.refs_1_.refs_2_.refs_3_, ...), custom_call_target="tpu_custom_call" | custom-call | bytes 157286 | tf_op jit(solution)/shard_map/add/pallas_call | solution.py:213
  624.8 0.8 add_bitcast_fusion
  626.4 5.5 gate.9
  631.9 5.8 first_half.4
  638.0 0.9 slice.98
  638.9 1.7 collective-permute-start.7
  640.6 5.6 first_half.5
  646.2 12.7 %collective-permute-done.7.refs_3_ = bf16[256,1536]{1,0:T(8,128)(2,1)S(1)} collective-permute-done((bf16[256,1536]{1,0:T(8,128)(2,1)}, bf16[256,1536]{1,0:T(8,128)(2,1)S(1)}, u32[]{:S(2)}, u32[]{:S(2)}) %collective-permute-start.7) | collective-permute-done | bytes 786464 | tf_op jit(solution)/shard_map/ppermute | solution.py:107
  658.8 0.9 copy-done.9
  659.8 4.5 first_half.6
  665.0 1.7 collective-permute-start.9
  668.0 4.2 finish.3.refs_0_
  672.2 4.5 gate.11
  676.7 3.4 second_half.4.refs_0_
  680.9 2.5 first_half.7
  684.8 1.3 copy-done.6
  686.1 3.4 second_half.5.refs_0_
  689.5 3.9 finish.4.refs_0_.refs_3_
  693.4 2.9 second_half.6.refs_0_
  697.7 2.0 second_half.7.refs_0_
  699.7 2.3 finish.5
  (173 shorter events, 14.1 us)
Async XLA Ops:
  7.2 6.2 copy-start.31
  7.2 6.1 copy-start.40
  7.2 6.1 copy-start.41
  7.2 6.1 copy-start.42
  7.2 6.1 copy-start.43
  7.2 6.1 copy-start.36
  7.2 6.1 copy-start.38
  7.3 6.4 copy-start.35
  7.3 660.7 %reduce-scatter.9.cloned.1.call-start = ((), (), s32[]{:S(2)}) async-start(), calls=%async_computation.8 | async-start | bytes 2621440 | tf_op jit(solution)/shard_map/reduce_scatter | solution.py:1049
  10.3 73.1 %collective-permute-start.1 = (bf16[512,2048]{1,0:T(8,128)(2,1)}, bf16[512,2048]{1,0:T(8,128)(2,1)S(1)}, u32[]{:S(2)}, u32[]{:S(2)}) collective-permute-start(bf16[512,2048]{1,0:T(8,128)(2,1)} %pick.2.refs_0_), channel_id=1, source_target_pairs={{0,1},{1,0},{2,3},{3,2},{4,5},{5,4},{6,7},{7,6},{8,9},{9,8},{10,11... | collective-permute-start | bytes 6291464 | tf_op jit(solution)/shard_map/ppermute | solution.py:107
  13.8 45.6 %collective-permute-start = (bf16[7936]{0:T(1024)(128)(2,1)S(1)}, bf16[7936]{0:T(1024)(128)(2,1)S(1)}, u32[]{:S(2)}, u32[]{:S(2)}) collective-permute-start(bf16[7936]{0:T(1024)(128)(2,1)S(1)} %dynamic-update-slice.7), channel_id=1, source_target_pairs={{0,1},{1,0},{2,3},{3,2},{4,5},{5,4},{6,7},{7,6},{8,9},{9,8},{10,11... | collective-permute-start | bytes 47624 | tf_op jit(solution)/shard_map/ppermute | solution.py:107
  59.5 27.0 %copy-start.33 = (bf16[7936]{0:T(1024)(128)(2,1)}, bf16[7936]{0:T(1024)(128)(2,1)S(1)}, u32[]{:S(2)}) copy-start(bf16[7936]{0:T(1024)(128)(2,1)S(1)} %collective-permute-done) | copy-start | bytes 47620
  59.7 19.4 %copy-start.26 = (f32[2048]{0:T(1024)}, f32[2048]{0:T(1024)S(1)}, u32[]{:S(2)}) copy-start(f32[2048]{0:T(1024)S(1)} %pad_maximum_fusion.3) | copy-start | bytes 24580
  83.4 1.3 copy-start
  84.7 4.4 collective-permute-start.2
  84.7 64.7 %collective-permute-start.3 = (bf16[512,2048]{1,0:T(8,128)(2,1)}, bf16[512,2048]{1,0:T(8,128)(2,1)}, u32[]{:S(2)}, u32[]{:S(2)}) collective-permute-start(bf16[512,2048]{1,0:T(8,128)(2,1)} %get-tuple-element.161), channel_id=1, source_target_pairs={{0,1},{1,0},{2,3},{3,2},{4,5},{5,4},{6,7},{7,6},{8,9},{9,8},{10,11... | collective-permute-start | bytes 6291464 | tf_op jit(solution)/shard_map/ppermute | solution.py:107
  89.1 1.3 copy-start.1
  149.5 4.6 collective-permute-start.4
  149.6 48.3 %collective-permute-start.5 = (bf16[2048,512]{1,0:T(8,128)(2,1)}, bf16[2048,512]{1,0:T(8,128)(2,1)S(1)}, u32[]{:S(2)}, u32[]{:S(2)}) collective-permute-start(bf16[2048,512]{1,0:T(8,128)(2,1)} %get-tuple-element.148.refs_0_), channel_id=1, source_target_pairs={{0,1},{1,0},{2,3},{3,2},{4,5},{5,4},{6,7},{7,6},{8,9},{9,8},{10,11... | collective-permute-start | bytes 6291464 | tf_op jit(solution)/shard_map/ppermute | solution.py:107
  197.8 1.3 copy-start.2
  199.1 4.4 collective-permute-start.6
  203.5 1.3 copy-start.4
  221.6 446.4 %reduce-scatter.11.cloned.1.call-start = ((), (), s32[]{:S(2)}) async-start(), calls=%async_computation.9 | async-start | bytes 2621440 | tf_op jit(solution)/shard_map/reduce_scatter | solution.py:1049
  302.7 365.3 %reduce-scatter.13.cloned.1.call-start = ((), (), s32[]{:S(2)}) async-start(), calls=%async_computation.10 | async-start | bytes 2621440 | tf_op jit(solution)/shard_map/reduce_scatter | solution.py:1049
  367.0 301.0 %reduce-scatter.15.cloned.1.call-start = ((), (), s32[]{:S(2)}) async-start(), calls=%async_computation.11 | async-start | bytes 2621440 | tf_op jit(solution)/shard_map/reduce_scatter | solution.py:1049
  402.9 286.5 %reduce-scatter.17.cloned.1.call-start = ((), (), s32[]{:S(2)}) async-start(), calls=%async_computation.12 | async-start | bytes 2621440 | tf_op jit(solution)/shard_map/reduce_scatter | solution.py:1054
  480.7 208.7 %reduce-scatter.19.cloned.1.call-start = ((), (), s32[]{:S(2)}) async-start(), calls=%async_computation.13 | async-start | bytes 2621440 | tf_op jit(solution)/shard_map/reduce_scatter | solution.py:1054
  532.9 156.6 %reduce-scatter.21.cloned.1.call-start = ((), (), s32[]{:S(2)}) async-start(), calls=%async_computation.14 | async-start | bytes 2621440 | tf_op jit(solution)/shard_map/reduce_scatter | solution.py:1054
  569.8 0.8 copy-start.19
  569.8 0.9 copy-start.20
  569.8 129.9 %reduce-scatter.23.cloned.1.call-start = ((), (), s32[]{:S(2)}) async-start(), calls=%async_computation.15 | async-start | bytes 2621440 | tf_op jit(solution)/shard_map/reduce_scatter | solution.py:1054
  612.9 0.9 copy-start.10
  612.9 1.0 copy-start.11
  612.9 1.0 copy-start.12
  613.0 1.1 copy-start.15
  613.0 1.1 copy-start.13
  613.0 12.6 %copy-start.21 = (f32[8,1536]{1,0:T(8,128)S(1)}, f32[8,1536]{1,0:T(8,128)}, u32[]{:S(2)}) copy-start(f32[8,1536]{1,0:T(8,128)} %get-tuple-element.171.refs_0_) | copy-start | bytes 147460
  613.0 12.6 %copy-start.22 = (f32[8,1536]{1,0:T(8,128)S(1)}, f32[8,1536]{1,0:T(8,128)}, u32[]{:S(2)}) copy-start(f32[8,1536]{1,0:T(8,128)} %get-tuple-element.185.refs_0_) | copy-start | bytes 147460
  613.0 12.6 %copy-start.23 = (f32[8,1536]{1,0:T(8,128)S(1)}, f32[8,1536]{1,0:T(8,128)}, u32[]{:S(2)}) copy-start(f32[8,1536]{1,0:T(8,128)} %get-tuple-element.204.refs_0_) | copy-start | bytes 147460
  613.0 12.6 %copy-start.24 = (f32[8,1536]{1,0:T(8,128)S(1)}, f32[8,1536]{1,0:T(8,128)}, u32[]{:S(2)}) copy-start(f32[8,1536]{1,0:T(8,128)} %get-tuple-element.211.refs_0_) | copy-start | bytes 147460
  614.1 12.3 %copy-start.5 = (f32[16,2048]{1,0:T(8,128)}, f32[16,2048]{1,0:T(8,128)S(1)}, u32[]{:S(2)}) copy-start(f32[16,2048]{1,0:T(8,128)S(1)} %add_add_fusion.refs_4_) | copy-start | bytes 393220
  631.9 6.1 copy-start.3
  637.7 39.0 %collective-permute-start.8 = (bf16[2048,512]{1,0:T(8,128)(2,1)}, bf16[2048,512]{1,0:T(8,128)(2,1)}, u32[]{:S(2)}, u32[]{:S(2)}) collective-permute-start(bf16[2048,512]{1,0:T(8,128)(2,1)} %get-tuple-element.254.refs_0_), channel_id=1, source_target_pairs={{0,8},{8,0},{16,24},{24,16},{1,9},{9,1},{17,25},{25,17},{2,10},{10... | collective-permute-start | bytes 6291464 | tf_op jit(solution)/shard_map/ppermute | solution.py:107
  638.9 19.9 %collective-permute-start.7 = (bf16[256,1536]{1,0:T(8,128)(2,1)}, bf16[256,1536]{1,0:T(8,128)(2,1)S(1)}, u32[]{:S(2)}, u32[]{:S(2)}) collective-permute-start(bf16[256,1536]{1,0:T(8,128)(2,1)} %slice.98), channel_id=1, source_target_pairs={{0,16},{8,24},{16,0},{24,8},{1,17},{9,25},{17,1},{25,9},{2,18},{10... | collective-permute-start | bytes 2359304 | tf_op jit(solution)/shard_map/ppermute | solution.py:107
  646.2 38.6 %collective-permute-start.10 = (bf16[512,2048]{1,0:T(8,128)(2,1)}, bf16[512,2048]{1,0:T(8,128)(2,1)S(1)}, u32[]{:S(2)}, u32[]{:S(2)}) collective-permute-start(bf16[512,2048]{1,0:T(8,128)(2,1)} %get-tuple-element.259.refs_0_), channel_id=1, source_target_pairs={{0,8},{8,0},{16,24},{24,16},{1,9},{9,1},{17,25},{25,17},{2,10},{10... | collective-permute-start | bytes 6291464 | tf_op jit(solution)/shard_map/ppermute | solution.py:107
  658.8 0.9 copy-start.9
  659.7 4.6 copy-start.37
  659.7 4.6 copy-start.39
  659.7 5.3 copy-start.7
  659.7 7.6 %copy-start.8 = (f32[8,1792]{1,0:T(8,128)S(1)}, f32[8,1792]{1,0:T(8,128)}, u32[]{:S(2)}) copy-start(f32[8,1792]{1,0:T(8,128)} %reshape.266.refs_1_.refs_2_.refs_3_) | copy-start | bytes 172036
  659.7 7.6 %copy-start.27 = (f32[8,1792]{1,0:T(8,128)S(1)}, f32[8,1792]{1,0:T(8,128)}, u32[]{:S(2)}) copy-start(f32[8,1792]{1,0:T(8,128)} %get-tuple-element.266) | copy-start | bytes 172036
  659.7 7.6 %copy-start.28 = (f32[8,1792]{1,0:T(8,128)S(1)}, f32[8,1792]{1,0:T(8,128)}, u32[]{:S(2)}) copy-start(f32[8,1792]{1,0:T(8,128)} %get-tuple-element.267) | copy-start | bytes 172036
  659.7 7.6 %copy-start.29 = (f32[8,1792]{1,0:T(8,128)S(1)}, f32[8,1792]{1,0:T(8,128)}, u32[]{:S(2)}) copy-start(f32[8,1792]{1,0:T(8,128)} %get-tuple-element.268) | copy-start | bytes 172036
  659.7 7.6 %copy-start.34 = (pred[8,1792]{1,0:T(8,128)(4,1)S(1)}, pred[8,1792]{1,0:T(8,128)(4,1)}, u32[]{:S(2)}) copy-start(pred[8,1792]{1,0:T(8,128)(4,1)} %constant.47.clone.1) | copy-start | bytes 43012
  664.3 29.1 %collective-permute-start.11 = (bf16[512,1536]{1,0:T(8,128)(2,1)}, bf16[512,1536]{1,0:T(8,128)(2,1)}, u32[]{:S(2)}, u32[]{:S(2)}) collective-permute-start(bf16[512,1536]{1,0:T(8,128)(2,1)} %get-tuple-element.261.refs_0_), channel_id=1, source_target_pairs={{0,8},{8,0},{16,24},{24,16},{1,9},{9,1},{17,25},{25,17},{2,10},{10... | collective-permute-start | bytes 4718600 | tf_op jit(solution)/shard_map/ppermute | solution.py:107
  665.0 15.1 %collective-permute-start.9 = (bf16[512,512]{1,0:T(8,128)(2,1)S(1)}, bf16[512,512]{1,0:T(8,128)(2,1)S(1)}, u32[]{:S(2)}, u32[]{:S(2)}) collective-permute-start(bf16[512,512]{1,0:T(8,128)(2,1)S(1)} %copy-done.7), channel_id=1, source_target_pairs={{0,16},{8,24},{16,0},{24,8},{1,17},{9,25},{17,1},{25,9},{2,18},{10... | collective-permute-start | bytes 1572872 | tf_op jit(solution)/shard_map/ppermute | solution.py:107
  680.1 3.3 copy-start.17
  680.1 3.3 copy-start.30
  680.1 0.8 copy-start.14
  683.4 13.6 %collective-permute-start.12 = (bf16[512,512]{1,0:T(8,128)(2,1)}, bf16[512,512]{1,0:T(8,128)(2,1)S(1)}, u32[]{:S(2)}, u32[]{:S(2)}) collective-permute-start(bf16[512,512]{1,0:T(8,128)(2,1)} %get-tuple-element.271.refs_0_), channel_id=1, source_target_pairs={{0,8},{8,0},{16,24},{24,16},{1,9},{9,1},{17,25},{25,17},{2,10},{10... | collective-permute-start | bytes 1572872 | tf_op jit(solution)/shard_map/ppermute | solution.py:107
  683.4 6.1 copy-start.25
  684.8 17.2 %copy-start.32 = (f32[1024]{0:T(1024)}, f32[1024]{0:T(1024)S(1)}, u32[]{:S(2)}) copy-start(f32[1024]{0:T(1024)S(1)} %get-tuple-element.342) | copy-start | bytes 12292
  684.8 1.3 copy-start.6
  693.4 2.9 slice-start
  (2 other events, 1.4 us)
Sparse Core Ops, SparseCore 0:
  221.7 44.9 reduce-scatter.8
  302.8 44.4 reduce-scatter.10
  367.1 44.0 reduce-scatter.12
  413.4 43.1 reduce-scatter.14
  480.9 44.0 reduce-scatter.16
  533.0 44.0 reduce-scatter.18
  579.4 45.1 reduce-scatter.20
  627.0 43.3 reduce-scatter.22

commit v5 on v3

--- a/solution.py
+++ b/solution.py
@@ -1246,6 +1246,9 @@
     keep("qkv")
     over_y("qkv", 1)
     go_back(2)
+    mine_done("down")
+    sibling_swap("down")
+    finish_out(0, micros)
     over_y("qkv", 1)
     keep("dense")
     add_up("qkv")
@@ -1264,18 +1267,15 @@
     vector = summed(spreads, size)
     found["qkv"] = gate(line, w, found["qkv"])
     rest_over_x("qkv")
-    mine_done("down")
-    sibling_swap("down")
     mine_done("up")
     sibling_swap("up")
-    finish_out(0, micros)
+    all_done("down")
     mine_done("qkv")
     sibling_swap("qkv")
     rest_over_x("dense")
     spreads = spread(vector, "dp")
     one_sums = gate(line, w, one_sums)
     vector = summed(spreads, size)
-    all_done("down")
     all_done("up")
     mine_done("dense")
     sibling_swap("dense")

time: 704 us -> 715 us (1.016)
    unnamed x79 -> x81, local copies, waits for them, and re-layouts: 14.9 us -> 16.1 us
  transfers between devices with their start and end apart: 21 -> 21, of which waited for: 7 -> 8; matrix products, arithmetic and copies ran while one was open for 2% -> 2% of each run, Pallas kernels for 82% -> 81%
where the time goes in v5:
time: 715 us; the launch traced here: 707 us
  Pallas kernels  597 us (83%)
  waiting for transfers between devices  49.9 us (7%)
  local copies, waits for them, and re-layouts  21.3 us (3%)
  between operations  15.3 us (2%)
  starting transfers between devices  13.5 us (2%)
  other arithmetic  9.29 us (1%)
    pallas_call x49, Pallas kernels, call(): pl.pallas_call(body, grid=grid, in_specs=[anywhere] * skip + [anywhere if...  597 us
    ppermute x13, waiting for transfers between devices, swap(): lax.ppermute(block, axis, [(i, i ^ distance) for i in range(lax.axis_size...  49.7 us
    unnamed x81, local copies, waits for them, and re-layouts  16.1 us
  transfers between devices with their start and end apart: 21, of which 8 were waited for; matrix products, arithmetic and copies ran while one was open for 2% of the time, Pallas kernels for 81%

profile of v5, /device:TPU:0, one launch (start us, length us, event | category | flops | bytes accessed | tf_op | source)
XLA Modules:
  0.0 706.7 jit_solution(3762972212128151431)
XLA Ops:
  13.4 3.0 collective-permute-start
  16.3 1.7 collective-permute-done.refs_0_
  18.7 3.0 pick.2.refs_0_
  21.6 2.0 collective-permute-start.1
  25.8 18.1 %norms.1 = (bf16[2048,2048]{1,0:T(8,128)(2,1)}, bf16[2048,2048]{1,0:T(8,128)(2,1)}, f32[8,2048]{1,0:T(8,128)}) custom-call(bf16[512,2048]{1,0:T(8,128)(2,1)} %pick.2.refs_0_, bf16[2048,2048]{1,0:T(8,128)(2,1)} %bitcast.52, bf16[2048,2048]{1,0:T(8,128)(2,1)} %bitcast.31, f32[4,2048]{1,0:T(4,128)} %pad_maximum_fusion.refs_3_), custom_call_target="tpu_custom_call" | custom-call | flops 12582912 | bytes 3355443 | tf_op jit(solution)/shard_map/norms/pallas_call | solution.py:213
  43.9 4.4 pick.3
  48.3 20.0 %collective-permute-done.1.refs_1_ = bf16[512,2048]{1,0:T(8,128)(2,1)S(1)} collective-permute-done((bf16[512,2048]{1,0:T(8,128)(2,1)}, bf16[512,2048]{1,0:T(8,128)(2,1)S(1)}, u32[]{:S(2)}, u32[]{:S(2)}) %collective-permute-start.1) | collective-permute-done | bytes 2097184 | tf_op jit(solution)/shard_map/ppermute | solution.py:107
  68.4 1.3 copy-done
  69.7 1.7 collective-permute-start.3
  72.7 1.3 collective-permute-done.2.refs_4_.refs_14_.refs_7_.refs_17_.refs_9_.refs_8_.refs_10_.refs_5_.refs_6_
  74.0 1.3 copy-done.1
  75.4 10.6 %projections.2 = (bf16[512,512]{1,0:T(8,128)(2,1)}, bf16[512,512]{1,0:T(8,128)(2,1)}, bf16[512,512]{1,0:T(8,128)(2,1)}, bf16[512,512]{1,0:T(8,128)(2,1)}) custom-call(bf16[512,2048]{1,0:T(8,128)(2,1)} %gate.6.refs_0_.refs_3_.refs_13_.refs_6_.refs_16_.refs_8_.refs_7_.refs_9_.refs_4_.refs_5_, bf16[2048,2048]{1,0:T(8,128)(2,1)} %get-tuple-element.149.refs_1_.refs_4_.refs_2_, ...), custom_call_target="tpu_custom_call" | custom-call | flops 429496736 | bytes 1468006 | tf_op jit(solution)/shard_map/projections/pallas_call | solution.py:213
  86.0 32.5 %projections.3 = (bf16[1536,512]{1,0:T(8,128)(2,1)}, bf16[1536,512]{1,0:T(8,128)(2,1)}, bf16[1536,512]{1,0:T(8,128)(2,1)}, bf16[1536,512]{1,0:T(8,128)(2,1)}, bf...) custom-call(bf16[512,512]{1,0:T(8,128)(2,1)} %get-tuple-element.150.refs_0_.refs_3_, ...), custom_call_target="tpu_custom_call" | custom-call | flops 1288490240 | bytes 2726297 | tf_op jit(solution)/shard_map/projections/pallas_call | solution.py:213
  118.4 16.1 %attention.4 = (bf16[512,512]{1,0:T(8,128)(2,1)}, bf16[512,512]{1,0:T(8,128)(2,1)}, bf16[512,512]{1,0:T(8,128)(2,1)}, bf16[512,512]{1,0:T(8,128)(2,1)}, bf16[512...) custom-call(bf16[1536,512]{1,0:T(8,128)(2,1)} %get-tuple-element.153.refs_0_.refs_1_, ...), custom_call_target="tpu_custom_call" | custom-call | flops 751619264 | bytes 629145 | tf_op jit(solution)/shard_map/attention/pallas_call | solution.py:213
  134.7 1.8 collective-permute-start.5
  137.1 2.1 collective-permute-done.4.refs_8_.refs_10_
  139.2 41.0 %feed_up.1 = (bf16[2048,2048]{1,0:T(8,128)(2,1)}, bf16[2048,2048]{1,0:T(8,128)(2,1)}, bf16[512,512]{1,0:T(8,128)(2,1)}, bf16[512,512]{1,0:T(8,128)(2,1)}, bf16[5...) custom-call(bf16[512,2048]{1,0:T(8,128)(2,1)} %gate.7.refs_0_.refs_7_.refs_9_, ...), custom_call_target="tpu_custom_call" | custom-call | flops 1717986944 | bytes 4194304 | tf_op jit(solution)/shard_map/feed_up/pallas_call | solution.py:213
  180.2 2.7 collective-permute-done.5.refs_1_
  183.0 1.3 copy-done.2
  184.3 4.4 collective-permute-done.6.refs_6_.refs_11_.refs_5_.refs_7_
  188.6 1.3 copy-done.4
  190.0 16.7 %outputs.4 = (bf16[512,2048]{1,0:T(8,128)(2,1)}, bf16[512,512]{1,0:T(8,128)(2,1)}, bf16[512,1536]{1,0:T(8,128)(2,1)}, f32[8,1536]{1,0:T(8,128)}, bf16[512,512]{1,0:T(8,128)(2,1)}, /*index=5*/bf16[512,512]{1,0:T(8,128)(2,1)}) custom-call(bf16[2048,512]{1,0:T(8,128)(2,1)} %gate.8.refs_0_.refs_5_.refs_10_.refs_4_.refs_6_, ...), custom_call_target="tpu_custom_call" | custom-call | flops 536870912 | bytes 1887436 | tf_op jit(solution)/shard_map/outputs/pallas_call | solution.py:213
  207.0 15.9 %attention.5 = (bf16[512,512]{1,0:T(8,128)(2,1)}, bf16[512,512]{1,0:T(8,128)(2,1)}, bf16[512,512]{1,0:T(8,128)(2,1)}, bf16[512,512]{1,0:T(8,128)(2,1)}, bf16[512,512]{1,0:T(8,128)(2,1)}) custom-call(f32[8,1536]{1,0:T(8,128)} %get-tuple-element.171.refs_0_, bf16[1536,512]{1,0:T(8,128)(2,1)} %get-tuple-element.153.refs_0_.refs_1_, ...), custom_call_target="tpu_custom_call" | custom-call | flops 751619264 | bytes 629145 | tf_op jit(solution)/shard_map/attention/pallas_call | solution.py:213
  222.9 18.3 %weight_grad.8 = (bf16[2,2048,512]{2,1,0:T(8,128)(2,1)}, bf16[512,512]{1,0:T(8,128)(2,1)}, bf16[512,512]{1,0:T(8,128)(2,1)}) custom-call(bf16[512,512]{1,0:T(8,128)(2,1)} %get-tuple-element.176.refs_0_.refs_1_, bf16[512,512]{1,0:T(8,128)(2,1)} %get-tuple-element.177.refs_1_, bf16[512,512]{1,0:T(8,128)(2,1)} %get-tuple-element.178.refs_2_, ...), custom_call_target="tpu_custom_call" | custom-call | flops 858993472 | bytes 2097152 | tf_op jit(solution)/shard_map/weight_grad/pallas_call | solution.py:213
  241.2 30.2 %pre_grads.1 = (bf16[2048,2048]{1,0:T(8,128)(2,1)}, f32[8,2048]{1,0:T(8,128)}, bf16[512,512]{1,0:T(8,128)(2,1)}, bf16[512,512]{1,0:T(8,128)(2,1)}, bf16[512,512]{1,0:T(8,128)(2,1)}, /*index=5*/bf16[4096,512]{1,0:T(8,128)(2,1)}) custom-call(bf16[2,2048,512]{2,1,0:T(8,128)(2,1)} %get-tuple-element.179.refs_0_, ...), custom_call_target="tpu_custom_call" | custom-call | flops 1717986944 | bytes 4194304 | tf_op jit(solution)/shard_map/pre_grads/pallas_call | solution.py:213
  271.4 16.5 %outputs.5 = (bf16[512,2048]{1,0:T(8,128)(2,1)}, bf16[512,512]{1,0:T(8,128)(2,1)}, bf16[512,1536]{1,0:T(8,128)(2,1)}, f32[8,1536]{1,0:T(8,128)}, bf16[512,512]{1,0:T(8,128)(2,1)}) custom-call(f32[8,2048]{1,0:T(8,128)} %get-tuple-element.180.refs_0_, bf16[1536,512]{1,0:T(8,128)(2,1)} %get-tuple-element.153.refs_0_.refs_1_, ...), custom_call_target="tpu_custom_call" | custom-call | flops 536870912 | bytes 1887436 | tf_op jit(solution)/shard_map/outputs/pallas_call | solution.py:213
  288.5 13.0 %attention.6 = (bf16[512,512]{1,0:T(8,128)(2,1)}, bf16[512,512]{1,0:T(8,128)(2,1)}, bf16[512,512]{1,0:T(8,128)(2,1)}, bf16[512,512]{1,0:T(8,128)(2,1)}) custom-call(f32[8,1536]{1,0:T(8,128)} %get-tuple-element.185.refs_0_, bf16[1536,512]{1,0:T(8,128)(2,1)} %get-tuple-element.172.refs_2_.refs_1_.refs_3_, bf16[512,512]{1,0:T(8,128)(2,1)} %get-tuple-element.186.refs_2_, ...), custom_call_target="tpu_custom_call" | custom-call | flops 751619264 | bytes 629145 | tf_op jit(solution)/shard_map/attention/pallas_call | solution.py:213
  301.5 17.8 %weight_grad.9 = (bf16[2,2048,512]{2,1,0:T(8,128)(2,1)}, bf16[512,512]{1,0:T(8,128)(2,1)}, bf16[512,512]{1,0:T(8,128)(2,1)}) custom-call(bf16[512,512]{1,0:T(8,128)(2,1)} %get-tuple-element.189.refs_0_.refs_1_, bf16[512,512]{1,0:T(8,128)(2,1)} %get-tuple-element.190.refs_1_, bf16[512,512]{1,0:T(8,128)(2,1)} %get-tuple-element.191.refs_2_, ...), custom_call_target="tpu_custom_call" | custom-call | flops 858993472 | bytes 2097152 | tf_op jit(solution)/shard_map/weight_grad/pallas_call | solution.py:213
  319.3 16.5 %attention.7 = (bf16[512,512]{1,0:T(8,128)(2,1)}, bf16[512,512]{1,0:T(8,128)(2,1)}, bf16[512,512]{1,0:T(8,128)(2,1)}, bf16[512,512]{1,0:T(8,128)(2,1)}, bf16[512...) custom-call(bf16[2,2048,512]{2,1,0:T(8,128)(2,1)} %get-tuple-element.193.refs_0_.refs_2_.refs_3_.refs_1_, ...), custom_call_target="tpu_custom_call" | custom-call | flops 751619264 | bytes 629145 | tf_op jit(solution)/shard_map/attention/pallas_call | solution.py:213
  335.8 16.4 %outputs.6 = (bf16[512,2048]{1,0:T(8,128)(2,1)}, bf16[512,512]{1,0:T(8,128)(2,1)}, bf16[512,1536]{1,0:T(8,128)(2,1)}, f32[8,1536]{1,0:T(8,128)}, bf16[512,512]{1...) custom-call(bf16[512,512]{1,0:T(8,128)(2,1)} %get-tuple-element.197.refs_0_.refs_1_, ...), custom_call_target="tpu_custom_call" | custom-call | flops 536870912 | bytes 1887436 | tf_op jit(solution)/shard_map/outputs/pallas_call | solution.py:213
  352.3 19.4 %weight_grad.10 = (bf16[2,512,2048]{2,1,0:T(8,128)(2,1)}, bf16[512,512]{1,0:T(8,128)(2,1)}, bf16[512,512]{1,0:T(8,128)(2,1)}) custom-call(f32[8,1536]{1,0:T(8,128)} %get-tuple-element.204.refs_0_, bf16[512,512]{1,0:T(8,128)(2,1)} %get-tuple-element.197.refs_0_.refs_1_, bf16[2,2048,512]{2,1,0:T(8,128)(2,1)} %get-tuple-element.193.refs_0_.refs_2_.refs_3_.refs_1_, ...), custom_call_target="tpu_custom_call" | custom-call | flops 858993472 | bytes 2097152 | tf_op jit(solution)/shard_map/weight_grad/pallas_call | solution.py:213
  371.7 16.5 %outputs.7 = (bf16[512,2048]{1,0:T(8,128)(2,1)}, bf16[512,512]{1,0:T(8,128)(2,1)}, bf16[512,1536]{1,0:T(8,128)(2,1)}, f32[8,1536]{1,0:T(8,128)}, bf16[512,512]{1,0:T(8,128)(2,1)}, /*index=5*/bf16[1024,2048]{1,0:T(8,128)(2,1)}) custom-call(bf16[2,512,2048]{2,1,0:T(8,128)(2,1)} %get-tuple-element.206.refs_0_, ...), custom_call_target="tpu_custom_call" | custom-call | flops 536870912 | bytes 1887436 | tf_op jit(solution)/shard_map/outputs/pallas_call | solution.py:213
  388.3 3.9 add.150.refs_0_.refs_1_.refs_2_.refs_3_
  392.2 18.8 %weight_grad.11 = (bf16[2,512,2048]{2,1,0:T(8,128)(2,1)}, bf16[512,512]{1,0:T(8,128)(2,1)}) custom-call(bf16[2048,512]{1,0:T(8,128)(2,1)} %add.150.refs_0_.refs_1_.refs_2_.refs_3_, bf16[2048,512]{1,0:T(8,128)(2,1)} %add.150.refs_0_.refs_1_.refs_2_.refs_3_, bf16[2048,2048]{1,0:T(8,128)(2,1)} %get-tuple-element.164.refs_5_.refs_3_.refs_2_, ...), custom_call_target="tpu_custom_call" | custom-call | flops 858993472 | bytes 2097152 | tf_op jit(solution)/shard_map/weight_grad/pallas_call | solution.py:213
  411.0 41.8 %backs.5 = (bf16[2048,2048]{1,0:T(8,128)(2,1)}, f32[16,2048]{1,0:T(8,128)}, bf16[512,512]{1,0:T(8,128)(2,1)}, bf16[512,512]{1,0:T(8,128)(2,1)}, bf16[512,512]{1,...) custom-call(bf16[2,512,2048]{2,1,0:T(8,128)(2,1)} %get-tuple-element.217.refs_0_.re, ...), custom_call_target="tpu_custom_call" | custom-call | flops 1717986944 | bytes 4194304 | tf_op jit(solution)/shard_map/backs/pallas_call | solution.py:213
  452.8 13.1 %backs.6 = (bf16[512,2048]{1,0:T(8,128)(2,1)}, f32[16,2048]{1,0:T(8,128)}, bf16[128,2048]{1,0:T(8,128)(2,1)}) custom-call(f32[16,2048]{1,0:T(8,128)} %get-tuple-element.218.refs_0_, bf16[2,512,2048]{2,1,0:T(8,128)(2,1)} %get-tuple-element.217.refs_0_.refs_4_.refs_5_.refs_6_.refs_1_, bf16[512,1536]{1,0:T(8,128)(2,1)} %get-tuple-element.219.refs_2_.refs_3_, ...), custom_call_target="tpu_custom_call" | custom-call | flops 322122560 | bytes 1415577 | tf_op jit(solution)/shard_map/backs/pallas_call | solution.py:213
  466.0 3.9 add.151.refs_0_.refs_1_
  469.9 14.9 %weight_grad.12 = (bf16[2,512,1536]{2,1,0:T(8,128)(2,1)}, bf16[128,2048]{1,0:T(8,128)(2,1)}) custom-call(bf16[512,2048]{1,0:T(8,128)(2,1)} %add.151.refs_0_.refs_1_, bf16[512,2048]{1,0:T(8,128)(2,1)} %add.151.refs_0_.refs_1_, bf16[2048,2048]{1,0:T(8,128)(2,1)} %get-tuple-element.149.refs_1_.refs_4_.refs_2_, ...), custom_call_target="tpu_custom_call" | custom-call | flops 644245120 | bytes 1677721 | tf_op jit(solution)/shard_map/weight_grad/pallas_call | solution.py:213
  484.9 18.0 %weight_grad.13 = (bf16[2,512,512]{2,1,0:T(8,128)(2,1)}, bf16[128,2048]{1,0:T(8,128)(2,1)}, bf16[1024,1536]{1,0:T(8,128)(2,1)}) custom-call(bf16[2,512,1536]{2,1,0:T(8,128)(2,1)} %get-tuple-element.229.refs_0_, bf16[512,2048]{1,0:T(8,128)(2,1)} %add.151.refs_0_.refs_1_, bf16[1024,1536]{1,0:T(8,128)(2,1)} %bitcast.60, bf16[2048,2048]{1,0:T(8,128)(2,1)} %bitcast.48, ...), custom_call_target="tpu_custom_call" | custom-call | flops 214748368 | bytes 838860 | tf_op jit(solution)/shard_map/weight_grad/pallas_call | solution.py:213
  502.8 15.2 %backs.7 = (bf16[512,2048]{1,0:T(8,128)(2,1)}, f32[16,2048]{1,0:T(8,128)}, bf16[128,2048]{1,0:T(8,128)(2,1)}, bf16[1024,512]{1,0:T(8,128)(2,1)}) custom-call(bf16[2,512,512]{2,1,0:T(8,128)(2,1)} %get-tuple-element.234.refs_0_, bf16[512,2048]{1,0:T(8,128)(2,1)} %add.151.refs_0_.refs_1_, bf16[1024,512]{1,0:T(8,128)(2,1)} %bitcast.61, ...), custom_call_target="tpu_custom_call" | custom-call | flops 322122560 | bytes 1415577 | tf_op jit(solution)/shard_map/backs/pallas_call | solution.py:213
  518.2 17.5 %weight_grad.14 = (bf16[2,512,1536]{2,1,0:T(8,128)(2,1)}, bf16[128,2048]{1,0:T(8,128)(2,1)}) custom-call(f32[16,2048]{1,0:T(8,128)} %get-tuple-element.235.refs_0_, bf16[512,2048]{1,0:T(8,128)(2,1)} %add.151.refs_0_.refs_1_, bf16[2048,2048]{1,0:T(8,128)(2,1)} %get-tuple-element.149.refs_1_.refs_4_.refs_2_, ...), custom_call_target="tpu_custom_call" | custom-call | flops 644245120 | bytes 1677721 | tf_op jit(solution)/shard_map/weight_grad/pallas_call | solution.py:213
  535.7 19.5 %backs.8 = (bf16[512,2048]{1,0:T(8,128)(2,1)}, f32[16,2048]{1,0:T(8,128)}, bf16[256,1536]{1,0:T(8,128)(2,1)}) custom-call(bf16[2,512,1536]{2,1,0:T(8,128)(2,1)} %get-tuple-element.237.refs_0_.refs_1_, bf16[2,512,1536]{2,1,0:T(8,128)(2,1)} %get-tuple-element.237.refs_0_.refs_1_, bf16[512,1536]{1,0:T(8,128)(2,1)} %get-tuple-element.227.refs_5_.refs_2_, ...), custom_call_target="tpu_custom_call" | custom-call | flops 322122560 | bytes 1415577 | tf_op jit(solution)/shard_map/backs/pallas_call | solution.py:213
  557.4 5.6 first_half.4
  563.2 4.2 finish.3.refs_0_
  567.4 24.5 %weight_grad.15 = (bf16[2,512,512]{2,1,0:T(8,128)(2,1)}, bf16[256,1536]{1,0:T(8,128)(2,1)}) custom-call(bf16[4,512,512]{2,1,0:T(8,128)(2,1)} %finish.3.refs_0_, bf16[2,512,1536]{2,1,0:T(8,128)(2,1)} %get-tuple-element.237.refs_0_.refs_1_, bf16[2048,2048]{1,0:T(8,128)(2,1)} %bitcast.50, bf16[2048,2048]{1,0:T(8,128)(2,1)} %bitcast.51, ...), custom_call_target="tpu_custom_call" | custom-call | flops 214748368 | bytes 838860 | tf_op jit(solution)/shard_map/weight_grad/pallas_call | solution.py:213
  591.9 3.4 add.152.refs_0_.refs_1_
  595.3 21.3 %backs.9 = (bf16[512,2048]{1,0:T(8,128)(2,1)}, f32[16,2048]{1,0:T(8,128)}, bf16[256,1536]{1,0:T(8,128)(2,1)}, bf16[512,512]{1,0:T(8,128)(2,1)}) custom-call(bf16[512,1536]{1,0:T(8,128)(2,1)} %add.152.refs_0_.refs_1_, bf16[512,1536]{1,0:T(8,128)(2,1)} %add.152.refs_0_.refs_1_, bf16[2,512,512]{2,1,0:T(8,128)(2,1)} %get-tuple-element.249.refs_0_.refs_2_.refs_4_, ...), custom_call_target="tpu_custom_call" | custom-call | flops 322122560 | bytes 1415577 | tf_op jit(solution)/shard_map/backs/pallas_call | solution.py:213
  618.5 8.4 %add.153 = (bf16[512,512]{1,0:T(8,128)(2,1)}, f32[8,1024]{1,0:T(8,128)}, f32[8,1024]{1,0:T(8,128)}, f32[8,1024]{1,0:T(8,128)}) custom-call(f32[16,2048]{1,0:T(8,128)} %get-tuple-element.252.refs_0_, f32[8,1024]{1,0:T(8,128)} %select_n.104.refs_1_.refs_2_.refs_3_, f32[8,1024]{1,0:T(8,128)} %select_n.104.refs_1_.refs_2_.refs_3_, ...), custom_call_target="tpu_custom_call" | custom-call | bytes 157286 | tf_op jit(solution)/shard_map/add/pallas_call | solution.py:213
  628.4 5.5 gate.9
  633.9 5.7 first_half.5
  641.0 1.7 collective-permute-start.8
  642.7 1.3 copy-done.6
  644.0 3.4 second_half.4.refs_0_
  647.4 13.3 %collective-permute-done.8.refs_3_ = bf16[256,1536]{1,0:T(8,128)(2,1)S(1)} collective-permute-done((bf16[256,1536]{1,0:T(8,128)(2,1)}, bf16[256,1536]{1,0:T(8,128)(2,1)S(1)}, u32[]{:S(2)}, u32[]{:S(2)}) %collective-permute-start.8) | collective-permute-done | bytes 786464 | tf_op jit(solution)/shard_map/ppermute | solution.py:107
  661.6 4.5 first_half.6
  666.1 1.7 collective-permute-start.10
  668.5 4.5 gate.11
  673.1 3.4 second_half.5.refs_0_
  676.4 4.0 collective-permute-done.10.refs_2_
  681.3 2.5 first_half.7
  685.9 3.9 finish.4.refs_0_.refs_3_
  690.9 2.9 second_half.6.refs_0_
  694.6 2.0 second_half.7.refs_0_
  696.5 2.3 finish.5
  (160 shorter events, 25.9 us)
Async XLA Ops:
  7.2 555.9 %reduce-scatter.9.cloned.1.call-start = ((), (), s32[]{:S(2)}) async-start(), calls=%async_computation.8 | async-start | bytes 2621440 | tf_op jit(solution)/shard_map/reduce_scatter | solution.py:1049
  13.4 4.7 collective-permute-start
  18.1 0.6 copy-start.27
  21.6 46.7 %collective-permute-start.1 = (bf16[512,2048]{1,0:T(8,128)(2,1)}, bf16[512,2048]{1,0:T(8,128)(2,1)S(1)}, u32[]{:S(2)}, u32[]{:S(2)}) collective-permute-start(bf16[512,2048]{1,0:T(8,128)(2,1)} %pick.2.refs_0_), channel_id=1, source_target_pairs={{0,1},{1,0},{2,3},{3,2},{4,5},{5,4},{6,7},{7,6},{8,9},{9,8},{10,11... | collective-permute-start | bytes 6291464 | tf_op jit(solution)/shard_map/ppermute | solution.py:107
  24.5 0.6 copy-start.19
  24.5 19.4 %copy-start.26 = (f32[2048]{0:T(1024)}, f32[2048]{0:T(1024)S(1)}, u32[]{:S(2)}) copy-start(f32[2048]{0:T(1024)S(1)} %pad_maximum_fusion.3) | copy-start | bytes 24580
  68.3 1.3 copy-start
  69.7 1.7 copy-start.35
  69.7 4.4 collective-permute-start.2
  69.7 64.9 %collective-permute-start.3 = (bf16[512,2048]{1,0:T(8,128)(2,1)}, bf16[512,2048]{1,0:T(8,128)(2,1)}, u32[]{:S(2)}, u32[]{:S(2)}) collective-permute-start(bf16[512,2048]{1,0:T(8,128)(2,1)} %get-tuple-element.161), channel_id=1, source_target_pairs={{0,1},{1,0},{2,3},{3,2},{4,5},{5,4},{6,7},{7,6},{8,9},{9,8},{10,11... | collective-permute-start | bytes 6291464 | tf_op jit(solution)/shard_map/ppermute | solution.py:107
  74.0 1.3 copy-start.1
  134.6 1.9 copy-start.34
  134.6 4.6 collective-permute-start.4
  134.7 48.3 %collective-permute-start.5 = (bf16[2048,512]{1,0:T(8,128)(2,1)}, bf16[2048,512]{1,0:T(8,128)(2,1)S(1)}, u32[]{:S(2)}, u32[]{:S(2)}) collective-permute-start(bf16[2048,512]{1,0:T(8,128)(2,1)} %get-tuple-element.148.refs_0_), channel_id=1, source_target_pairs={{0,1},{1,0},{2,3},{3,2},{4,5},{5,4},{6,7},{7,6},{8,9},{9,8},{10,11... | collective-permute-start | bytes 6291464 | tf_op jit(solution)/shard_map/ppermute | solution.py:107
  183.0 1.3 copy-start.2
  184.3 4.4 collective-permute-start.6
  188.6 1.3 copy-start.4
  206.7 356.4 %reduce-scatter.11.cloned.1.call-start = ((), (), s32[]{:S(2)}) async-start(), calls=%async_computation.9 | async-start | bytes 2621440 | tf_op jit(solution)/shard_map/reduce_scatter | solution.py:1049
  288.0 275.2 %reduce-scatter.13.cloned.1.call-start = ((), (), s32[]{:S(2)}) async-start(), calls=%async_computation.10 | async-start | bytes 2621440 | tf_op jit(solution)/shard_map/reduce_scatter | solution.py:1049
  352.2 210.9 %reduce-scatter.15.cloned.1.call-start = ((), (), s32[]{:S(2)}) async-start(), calls=%async_computation.11 | async-start | bytes 2621440 | tf_op jit(solution)/shard_map/reduce_scatter | solution.py:1049
  388.2 297.6 %reduce-scatter.17.cloned.1.call-start = ((), (), s32[]{:S(2)}) async-start(), calls=%async_computation.12 | async-start | bytes 2621440 | tf_op jit(solution)/shard_map/reduce_scatter | solution.py:1054
  465.9 219.9 %reduce-scatter.19.cloned.1.call-start = ((), (), s32[]{:S(2)}) async-start(), calls=%async_computation.13 | async-start | bytes 2621440 | tf_op jit(solution)/shard_map/reduce_scatter | solution.py:1054
  518.1 167.7 %reduce-scatter.21.cloned.1.call-start = ((), (), s32[]{:S(2)}) async-start(), calls=%async_computation.14 | async-start | bytes 2621440 | tf_op jit(solution)/shard_map/reduce_scatter | solution.py:1054
  555.2 0.7 copy-start.36
  555.2 0.7 copy-start.37
  555.2 0.8 copy-start.20
  555.2 2.2 copy-start.21
  555.2 141.3 %reduce-scatter.23.cloned.1.call-start = ((), (), s32[]{:S(2)}) async-start(), calls=%async_computation.15 | async-start | bytes 2621440 | tf_op jit(solution)/shard_map/reduce_scatter | solution.py:1054
  557.4 5.6 copy-start.22
  557.4 5.6 copy-start.23
  557.4 5.6 copy-start.24
  557.4 5.6 copy-start.25
  563.0 79.7 %collective-permute-start.7 = (bf16[2048,512]{1,0:T(8,128)(2,1)}, bf16[2048,512]{1,0:T(8,128)(2,1)S(1)}, u32[]{:S(2)}, u32[]{:S(2)}) collective-permute-start(bf16[2048,512]{1,0:T(8,128)(2,1)} %get-tuple-element.243.refs_0_), channel_id=1, source_target_pairs={{0,8},{8,0},{16,24},{24,16},{1,9},{9,1},{17,25},{25,17},{2,10},{10... | collective-permute-start | bytes 6291464 | tf_op jit(solution)/shard_map/ppermute | solution.py:107
  616.6 0.9 copy-start.11
  616.6 1.0 copy-start.12
  616.6 1.0 copy-start.15
  616.6 1.1 copy-start.16
  616.6 1.1 copy-start.13
  617.8 10.6 %copy-start.5 = (f32[16,2048]{1,0:T(8,128)}, f32[16,2048]{1,0:T(8,128)S(1)}, u32[]{:S(2)}) copy-start(f32[16,2048]{1,0:T(8,128)S(1)} %add_add_fusion.refs_4_) | copy-start | bytes 393220
  633.9 6.2 copy-start.3
  639.6 33.5 %collective-permute-start.9 = (bf16[512,2048]{1,0:T(8,128)(2,1)}, bf16[512,2048]{1,0:T(8,128)(2,1)}, u32[]{:S(2)}, u32[]{:S(2)}) collective-permute-start(bf16[512,2048]{1,0:T(8,128)(2,1)} %get-tuple-element.263.refs_0_), channel_id=1, source_target_pairs={{0,8},{8,0},{16,24},{24,16},{1,9},{9,1},{17,25},{25,17},{2,10},{10... | collective-permute-start | bytes 6291464 | tf_op jit(solution)/shard_map/ppermute | solution.py:107
  641.0 19.7 %collective-permute-start.8 = (bf16[256,1536]{1,0:T(8,128)(2,1)}, bf16[256,1536]{1,0:T(8,128)(2,1)S(1)}, u32[]{:S(2)}, u32[]{:S(2)}) collective-permute-start(bf16[256,1536]{1,0:T(8,128)(2,1)} %slice.100), channel_id=1, source_target_pairs={{0,16},{8,24},{16,0},{24,8},{1,17},{9,25},{17,1},{25,9},{2,18},{10... | collective-permute-start | bytes 2359304 | tf_op jit(solution)/shard_map/ppermute | solution.py:107
  642.7 1.3 copy-start.6
  660.7 0.9 copy-start.10
  661.6 4.6 copy-start.7
  661.6 6.3 copy-start.9
  661.6 6.3 copy-start.28
  661.6 6.3 copy-start.29
  661.6 6.3 copy-start.30
  661.6 6.3 copy-start.33
  666.1 23.6 %collective-permute-start.11 = (bf16[512,1536]{1,0:T(8,128)(2,1)}, bf16[512,1536]{1,0:T(8,128)(2,1)S(1)}, u32[]{:S(2)}, u32[]{:S(2)}) collective-permute-start(bf16[512,1536]{1,0:T(8,128)(2,1)} %get-tuple-element.266.refs_0_), channel_id=1, source_target_pairs={{0,8},{8,0},{16,24},{24,16},{1,9},{9,1},{17,25},{25,17},{2,10},{10... | collective-permute-start | bytes 4718600 | tf_op jit(solution)/shard_map/ppermute | solution.py:107
  666.1 14.3 %collective-permute-start.10 = (bf16[512,512]{1,0:T(8,128)(2,1)S(1)}, bf16[512,512]{1,0:T(8,128)(2,1)S(1)}, u32[]{:S(2)}, u32[]{:S(2)}) collective-permute-start(bf16[512,512]{1,0:T(8,128)(2,1)S(1)} %copy-done.7), channel_id=1, source_target_pairs={{0,16},{8,24},{16,0},{24,8},{1,17},{9,25},{17,1},{25,9},{2,18},{10... | collective-permute-start | bytes 1572872 | tf_op jit(solution)/shard_map/ppermute | solution.py:107
  676.4 7.3 %copy-start.18 = (f32[8,1792]{1,0:T(8,128)S(1)}, f32[8,1792]{1,0:T(8,128)}, u32[]{:S(2)}) copy-start(f32[8,1792]{1,0:T(8,128)} %add_select_fusion.refs_1_) | copy-start | bytes 172036
  676.4 7.3 %copy-start.31 = (f32[8,1792]{1,0:T(8,128)S(1)}, f32[8,1792]{1,0:T(8,128)}, u32[]{:S(2)}) copy-start(f32[8,1792]{1,0:T(8,128)} %get-tuple-element.279) | copy-start | bytes 172036
  680.5 0.8 copy-start.14
  683.7 10.0 %collective-permute-start.12 = (bf16[512,512]{1,0:T(8,128)(2,1)}, bf16[512,512]{1,0:T(8,128)(2,1)S(1)}, u32[]{:S(2)}, u32[]{:S(2)}) collective-permute-start(bf16[512,512]{1,0:T(8,128)(2,1)} %get-tuple-element.272.refs_0_), channel_id=1, source_target_pairs={{0,8},{8,0},{16,24},{24,16},{1,9},{9,1},{17,25},{25,17},{2,10},{10... | collective-permute-start | bytes 1572872 | tf_op jit(solution)/shard_map/ppermute | solution.py:107
  685.2 13.6 %copy-start.32 = (f32[1024]{0:T(1024)}, f32[1024]{0:T(1024)S(1)}, u32[]{:S(2)}) copy-start(f32[1024]{0:T(1024)S(1)} %get-tuple-element.342) | copy-start | bytes 12292
  689.7 1.1 copy-start.8
  693.8 0.8 copy-start.17
Sparse Core Ops, SparseCore 0:
  206.8 44.9 reduce-scatter.8
  288.1 44.4 reduce-scatter.10
  352.4 44.0 reduce-scatter.12
  398.8 43.1 reduce-scatter.14
  466.1 44.1 reduce-scatter.16
  518.2 44.0 reduce-scatter.18
  564.6 43.1 reduce-scatter.20
  616.8 43.9 reduce-scatter.22
